TPU v7x, 32 devices: a whole 2x2x4 slice. The times are simulated.
32 devices in a mesh: ens: 4 (over y, x), lat: 2 (over core), lon: 4 (over z).
Axes of the slice: x: 2, y: 2, z: 4, core: 2. Of those that a mesh axis runs over, the one named last changes fastest.
Arguments:
- state: bfloat16 [2, 72, 8, 1024], P(None, None, 'lat', 'lon'), may hold values from -6 to 6
- noise_field: bfloat16 [4, 8, 8, 1024], P('ens', None, 'lat', 'lon'), may hold values from -6 to 6
- cotangent: bfloat16 [4, 72, 8, 1024], P('ens', None, 'lat', 'lon'), may hold values from -6 to 6
- slot_date: int32 [4], P('ens'), may hold values from -1 to 1, as said below
- lon_reach: int32 [4], replicated, may hold values from 1 to 2
- enc_taps: float32 [3, 4, 25], replicated, may hold values from -1.2 to 1.2
- proc_taps: float32 [3, 4, 25], replicated, may hold values from -1.2 to 1.2
- dec_taps: float32 [3, 8, 9], replicated, may hold values from -1.2 to 1.2
- enc_weight: bfloat16 [3, 641, 80], replicated, may hold values from -0.375 to 0.375
- enc_bias: float32 [641], replicated, may hold values from -1.5 to 1.5
- gain_one: float32 [641], replicated, may hold values from 0.25 to 1.75
- shift_one: float32 [641], replicated, may hold values from -1.5 to 1.5
- proc_weight: bfloat16 [3, 641, 641], replicated, may hold values from -0.125 to 0.125
- proc_bias: float32 [641], replicated, may hold values from -1.5 to 1.5
- gain_two: float32 [641], replicated, may hold values from 0.25 to 1.75
- shift_two: float32 [641], replicated, may hold values from -1.5 to 1.5
- up_weight: bfloat16 [1282, 641], replicated, may hold values from -0.25 to 0.25
- up_bias: float32 [1282], replicated, may hold values from -1.5 to 1.5
- down_weight: bfloat16 [641, 1282], replicated, may hold values from -0.15625 to 0.15625
- down_bias: float32 [641], replicated, may hold values from -1.5 to 1.5
- dec_weight: bfloat16 [3, 72, 641], replicated, may hold values from -0.25 to 0.25
- dec_bias: float32 [72], replicated, may hold values from -1.5 to 1.5
Outputs:
- output: bfloat16 [4, 72, 8, 1024], P('ens', None, 'lat', 'lon')
- state_grad: bfloat16 [2, 72, 8, 1024], P(None, None, 'lat', 'lon')
- enc_weight_grad: float32 [3, 641, 80], replicated
- enc_bias_grad: float32 [641], replicated
- gain_one_grad: float32 [641], replicated
- shift_one_grad: float32 [641], replicated
- proc_weight_grad: float32 [3, 641, 641], replicated
- proc_bias_grad: float32 [641], replicated
- gain_two_grad: float32 [641], replicated
- shift_two_grad: float32 [641], replicated
- up_weight_grad: float32 [1282, 641], replicated
- up_bias_grad: float32 [1282], replicated
- down_weight_grad: float32 [641, 1282], replicated
- down_bias_grad: float32 [641], replicated
- dec_weight_grad: float32 [3, 72, 641], replicated
- dec_bias_grad: float32 [72], replicated
- mean_one: float32 [4, 641], P('ens')
- var_one: float32 [4, 641], P('ens')
- mean_two: float32 [4, 641], P('ens')
- var_two: float32 [4, 641], P('ens')
Inputs may be any that keep to these rules, and one draw needn't show every extreme that they name: `slot_date`: exactly 1 slots hold date 0 and exactly 2 hold date 1; the other slots hold -1. Which slots is drawn.
All inputs are finite; a program needn't handle non-finite values.
Results may differ from a plain program's by a relative error of at most 0.014.
Values may be sent and summed in bfloat16 or wider, within the bound.
A program may use at most 128 MiB of HBM per device.

v0:
```python
import jax
import jax.numpy as jnp
import numpy as np
from jax import lax
from jax.sharding import PartitionSpec as P

epsilon = 1e-05


def with_halo(cells, sides, width):
    for axis, dim in sides:
        count = lax.axis_size(axis)
        head = lax.slice_in_dim(cells, 0, width, axis=dim)
        tail = lax.slice_in_dim(cells, cells.shape[dim] - width, cells.shape[dim], axis=dim)
        cells = jnp.concatenate(
            [
                lax.ppermute(tail, axis, [(i, (i + 1) % count) for i in range(count)]),
                cells,
                lax.ppermute(head, axis, [((i + 1) % count, i) for i in range(count)]),
            ],
            axis=dim,
        )
    return cells


def tap_list(half_span):
    return [
        (row_step, col_step)
        for row_step in range(-half_span, half_span + 1)
        for col_step in range(-half_span, half_span + 1)
    ]


def masked_taps(tap_table, reach_rows, half_span, reduce_by):
    offsets = np.array(
        [abs(col_step) for row_step, col_step in tap_list(half_span)], dtype=np.int32
    )
    inside = (jnp.asarray(offsets)[None, :] <= reach_rows[:, None] - reduce_by).astype(jnp.float32)
    return tap_table * inside[None]


def rows_from(tap_table, start_row, row_count, margin):
    padded = jnp.pad(tap_table, ((0, 0), (margin, margin), (0, 0)), mode="edge")
    return lax.dynamic_slice_in_dim(padded, start_row + margin, row_count, 1)


def keep_rows(padded, start_row, half_span, total_rows):
    global_row = start_row - half_span + jnp.arange(padded.shape[-2])
    inside = ((global_row >= 0) & (global_row < total_rows)).astype(padded.dtype)
    return padded * inside[:, None]


def disco_filter(padded, weights, stride, half_span, row_count, col_count):
    running = None
    for position, (row_step, col_step) in enumerate(tap_list(half_span)):
        top = half_span + row_step
        left = half_span + col_step
        sliced = padded[
            ...,
            top : top + stride * (row_count - 1) + 1 : stride,
            left : left + stride * (col_count - 1) + 1 : stride,
        ]
        weighted = weights[:, None, :, position, None] * sliced[..., None, :, :, :]
        running = weighted if running is None else running + weighted
    return running


def upfilter(padded, weights, row_count, col_count):
    running = None
    for position, (row_step, col_step) in enumerate(tap_list(1)):
        sliced = padded[
            ..., 1 + row_step : 1 + row_step + row_count, 1 + col_step : 1 + col_step + col_count
        ]
        doubled = jnp.repeat(jnp.repeat(sliced, 2, axis=-2), 2, axis=-1)
        weighted = jnp.sum(weights[:, None, :, position, None] * doubled, axis=-4)
        running = weighted if running is None else running + weighted
    return running


def upfilter_adjoint(cot_wide, dec_ext, half_rows, half_cols):
    slot_count, in_width, wide_rows, wide_cols = cot_wide.shape
    pair_rows, pair_cols = (wide_rows // 2, wide_cols // 2)
    col_sums = jnp.sum(
        cot_wide.astype(jnp.float32).reshape(slot_count, in_width, wide_rows, pair_cols, 2), axis=-1
    )
    col_pairs = col_sums.reshape(slot_count, in_width, pair_rows, 2, pair_cols)
    row_pairs = dec_ext.reshape(dec_ext.shape[0], pair_rows, 2, dec_ext.shape[-1])
    running = None
    for position, (row_step, col_step) in enumerate(tap_list(1)):
        top = 1 - row_step
        left = 1 - col_step
        taps_now = row_pairs[:, top : top + half_rows, :, position]
        block = col_pairs[:, :, top : top + half_rows, :, left : left + half_cols]
        weighted = jnp.sum(taps_now[None, :, None, :, :, None] * block[:, None], axis=-2)
        running = weighted if running is None else running + weighted
    return running


def proc_adjoint(filt_grad, proc_ext, half_rows, half_cols):
    grad_float = filt_grad.astype(jnp.float32)
    running = None
    for position, (row_step, col_step) in enumerate(tap_list(2)):
        top = 2 - row_step
        left = 2 - col_step
        taps_now = proc_ext[:, top : top + half_rows, position]
        block = grad_float[:, :, :, top : top + half_rows, left : left + half_cols]
        weighted = jnp.sum(taps_now[None, :, None, :, None] * block, axis=1)
        running = weighted if running is None else running + weighted
    return running


def encode_adjoint(by_date, enc_ext, half_rows, half_cols):
    phases = [[None, None], [None, None]]
    for position, (row_step, col_step) in enumerate(tap_list(2)):
        top = -((row_step - 2) // 2)
        left = -((col_step - 2) // 2)
        taps_now = enc_ext[:, top : top + half_rows, position]
        block = by_date[:, :, :, top : top + half_rows, left : left + half_cols]
        weighted = jnp.sum(taps_now[None, :, None, :, None] * block, axis=1)
        row_phase, col_phase = (row_step % 2, col_step % 2)
        current = phases[row_phase][col_phase]
        phases[row_phase][col_phase] = weighted if current is None else current + weighted
    upper = jnp.stack([phases[0][0], phases[0][1]], axis=-1)
    lower = jnp.stack([phases[1][0], phases[1][1]], axis=-1)
    joined = jnp.stack([upper, lower], axis=-3)
    return joined.reshape(joined.shape[0], joined.shape[1], 2 * half_rows, 2 * half_cols)


def normalize(values, gain_vector, shift_vector, pixel_count):
    totals = lax.psum(jnp.sum(values, axis=(2, 3)), ("lat", "lon"))
    average = totals / pixel_count
    centred = values - average[:, :, None, None]
    variance = lax.psum(jnp.sum(centred * centred, axis=(2, 3)), ("lat", "lon")) / pixel_count
    rescale = lax.rsqrt(variance + epsilon)
    standard = (values - average[:, :, None, None]) * rescale[:, :, None, None]
    result = (
        standard * gain_vector[None, :, None, None] + shift_vector[None, :, None, None]
    ).astype(jnp.bfloat16)
    return (result, standard, rescale, average, variance)


def norm_back(grad_norm, standard, rescale, gain_vector, pixel_count):
    gain_grad = jnp.sum(grad_norm * standard, axis=(0, 2, 3))
    shift_grad = jnp.sum(grad_norm, axis=(0, 2, 3))
    scaled = grad_norm * gain_vector[None, :, None, None]
    first_sum, second_sum = lax.psum(
        (jnp.sum(scaled, axis=(2, 3)), jnp.sum(scaled * standard, axis=(2, 3))), ("lat", "lon")
    )
    grad_values = rescale[:, :, None, None] * (
        scaled
        - first_sum[:, :, None, None] / pixel_count
        - standard * (second_sum[:, :, None, None] / pixel_count)
    )
    return (grad_values, gain_grad, shift_grad)


def per_device(
    state,
    noise_field,
    cotangent,
    slot_date,
    lon_reach,
    enc_taps,
    proc_taps,
    dec_taps,
    enc_weight,
    enc_bias,
    gain_one,
    shift_one,
    proc_weight,
    proc_bias,
    gain_two,
    shift_two,
    up_weight,
    up_bias,
    down_weight,
    down_bias,
    dec_weight,
    dec_bias,
):
    slot_count, noise_width = (noise_field.shape[0], noise_field.shape[1])
    date_count, in_width, full_rows, full_cols = state.shape
    half_rows, half_cols = (full_rows // 2, full_cols // 2)
    basis_count = enc_taps.shape[0]
    lat_total = half_rows * lax.axis_size("lat")
    pixel_count = float(lat_total * half_cols * lax.axis_size("lon"))
    row_start = lax.axis_index("lat") * half_rows
    full_start = 2 * row_start
    enc_eff = masked_taps(enc_taps, lon_reach, 2, 0)
    proc_eff = masked_taps(proc_taps, lon_reach, 2, 0)
    dec_eff = masked_taps(dec_taps, jnp.repeat(lon_reach, 2), 1, 1)
    date_pick = (slot_date[:, None] == jnp.arange(date_count)[None, :]).astype(jnp.bfloat16)
    slot_live = (slot_date >= 0).astype(jnp.float32)
    cot_live = cotangent * slot_live.astype(jnp.bfloat16)[:, None, None, None]
    stacked = jnp.concatenate(
        [
            state.reshape(-1, full_rows, full_cols),
            noise_field.reshape(-1, full_rows, full_cols),
            cot_live.reshape(-1, full_rows, full_cols),
        ],
        0,
    )
    full_wide = with_halo(stacked, (("lat", 1), ("lon", 2)), 2)
    full_wide = keep_rows(full_wide, full_start, 2, 2 * lat_total)
    first_cut = date_count * in_width
    second_cut = first_cut + slot_count * noise_width
    state_wide = full_wide[:first_cut].reshape(date_count, in_width, full_rows + 4, full_cols + 4)
    noise_wide = full_wide[first_cut:second_cut].reshape(
        slot_count, noise_width, full_rows + 4, full_cols + 4
    )
    cot_wide = full_wide[second_cut:].reshape(slot_count, in_width, full_rows + 4, full_cols + 4)
    enc_rows = lax.dynamic_slice_in_dim(enc_eff, row_start, half_rows, 1)
    state_filt = disco_filter(state_wide, enc_rows, 2, 2, half_rows, half_cols).astype(jnp.bfloat16)
    noise_filt = disco_filter(noise_wide, enc_rows, 2, 2, half_rows, half_cols).astype(jnp.bfloat16)
    chosen = jnp.einsum(
        "sd,dkchw->skchw", date_pick, state_filt, preferred_element_type=jnp.float32
    ).astype(jnp.bfloat16)
    filtered = jnp.concatenate([chosen, noise_filt], 2)
    h_zero = (
        jnp.einsum("kdc,skchw->sdhw", enc_weight, filtered, preferred_element_type=jnp.float32)
        + enc_bias[None, :, None, None]
    )
    norm_one, standard_one, rescale_one, mean_one, var_one = normalize(
        h_zero, gain_one, shift_one, pixel_count
    )
    norm_wide = with_halo(norm_one, (("lat", 2), ("lon", 3)), 2)
    norm_wide = keep_rows(norm_wide, row_start, 2, lat_total)
    proc_rows = lax.dynamic_slice_in_dim(proc_eff, row_start, half_rows, 1)
    proc_filt = disco_filter(norm_wide, proc_rows, 1, 2, half_rows, half_cols).astype(jnp.bfloat16)
    h_one = (
        h_zero
        + jnp.einsum("kdc,skchw->sdhw", proc_weight, proc_filt, preferred_element_type=jnp.float32)
        + proc_bias[None, :, None, None]
    )
    norm_two, standard_two, rescale_two, mean_two, var_two = normalize(
        h_one, gain_two, shift_two, pixel_count
    )
    hidden_pre = (
        jnp.einsum("fc,schw->sfhw", up_weight, norm_two, preferred_element_type=jnp.float32)
        + up_bias[None, :, None, None]
    )
    activated = jax.nn.gelu(hidden_pre).astype(jnp.bfloat16)
    h_two = (
        h_one
        + jnp.einsum("cf,sfhw->schw", down_weight, activated, preferred_element_type=jnp.float32)
        + down_bias[None, :, None, None]
    )
    h_two_low = h_two.astype(jnp.bfloat16)
    projected = jnp.einsum(
        "kic,schw->skihw", dec_weight, h_two_low, preferred_element_type=jnp.float32
    ).astype(jnp.bfloat16)
    proj_wide = with_halo(projected, (("lat", 3), ("lon", 4)), 1)
    proj_wide = keep_rows(proj_wide, row_start, 1, lat_total)
    dec_rows = lax.dynamic_slice_in_dim(dec_eff, full_start, full_rows, 1)
    decoded = upfilter(proj_wide, dec_rows, half_rows, half_cols) + dec_bias[None, :, None, None]
    output = (decoded * slot_live[:, None, None, None]).astype(jnp.bfloat16)
    dec_bias_grad = jnp.sum(cot_live, axis=(0, 2, 3), dtype=jnp.float32)
    dec_ext = rows_from(dec_eff, full_start - 2, full_rows + 4, 2)
    proj_grad = upfilter_adjoint(cot_wide, dec_ext, half_rows, half_cols).astype(jnp.bfloat16)
    dec_weight_grad = jnp.einsum(
        "skihw,schw->kic", proj_grad, h_two_low, preferred_element_type=jnp.float32
    )
    two_grad = jnp.einsum(
        "kic,skihw->schw", dec_weight, proj_grad, preferred_element_type=jnp.float32
    )
    mixed_grad = two_grad.astype(jnp.bfloat16)
    down_weight_grad = jnp.einsum(
        "schw,sfhw->cf", mixed_grad, activated, preferred_element_type=jnp.float32
    )
    down_bias_grad = jnp.sum(mixed_grad, axis=(0, 2, 3), dtype=jnp.float32)
    act_grad = jnp.einsum(
        "cf,schw->sfhw", down_weight, mixed_grad, preferred_element_type=jnp.float32
    )
    _, pull_gelu = jax.vjp(jax.nn.gelu, hidden_pre)
    hidden_grad = pull_gelu(act_grad)[0].astype(jnp.bfloat16)
    up_weight_grad = jnp.einsum(
        "sfhw,schw->fc", hidden_grad, norm_two, preferred_element_type=jnp.float32
    )
    up_bias_grad = jnp.sum(hidden_grad, axis=(0, 2, 3), dtype=jnp.float32)
    norm_two_grad = jnp.einsum(
        "fc,sfhw->schw", up_weight, hidden_grad, preferred_element_type=jnp.float32
    )
    one_grad, gain_two_grad, shift_two_grad = norm_back(
        norm_two_grad, standard_two, rescale_two, gain_two, pixel_count
    )
    one_grad = one_grad + two_grad
    branch_grad = one_grad.astype(jnp.bfloat16)
    proc_weight_grad = jnp.einsum(
        "sdhw,skchw->kdc", branch_grad, proc_filt, preferred_element_type=jnp.float32
    )
    proc_bias_grad = jnp.sum(branch_grad, axis=(0, 2, 3), dtype=jnp.float32)
    local_grad = jnp.einsum(
        "kdc,sdhw->skchw", proc_weight, branch_grad, preferred_element_type=jnp.float32
    ).astype(jnp.bfloat16)
    filt_grad = with_halo(local_grad, (("lat", 3), ("lon", 4)), 2)
    filt_grad = keep_rows(filt_grad, row_start, 2, lat_total)
    proc_ext = rows_from(proc_eff, row_start - 2, half_rows + 4, 2)
    norm_one_grad = proc_adjoint(filt_grad, proc_ext, half_rows, half_cols)
    zero_sum, gain_one_grad, shift_one_grad = norm_back(
        norm_one_grad, standard_one, rescale_one, gain_one, pixel_count
    )
    zero_grad = (zero_sum + one_grad).astype(jnp.bfloat16)
    enc_weight_grad = jnp.einsum(
        "sdhw,skchw->kdc", zero_grad, filtered, preferred_element_type=jnp.float32
    )
    enc_bias_grad = jnp.sum(zero_grad, axis=(0, 2, 3), dtype=jnp.float32)
    part_grad = jnp.einsum(
        "kdc,sdhw->skchw",
        enc_weight[:, :, :in_width],
        zero_grad,
        preferred_element_type=jnp.float32,
    ).astype(jnp.bfloat16)
    part_wide = with_halo(
        part_grad.reshape(slot_count, basis_count * in_width, half_rows, half_cols),
        (("lat", 2), ("lon", 3)),
        1,
    )
    part_wide = keep_rows(part_wide, row_start, 1, lat_total).reshape(
        slot_count, basis_count, in_width, half_rows + 2, half_cols + 2
    )
    by_date = jnp.einsum(
        "sd,skchw->dkchw", date_pick, part_wide, preferred_element_type=jnp.float32
    )
    enc_ext = rows_from(enc_eff, row_start - 1, half_rows + 2, 1)
    state_local = encode_adjoint(by_date, enc_ext, half_rows, half_cols)
    state_grad = lax.psum(state_local.astype(jnp.bfloat16), "ens")
    summed = lax.psum(
        (
            enc_weight_grad,
            enc_bias_grad,
            gain_one_grad,
            shift_one_grad,
            proc_weight_grad,
            proc_bias_grad,
            gain_two_grad,
            shift_two_grad,
            up_weight_grad,
            up_bias_grad,
            down_weight_grad,
            down_bias_grad,
            dec_weight_grad,
            dec_bias_grad,
        ),
        ("ens", "lat", "lon"),
    )
    live_column = slot_live[:, None]
    return (
        output,
        state_grad,
        summed[0],
        summed[1],
        summed[2],
        summed[3],
        summed[4],
        summed[5],
        summed[6],
        summed[7],
        summed[8],
        summed[9],
        summed[10],
        summed[11],
        summed[12],
        summed[13],
        mean_one * live_column,
        var_one * live_column,
        mean_two * live_column,
        var_two * live_column,
    )


def solution(mesh):
    in_specs = (
        P(None, None, "lat", "lon"),
        P("ens", None, "lat", "lon"),
        P("ens", None, "lat", "lon"),
        P("ens"),
        P(),
        P(),
        P(),
        P(),
        P(),
        P(),
        P(),
        P(),
        P(),
        P(),
        P(),
        P(),
        P(),
        P(),
        P(),
        P(),
        P(),
        P(),
    )
    out_specs = (
        P("ens", None, "lat", "lon"),
        P(None, None, "lat", "lon"),
        P(),
        P(),
        P(),
        P(),
        P(),
        P(),
        P(),
        P(),
        P(),
        P(),
        P(),
        P(),
        P(),
        P(),
        P("ens", None),
        P("ens", None),
        P("ens", None),
        P("ens", None),
    )
    return jax.shard_map(
        per_device, mesh=mesh, in_specs=in_specs, out_specs=out_specs, check_vma=False
    )
```

profile of v0, /device:TPU:0, one launch (start us, length us, event | category | flops | bytes accessed | tf_op | source)
XLA Modules:
  0.0 1032.7 jit_solution(18224808166621338521)
XLA Ops:
  62.3 5.0 collective-permute-start.3
  178.5 7.5 slice.923
  186.0 7.5 slice.921
  193.5 7.9 slice.919
  201.4 7.8 slice.917
  209.2 7.8 slice.915
  217.0 7.9 slice.913
  224.9 8.0 slice.911
  233.0 7.9 slice.909
  240.8 7.8 slice.907
  248.7 7.8 slice.905
  256.5 7.9 slice.903
  264.4 7.9 slice.901
  272.2 7.9 slice.899
  280.1 7.8 slice.897
  287.9 7.8 slice.895
  295.7 7.9 slice.893
  303.6 7.9 slice.891
  311.5 8.1 slice.889
  319.6 7.8 slice.887
  327.4 7.8 slice.885
  335.2 7.9 slice.883
  343.1 7.9 slice.881
  351.0 7.9 slice.879
  358.9 7.8 slice.877
  366.7 7.8 slice.875
  389.9 4.4 add_convert_fusion.1
  398.2 16.5 %psum.161 = f32[1,641]{1,0:T(1,128)S(1)} all-reduce(f32[1,641]{1,0:T(1,128)S(1)} %reduce_sum.851), channel_id=1, replica_groups=mesh['ens'=4,'lat'=2,'lon'=4] {'lat','lon'}, use_global_device_ids=true, to_apply=%region_1.0 | all-reduce | flops 641 | bytes 5128 | tf_op jit(solution)/shard_map/psum | solution.py:130
  416.7 13.7 %psum.162 = f32[1,641]{1,0:T(1,128)S(1)} all-reduce(f32[1,641]{1,0:T(1,128)S(1)} %reduce_sum.853), channel_id=1, replica_groups=mesh['ens'=4,'lat'=2,'lon'=4] {'lat','lon'}, use_global_device_ids=true, to_apply=%region_3.0 | all-reduce | flops 641 | bytes 5128 | tf_op jit(solution)/shard_map/psum | solution.py:133
  482.9 5.9 fusion.124
  491.8 10.7 %add_convert_fusion = bf16[3,641,2,128]{3,1,2,0:T(8,128)(2,1)} fusion(f32[641,2,128]{2,0,1:T(8,128)} %get-tuple-element.254, f32[3,2]{1,0:T(4,128)S(1)} %copy-done.107, f32[641,2,128]{2,0,1:T(8,128)} %get-tuple-element.255, f32[3,2]{1,0:T(4,128)S(1)} %copy-done.108, f32[641,2,128]{2,0,1:T(8,128)} %get-tuple-element.256, f32[3,2]{1,0:T(4,128)S(1)} %copy-done.109, ...), kind=kLoop, calls=%fused_computation.65 | loop fusion | flops 24614400 | bytes 17394776 | tf_op jit(solution)/shard_map/convert_element_type | solution.py:229
  505.8 13.7 %psum.163 = f32[1,641]{1,0:T(1,128)S(1)} all-reduce(f32[1,641]{1,0:T(1,128)S(1)} %reduce_sum.855), channel_id=1, replica_groups=mesh['ens'=4,'lat'=2,'lon'=4] {'lat','lon'}, use_global_device_ids=true, to_apply=%region_5.0 | all-reduce | flops 641 | bytes 5128 | tf_op jit(solution)/shard_map/psum | solution.py:130
  521.4 16.1 %psum.164 = f32[1,641]{1,0:T(1,128)S(1)} all-reduce(f32[1,641]{1,0:T(1,128)S(1)} %reduce_sum.857), channel_id=1, replica_groups=mesh['ens'=4,'lat'=2,'lon'=4] {'lat','lon'}, use_global_device_ids=true, to_apply=%region_7.0 | all-reduce | flops 641 | bytes 5128 | tf_op jit(solution)/shard_map/psum | solution.py:133
  546.0 14.1 %all-reduce.3 = (f32[1,641]{1,0:T(1,128)S(1)}, f32[1,641]{1,0:T(1,128)S(1)}) all-reduce(f32[1,641]{1,0:T(1,128)S(1)} %reduce_sum.884, f32[1,641]{1,0:T(1,128)S(1)} %reduce_sum.882), channel_id=1, replica_groups=mesh['ens'=4,'lat'=2,'lon'=4] {'lat','lon'}, use_global_device_ids=true, to_apply=%region_30.31 | all-reduce | flops 1282 | bytes 10256 | tf_op jit(solution)/shard_map/psum | solution.py:146
  612.3 3.6 fusion.72
  621.9 6.9 fusion
  628.8 6.0 fusion.29
  634.8 6.9 fusion.30
  641.7 7.8 fusion.31
  649.5 5.9 add_add_fusion.1
  657.3 16.9 %all-reduce.2 = (f32[1,641]{1,0:T(1,128)S(1)}, f32[1,641]{1,0:T(1,128)S(1)}) all-reduce(f32[1,641]{1,0:T(1,128)S(1)} %reduce_sum.933, f32[1,641]{1,0:T(1,128)S(1)} %reduce_sum.931), channel_id=1, replica_groups=mesh['ens'=4,'lat'=2,'lon'=4] {'lat','lon'}, use_global_device_ids=true, to_apply=%region_59.60 | all-reduce | flops 1282 | bytes 10256 | tf_op jit(solution)/shard_map/psum | solution.py:146
  688.1 6.5 collective-permute-done.19
  711.7 5.3 collective-permute-done.11
  717.0 4.9 collective-permute-done.10
  725.6 40.4 %all-reduce = (f32[641]{0:T(1024)}, f32[641]{0:T(1024)}, f32[641]{0:T(1024)}, f32[641]{0:T(1024)}, f32[641]{0:T(1024)}, /*index=5*/f32[641]{0:T(1024)}, f32[1282]{0:T(1024)}, f32[641]{0:T(1024)}, f32[72]{0:T(128)}) all-reduce(f32[641]{0:T(1024)S(1)} %get-tuple-element.246, ...), channel_id=1, replica_groups=mesh['ens'=4,'lat'=2,'lon'=4] {'ens','lat','lon'}, use_global_device_ids=true, to_apply=%region_88.89 | all-reduce | flops 5841 | bytes 46728 | tf_op jit(solution)/shard_map/psum | solution.py:327
  768.0 241.4 %all-reduce.9.cloned.1.call-done = (f32[3,641,80]{1,2,0:T(8,128)}, f32[3,641,641]{1,2,0:T(8,128)}, f32[1282,641]{0,1:T(8,128)}, f32[641,1282]{1,0:T(8,128)}, f32[3,72,641]{2,1,0:T(8,128)}) async-done(((f32[3,641,80]{1,2,0:T(8,128)}, f32[3,641,641]{1,2,0:T(8,128)}, f32[1282,641]{0,1:T(8,128)}, f32[641,1282]{1,0:T(8,128)}, f32[3,72,641]{2,1,0:T(8,128)}), (f32[3,641,80]{1,2,0:T(8,128)}, ...) | async-done | bytes 12673868 | tf_op jit(solution)/shard_map/psum | solution.py:327
  1009.4 7.5 copy.1747
  1017.8 4.2 copy.1802
  (853 shorter events, 353.8 us)
Async XLA Ops:
  7.2 495.2 %copy-start = (bf16[3,641,641]{2,1,0:T(8,128)(2,1)S(1)}, bf16[3,641,641]{2,1,0:T(8,128)(2,1)}, u32[]{:S(2)}) copy-start(bf16[3,641,641]{2,1,0:T(8,128)(2,1)} %param.37) | copy-start | bytes 7395862
  7.3 758.7 %all-reduce.7.cloned.1.call-start = ((), (), s32[]{:S(2)}) async-start(), calls=%async_computation | async-start | bytes 1048576 | tf_op jit(solution)/shard_map/psum | solution.py:326
  11.7 48.4 %collective-permute-start.1 = (bf16[224,2,256]{2,0,1:T(8,128)(2,1)}, bf16[224,2,256]{2,0,1:T(8,128)(2,1)}, u32[]{:S(2)}, u32[]{:S(2)}) collective-permute-start(bf16[224,2,256]{2,0,1:T(8,128)(2,1)} %get-tuple-element.293), channel_id=1, source_target_pairs={{4,0},{0,4},{5,1},{1,5},{6,2},{2,6},{7,3},{3,7},{12,8},{8,12},{13,... | collective-permute-start | bytes 688136 | tf_op jit(solution)/shard_map/ppermute | solution.py:19
  12.2 47.9 %collective-permute-start = (bf16[224,2,256]{2,0,1:T(8,128)(2,1)}, bf16[224,2,256]{2,0,1:T(8,128)(2,1)}, u32[]{:S(2)}, u32[]{:S(2)}) collective-permute-start(bf16[224,2,256]{2,0,1:T(8,128)(2,1)} %get-tuple-element.292), channel_id=1, source_target_pairs={{0,4},{4,0},{1,5},{5,1},{2,6},{6,2},{3,7},{7,3},{8,12},{12,8},{9,1... | collective-permute-start | bytes 688136 | tf_op jit(solution)/shard_map/ppermute | solution.py:17
  22.7 36.7 %copy-start.89 = (f32[3,2,1]{0,1,2:T(2,128)}, f32[3,2,1]{0,1,2:T(2,128)S(1)}, u32[]{:S(2)}) copy-start(f32[3,2,1]{0,1,2:T(2,128)S(1)} %copy.1553) | copy-start | bytes 76
  23.4 35.9 %copy-start.91 = (f32[3,2,1]{0,1,2:T(2,128)}, f32[3,2,1]{0,1,2:T(2,128)S(1)}, u32[]{:S(2)}) copy-start(f32[3,2,1]{0,1,2:T(2,128)S(1)} %copy.1551) | copy-start | bytes 76
  34.9 24.5 %copy-start.102 = (f32[3,2,1]{0,1,2:T(2,128)}, f32[3,2,1]{0,1,2:T(2,128)S(1)}, u32[]{:S(2)}) copy-start(f32[3,2,1]{0,1,2:T(2,128)S(1)} %copy.1531) | copy-start | bytes 76
  35.0 24.4 %copy-start.104 = (f32[3,2,1]{0,1,2:T(2,128)}, f32[3,2,1]{0,1,2:T(2,128)S(1)}, u32[]{:S(2)}) copy-start(f32[3,2,1]{0,1,2:T(2,128)S(1)} %copy.1529) | copy-start | bytes 76
  60.0 75.2 %copy-start.80 = (f32[3,2,1]{2,1,0:T(2,128)S(1)}, f32[3,2,1]{2,1,0:T(2,128)}, u32[]{:S(2)}) copy-start(f32[3,2,1]{2,1,0:T(2,128)} %get-tuple-element.398) | copy-start | bytes 76
  60.1 81.5 %copy-start.56 = (f32[3,2,2,1]{3,2,1,0:T(2,128)S(1)}, f32[3,2,2,1]{3,2,1,0:T(2,128)}, u32[]{:S(2)}) copy-start(f32[3,2,2,1]{3,2,1,0:T(2,128)} %get-tuple-element.338) | copy-start | bytes 148
  62.3 87.5 %collective-permute-start.3 = (bf16[224,8,2]{2,0,1:T(8,128)(2,1)}, bf16[224,8,2]{2,0,1:T(8,128)(2,1)}, u32[]{:S(2)}, u32[]{:S(2)}) collective-permute-start(bf16[224,8,2]{2,0,1:T(8,128)(2,1)} %get-tuple-element.281), channel_id=1, source_target_pairs={{1,0},{2,1},{3,2},{0,3},{5,4},{6,5},{7,6},{4,7},{9,8},{10,9},{11,1... | collective-permute-start | bytes 21512 | tf_op jit(solution)/shard_map/ppermute | solution.py:19
  67.4 82.4 %collective-permute-start.2 = (bf16[224,8,2]{2,0,1:T(8,128)(2,1)}, bf16[224,8,2]{2,0,1:T(8,128)(2,1)}, u32[]{:S(2)}, u32[]{:S(2)}) collective-permute-start(bf16[224,8,2]{2,0,1:T(8,128)(2,1)} %get-tuple-element.280), channel_id=1, source_target_pairs={{0,1},{1,2},{2,3},{3,0},{4,5},{5,6},{6,7},{7,4},{8,9},{9,10},{10,1... | collective-permute-start | bytes 21512 | tf_op jit(solution)/shard_map/ppermute | solution.py:17
  374.5 14.4 %copy-start.49 = (bf16[2,72,2,128]{3,2,1,0:T(2,128)(2,1)S(1)}, bf16[2,72,2,128]{3,2,1,0:T(2,128)(2,1)}, u32[]{:S(2)}) copy-start(bf16[2,72,2,128]{3,2,1,0:T(2,128)(2,1)} %slice.889) | copy-start | bytes 221188
  374.5 14.5 %copy-start.48 = (bf16[2,72,2,128]{3,2,1,0:T(2,128)(2,1)S(1)}, bf16[2,72,2,128]{3,2,1,0:T(2,128)(2,1)}, u32[]{:S(2)}) copy-start(bf16[2,72,2,128]{3,2,1,0:T(2,128)(2,1)} %slice.887) | copy-start | bytes 221188
  374.6 14.5 %copy-start.47 = (bf16[2,72,2,128]{3,2,1,0:T(2,128)(2,1)S(1)}, bf16[2,72,2,128]{3,2,1,0:T(2,128)(2,1)}, u32[]{:S(2)}) copy-start(bf16[2,72,2,128]{3,2,1,0:T(2,128)(2,1)} %slice.885) | copy-start | bytes 221188
  374.7 14.5 %copy-start.46 = (bf16[2,72,2,128]{3,2,1,0:T(2,128)(2,1)S(1)}, bf16[2,72,2,128]{3,2,1,0:T(2,128)(2,1)}, u32[]{:S(2)}) copy-start(bf16[2,72,2,128]{3,2,1,0:T(2,128)(2,1)} %slice.883) | copy-start | bytes 221188
  375.7 13.6 %copy-start.45 = (bf16[2,72,2,128]{3,2,1,0:T(2,128)(2,1)S(1)}, bf16[2,72,2,128]{3,2,1,0:T(2,128)(2,1)}, u32[]{:S(2)}) copy-start(bf16[2,72,2,128]{3,2,1,0:T(2,128)(2,1)} %slice.881) | copy-start | bytes 221188
  394.3 36.7 %copy-start.54 = (f32[641]{0:T(1024)S(1)}, f32[641]{0:T(1024)}, u32[]{:S(2)}) copy-start(f32[641]{0:T(1024)} %param.35) | copy-start | bytes 7696
  394.7 41.5 %copy-start.30 = (bf16[1,3,72,2,128]{4,2,1,3,0:T(8,128)(2,1)}, bf16[1,3,72,2,128]{4,2,1,3,0:T(8,128)(2,1)S(1)}, u32[]{:S(2)}) copy-start(bf16[1,3,72,2,128]{4,2,1,3,0:T(8,128)(2,1)S(1)} %copy.1790) | copy-start | bytes 331780
  394.8 36.2 %copy-start.162 = (f32[641]{0:T(1024)S(1)}, f32[641]{0:T(1024)}, u32[]{:S(2)}) copy-start(f32[641]{0:T(1024)} %param.36) | copy-start | bytes 7696
  396.3 40.0 %copy-start.50 = (bf16[1,3,8,2,128]{4,2,1,3,0:T(8,128)(2,1)}, bf16[1,3,8,2,128]{4,2,1,3,0:T(8,128)(2,1)S(1)}, u32[]{:S(2)}) copy-start(bf16[1,3,8,2,128]{4,2,1,3,0:T(8,128)(2,1)S(1)} %add_convert_fusion.7) | copy-start | bytes 36868
  433.2 30.2 %collective-permute-start.5 = (bf16[1,641,2,128]{3,1,2,0:T(8,128)(2,1)}, bf16[1,641,2,128]{3,1,2,0:T(8,128)(2,1)}, u32[]{:S(2)}, u32[]{:S(2)}) collective-permute-start(bf16[1,641,2,128]{3,1,2,0:T(8,128)(2,1)} %fusion.84), channel_id=1, source_target_pairs={{4,0},{0,4},{5,1},{1,5},{6,2},{2,6},{7,3},{3,7},{12,8},{8,12},{13,... | collective-permute-start | bytes 984584 | tf_op jit(solution)/shard_map/ppermute | solution.py:19
  434.3 29.1 %collective-permute-start.4 = (bf16[1,641,2,128]{3,1,2,0:T(8,128)(2,1)}, bf16[1,641,2,128]{3,1,2,0:T(8,128)(2,1)}, u32[]{:S(2)}, u32[]{:S(2)}) collective-permute-start(bf16[1,641,2,128]{3,1,2,0:T(8,128)(2,1)} %fusion.84), channel_id=1, source_target_pairs={{0,4},{4,0},{1,5},{5,1},{2,6},{6,2},{3,7},{7,3},{8,12},{12,8},{9,1... | collective-permute-start | bytes 984584 | tf_op jit(solution)/shard_map/ppermute | solution.py:17
  442.0 13.0 %copy-start.28 = (f32[72,2,2,128]{0,2,1,3:T(2,128)S(1)}, f32[72,2,2,128]{0,2,1,3:T(2,128)}, u32[]{:S(2)}) copy-start(f32[72,2,2,128]{0,2,1,3:T(2,128)} %get-tuple-element.283) | copy-start | bytes 442372
  468.0 6.0 collective-permute-start.7
  472.6 5.8 collective-permute-start.6
  502.4 35.7 %copy-start.57 = (f32[641]{0:T(1024)S(1)}, f32[641]{0:T(1024)}, u32[]{:S(2)}) copy-start(f32[641]{0:T(1024)} %param.39) | copy-start | bytes 7696
  502.4 35.7 %copy-start.163 = (f32[641]{0:T(1024)S(1)}, f32[641]{0:T(1024)}, u32[]{:S(2)}) copy-start(f32[641]{0:T(1024)} %param.40) | copy-start | bytes 7696
  502.4 35.7 %copy-start.183 = (f32[1282]{0:T(1024)S(1)}, f32[1282]{0:T(1024)}, u32[]{:S(2)}) copy-start(f32[1282]{0:T(1024)} %param.42) | copy-start | bytes 15388
  565.0 12.7 %copy-start.84 = (f32[3,2,1]{2,1,0:T(2,128)S(1)}, f32[3,2,1]{2,1,0:T(2,128)}, u32[]{:S(2)}) copy-start(f32[3,2,1]{2,1,0:T(2,128)} %get-tuple-element.332) | copy-start | bytes 76
  565.0 13.1 %copy-start.83 = (f32[3,2,1]{2,1,0:T(2,128)S(1)}, f32[3,2,1]{2,1,0:T(2,128)}, u32[]{:S(2)}) copy-start(f32[3,2,1]{2,1,0:T(2,128)} %get-tuple-element.331) | copy-start | bytes 76
  565.0 13.2 %copy-start.82 = (f32[3,2,1]{2,1,0:T(2,128)S(1)}, f32[3,2,1]{2,1,0:T(2,128)}, u32[]{:S(2)}) copy-start(f32[3,2,1]{2,1,0:T(2,128)} %get-tuple-element.330) | copy-start | bytes 76
  565.1 13.4 %copy-start.160 = (f32[3,1,25]{2,1,0:T(1,128)S(1)}, f32[3,1,25]{2,1,0:T(1,128)}, u32[]{:S(2)}) copy-start(f32[3,1,25]{2,1,0:T(1,128)} %get-tuple-element.372) | copy-start | bytes 904
  565.1 13.4 %copy-start.161 = (f32[3,1,25]{2,1,0:T(1,128)S(1)}, f32[3,1,25]{2,1,0:T(1,128)}, u32[]{:S(2)}) copy-start(f32[3,1,25]{2,1,0:T(1,128)} %get-tuple-element.373) | copy-start | bytes 904
  565.8 33.2 %collective-permute-start.13 = (bf16[1,3,641,2,128]{4,3,2,1,0:T(2,128)(2,1)S(1)}, bf16[1,3,641,2,128]{4,3,2,1,0:T(2,128)(2,1)}, u32[]{:S(2)}, u32[]{:S(2)}) collective-permute-start(bf16[1,3,641,2,128]{4,3,2,1,0:T(2,128)(2,1)S(1)} %copy.1657), channel_id=1, source_target_pairs={{4,0},{0,4},{5,1},{1,5},{6,2},{2,6},{7,3},{3,7},{12,8},{8,12},{13,... | collective-permute-start | bytes 2953736 | tf_op jit(solution)/shard_map/ppermute | solution.py:19
  567.1 33.3 %collective-permute-start.12 = (bf16[1,3,641,2,128]{4,3,2,1,0:T(2,128)(2,1)S(1)}, bf16[1,3,641,2,128]{4,3,2,1,0:T(2,128)(2,1)S(1)}, u32[]{:S(2)}, u32[]{:S(2)}) collective-permute-start(bf16[1,3,641,2,128]{4,3,2,1,0:T(2,128)(2,1)S(1)} %copy.1657), channel_id=1, source_target_pairs={{0,4},{4,0},{1,5},{5,1},{2,6},{6,2},{3,7},{7,3},{8,12},{12,8},{9,1... | collective-permute-start | bytes 2953736 | tf_op jit(solution)/shard_map/ppermute | solution.py:17
  608.6 7.3 collective-permute-start.15
  612.0 7.1 collective-permute-start.14
  678.0 3.9 collective-permute-start.17
  679.1 2.8 collective-permute-start.16
  682.0 12.6 %collective-permute-start.19 = (bf16[1,216,4,1]{3,1,2,0:T(8,128)(2,1)S(1)}, bf16[1,216,4,1]{3,1,2,0:T(8,128)(2,1)S(1)}, u32[]{:S(2)}, u32[]{:S(2)}) collective-permute-start(bf16[1,216,4,1]{3,1,2,0:T(8,128)(2,1)S(1)} %get-tuple-element.304), channel_id=1, source_target_pairs={{1,0},{2,1},{3,2},{0,3},{5,4},{6,5},{7,6},{4,7},{9,8},{10,9},{11,1... | collective-permute-start | bytes 5192 | tf_op jit(solution)/shard_map/ppermute | solution.py:19
  682.4 12.8 %copy-start.173 = (bf16[4]{0:T(256)(128)(2,1)S(1)}, bf16[4]{0:T(256)(128)(2,1)}, u32[]{:S(2)}) copy-start(bf16[4]{0:T(256)(128)(2,1)} %and_convert_fusion) | copy-start | bytes 28
  682.4 12.5 %collective-permute-start.18 = (bf16[1,216,4,1]{3,1,2,0:T(8,128)(2,1)S(1)}, bf16[1,216,4,1]{3,1,2,0:T(8,128)(2,1)S(1)}, u32[]{:S(2)}, u32[]{:S(2)}) collective-permute-start(bf16[1,216,4,1]{3,1,2,0:T(8,128)(2,1)S(1)} %get-tuple-element.303), channel_id=1, source_target_pairs={{0,1},{1,2},{2,3},{3,0},{4,5},{5,6},{6,7},{7,4},{8,9},{9,10},{10,1... | collective-permute-start | bytes 5192 | tf_op jit(solution)/shard_map/ppermute | solution.py:17
  701.0 308.3 %all-reduce.9.cloned.1.call-start = ((), (), s32[]{:S(2)}) async-start(), calls=%async_computation.1 | async-start | bytes 29343744 | tf_op jit(solution)/shard_map/psum | solution.py:327
  707.4 1.3 collective-permute-start.9
  707.5 1.4 collective-permute-start.8
  709.0 7.9 collective-permute-start.11
  709.8 12.1 %collective-permute-start.10 = (bf16[1,3,72,4,1]{4,2,1,3,0:T(8,128)(2,1)S(1)}, bf16[1,3,72,4,1]{4,2,1,3,0:T(8,128)(2,1)S(1)}, u32[]{:S(2)}, u32[]{:S(2)}) collective-permute-start(bf16[1,3,72,4,1]{4,2,1,3,0:T(8,128)(2,1)S(1)} %get-tuple-element.305), channel_id=1, source_target_pairs={{0,1},{1,2},{2,3},{3,0},{4,5},{5,6},{6,7},{7,4},{8,9},{9,10},{10,1... | collective-permute-start | bytes 5192 | tf_op jit(solution)/shard_map/ppermute | solution.py:17
  (161 other events, 661.2 us)
Sparse Core Ops, SparseCore 0:
  701.1 43.8 all-reduce.6
  752.6 256.6 all-reduce.8
where the time goes:
time: 1040 us; the launch traced here: 1030 us
  local copies, waits for them, and re-layouts  455 us (44%)
  waiting for transfers between devices  262 us (25%)
  blocking collectives  131 us (13%)
  other arithmetic  114 us (11%)
  matrix products  32.2 us (3%)
  starting transfers between devices  19.3 us (2%)
  between operations  18.4 us (2%)
    psum x1, waiting for transfers between devices, per_device(): lax.psum((enc_weight_grad, enc_bias_grad, gain_one_grad, shift_one_grad,...  241 us
    slice x50, local copies, waits for them, and re-layouts, disco_filter(): padded[..., top:top + stride * (row_count - 1) + 1:stride, left:left + st...  219 us
    mul x50, local copies, waits for them, and re-layouts, disco_filter(): weighted = weights[:, None, :, position, None] * sliced[..., None, :, :, :]  61.7 us
    slice x53, local copies, waits for them, and re-layouts, disco_filter(): weighted = weights[:, None, :, position, None] * sliced[..., None, :, :, :]  52.8 us
    psum x1, blocking collectives, per_device(): lax.psum((enc_weight_grad, enc_bias_grad, gain_one_grad, shift_one_grad,...  40.4 us
    psum x2, blocking collectives, norm_back(): lax.psum((jnp.sum(scaled, axis=(2, 3)), jnp.sum(scaled * standard, axis=(...  30.9 us
    psum x2, blocking collectives, normalize(): totals = lax.psum(jnp.sum(values, axis=(2, 3)), ('lat', 'lon'))  30.2 us
    psum x2, blocking collectives, normalize(): lax.psum(jnp.sum(centred * centred, axis=(2, 3)), ('lat', 'lon'))  29.8 us
  transfers between devices with their start and end apart: 22, of which 7 were waited for; matrix products, arithmetic and copies ran while one was open for 22% of the time, Pallas kernels for 0%

commit v1 on v0

v1 whole, which is shorter than its diff:
```python
import functools

import jax
import jax.numpy as jnp
from jax import lax
from jax.experimental import pallas as pl
from jax.experimental.pallas import tpu as pltpu
from jax.sharding import PartitionSpec as P

MESH = pl.DeviceIdType.MESH
f32 = jnp.float32
bf16 = jnp.bfloat16
i32 = jnp.int32
EPS = 1e-05
LANES = 128
AXES = ("ens", "lat", "lon")


def nn(a, b):
    return lax.dot_general(a, b, (((1,), (0,)), ((), ())), preferred_element_type=f32)


def nt(a, b):
    return lax.dot_general(a, b, (((1,), (1,)), ((), ())), preferred_element_type=f32)


def tn(a, b):
    return lax.dot_general(a, b, (((0,), (0,)), ((), ())), preferred_element_type=f32)


def up_to(n, m):
    return -(-n // m) * m


class Sizes:
    def __init__(self, mesh, state, noise, enc_taps, enc_weight, up_weight):
        self.ne, self.nl, self.nz = (mesh.shape[a] for a in AXES)
        self.dates, self.cin, self.full_rows, self.full_cols = state
        self.noise = noise[1]
        self.full_rows = state[2] // self.nl
        self.full_cols = state[3] // self.nz
        self.hr, self.hc = self.full_rows // 2, self.full_cols // 2
        assert self.hr == 2 and self.hc == LANES and self.ne == 4
        self.lat_total = enc_taps[1]
        self.nb = enc_taps[0]
        self.c = enc_weight[1]
        self.cj = enc_weight[2]
        self.ff = up_weight[0]
        self.px = self.hr * self.hc
        self.pixels = float(self.px * self.nl * self.nz)
        self.c5 = self.c // LANES
        self.f10 = self.ff // LANES
        self.r641 = up_to(self.c, 16)
        self.r1282 = up_to(self.ff, 16)
        self.r80 = up_to(self.cj, 16)
        self.off_down = self.c5 * self.r1282
        self.off_dec = self.off_down + self.f10 * self.r641
        used1 = self.off_dec + self.nb * self.c5 * self.r80
        used2 = self.nb * self.c5 * self.r641
        used3 = self.nb * self.c5 * self.r80
        many = 2 if self.nl == 2 else 1
        unit = 16 * self.nl * self.ne * self.nz
        self.colors = (many, many, 1, 1)
        self.rows = (
            up_to(used1, unit * many),
            up_to(used2, unit * many),
            up_to(used3, unit),
            up_to(24 * 6, unit // 2),
        )


def add_into(dst, at, sources, count):
    step = next(s for s in (256, 128, 64, 32, 16, 8) if count % s == 0)

    def body(n, carry):
        lo = pl.multiple_of(n * step, 8 if step == 8 else 16)
        there = pl.ds(pl.multiple_of(at + lo, 8 if step == 8 else 16), step)
        value = dst[there, :].astype(f32)
        for source in sources:
            value = value + source[pl.ds(lo, step), :].astype(f32)
        dst[there, :] = value.astype(dst.dtype)
        return carry

    lax.fori_loop(0, count // step, body, 0)


class Links:
    def __init__(self, z, sems=None):
        self.s = z
        self.sems = sems
        self.used = 0
        if sems is not None:
            self.e, self.l, self.z = (lax.axis_index(a) for a in AXES)

    def take(self):
        self.used += 1
        return self.used - 1

    def at(self, de, dl, dz):
        s = self.s
        return (
            lax.rem(self.e + (de + s.ne), s.ne),
            lax.rem(self.l + (dl + s.nl), s.nl),
            lax.rem(self.z + (dz + s.nz), s.nz),
        )

    def bit(self, which):
        return lax.rem(self.e // (1 << which), 2)

    def flip(self, which):
        return (self.e + (1 << which) * (1 - 2 * self.bit(which)), self.l, self.z)

    def has_up(self):
        return self.l > 0

    def has_down(self):
        return self.l < self.s.nl - 1


class Send:
    def __init__(self, links, src, dst, device, dl=0):
        self.links = links
        self.ids = (links.take(), links.take())
        self.what = (src, dst, device)
        self.dl = dl

    def copy(self):
        src, dst, device = self.what
        return pltpu.make_async_remote_copy(
            src_ref=src,
            dst_ref=dst,
            send_sem=self.links.sems.at[self.ids[0]],
            recv_sem=self.links.sems.at[self.ids[1]],
            device_id=device,
            device_id_type=MESH,
        )

    def under(self, sending, act):
        if self.dl == 0:
            act()
        else:
            up = (self.dl < 0) == sending
            pl.when(self.links.has_up() if up else self.links.has_down())(act)

    def start(self):
        self.under(True, lambda: self.copy().start())

    def wait_recv(self):
        self.under(False, lambda: self.copy().wait_recv())

    def wait_send(self):
        self.under(True, lambda: self.copy().wait_send())


class AllReduce:
    def __init__(self, links, partial, total, rows, colors, bufs, own_sems):
        s = links.s
        self.k, self.g, self.h, self.nc = links, partial, total, colors
        self.rc, self.r1, self.r2, self.rz = bufs
        self.own_sems = own_sems
        self.b0 = rows // s.nl
        self.b1 = self.b0 // colors
        self.half, self.quarter = self.b1 // 2, self.b1 // 4
        self.zs = self.quarter // s.nz
        self.sent = []
        self.waiting = []
        self.locals = []
        self.stage = 0
        al = lambda v: pl.multiple_of(v, 8)
        self.base, self.keep1, self.keep2, self.mine = [], [], [], []
        for c in range(colors):
            first, second = self.bits(c)
            base = links.l * self.b0 + c * self.b1
            keep1 = base + links.bit(first) * self.half
            keep2 = keep1 + links.bit(second) * self.quarter
            self.base.append(al(base))
            self.keep1.append(al(keep1))
            self.keep2.append(al(keep2))
            self.mine.append(al(keep2 + links.z * self.zs))

    @staticmethod
    def shapes(s, rows, colors, dtype):
        b0 = rows // s.nl
        b1 = b0 // colors
        return [
            pltpu.VMEM((s.nl - 1, b0, LANES), dtype),
            pltpu.VMEM((colors, b1 // 2, LANES), dtype),
            pltpu.VMEM((colors, b1 // 4, LANES), dtype),
            pltpu.VMEM((colors, s.nz - 1, b1 // 4 // s.nz, LANES), dtype),
        ]

    def bits(self, c):
        return (0, 1) if c == 0 else (1, 0)

    def send(self, src, dst, device):
        m = Send(self.k, src, dst, device)
        m.start()
        self.sent.append(m)
        self.waiting.append(m)

    def arrive(self):
        for m in self.waiting:
            m.wait_recv()
        self.waiting = []

    def step(self):
        k, s, g, h = self.k, self.k.s, self.g, self.h
        al = lambda v: pl.multiple_of(v, 8)
        stage, self.stage = self.stage, self.stage + 1
        colors = range(self.nc)
        self.arrive()
        if stage == 0:
            for d in range(1, s.nl):
                to = k.at(0, d, 0)
                self.send(g.at[pl.ds(al(to[1] * self.b0), self.b0)], self.rc.at[d - 1], to)
        elif stage == 1:
            add_into(g, self.base[0], [self.rc.at[d] for d in range(s.nl - 1)], self.b0)
            for c in colors:
                first = self.bits(c)[0]
                away = al(self.base[c] + (1 - k.bit(first)) * self.half)
                self.send(g.at[pl.ds(away, self.half)], self.r1.at[c], k.flip(first))
        elif stage == 2:
            for c in colors:
                add_into(g, self.keep1[c], [self.r1.at[c]], self.half)
                second = self.bits(c)[1]
                away = al(self.keep1[c] + (1 - k.bit(second)) * self.quarter)
                self.send(g.at[pl.ds(away, self.quarter)], self.r2.at[c], k.flip(second))
        elif stage == 3:
            for c in colors:
                add_into(g, self.keep2[c], [self.r2.at[c]], self.quarter)
                for d in range(1, s.nz):
                    to = k.at(0, 0, d)
                    away = al(self.keep2[c] + to[2] * self.zs)
                    self.send(g.at[pl.ds(away, self.zs)], self.rz.at[c, d - 1], to)
        elif stage == 4:
            for c in colors:
                add_into(g, self.mine[c], [self.rz.at[c, d] for d in range(s.nz - 1)], self.zs)
                here = pl.ds(self.mine[c], self.zs)
                for d in range(1, s.nz):
                    self.send(g.at[here], h.at[here], k.at(0, 0, d))
                own = pltpu.make_async_copy(g.at[here], h.at[here], self.own_sems.at[c])
                own.start()
                self.locals.append(own)
        elif stage == 5:
            for own in self.locals:
                own.wait()
            for c in colors:
                here = pl.ds(self.keep2[c], self.quarter)
                self.send(h.at[here], h.at[here], k.flip(self.bits(c)[1]))
        elif stage == 6:
            for c in colors:
                here = pl.ds(self.keep1[c], self.half)
                self.send(h.at[here], h.at[here], k.flip(self.bits(c)[0]))
        elif stage == 7:
            here = pl.ds(self.base[0], self.b0)
            for d in range(1, s.nl):
                self.send(h.at[here], h.at[here], k.at(0, d, 0))
        else:
            for m in self.sent:
                m.wait_send()

    stages = 9


def misc_slots():
    names = [
        ("down_bias", 1),
        ("up_bias", 2),
        ("gain_two", 1),
        ("shift_two", 1),
        ("proc_bias", 1),
        ("gain_one", 1),
        ("shift_one", 1),
        ("enc_bias", 1),
        ("up_last", 2),
        ("down_last", 2),
        ("proc_last", 3),
        ("enc_last", 3),
        ("dec_last", 3),
        ("dec_bias", 1),
    ]
    table, at = {}, 0
    for name, count in names:
        table[name] = at
        at += count
    return table


MISC = misc_slots()


def put_misc(misc, slot, row):
    width = row.shape[1]
    for t in range(-(-width // LANES)):
        lo, hi = t * LANES, min(width, (t + 1) * LANES)
        misc[slot * 6 + t : slot * 6 + t + 1, 0 : hi - lo] = row[:, lo:hi]


def get_misc(misc, slot, width):
    parts = []
    for t in range(-(-width // LANES)):
        lo, hi = t * LANES, min(width, (t + 1) * LANES)
        parts.append(misc[slot * 6 + t : slot * 6 + t + 1, 0 : hi - lo])
    return parts


def scratch_list(s):
    c, ff, px = s.c, s.ff, s.px
    big = s.full_cols
    wide = 8 * big + LANES
    V = pltpu.VMEM
    shapes = {
        "xin": V((160, s.full_rows, big), f32),
        "xj": V((160, wide), bf16),
        "eb": V((2, 160, LANES), bf16),
        "eslot": V((6, 160, LANES), bf16),
        "em": V((2, s.nb * LANES, 5 * big + LANES), bf16),
        "dm": V((2, s.nb * LANES, 6 * big + LANES), bf16),
        "tm": V((s.nb * px, 6 * LANES + 48), bf16),
        "ew": V((s.nb, c, s.cj), bf16),
        "pw": V((s.nb, c, c), bf16),
        "uw": V((ff, c), bf16),
        "dw": V((c, ff), bf16),
        "cw": V((s.nb, s.cin, c), bf16),
        "filte": V((s.nb, px, s.cj), bf16),
        "hx": V((6 * LANES + 48, c), f32),
        "nx": V((6 * LANES + 48, c), bf16),
        "pe": V((2, 8, c), f32),
        "filt": V((s.nb * px, c), bf16),
        "h1": V((px, c), f32),
        "n2": V((px, c), bf16),
        "hp": V((px, ff), f32),
        "ag": V((px, ff), f32),
        "act": V((px, ff), bf16),
        "hg": V((px, ff), bf16),
        "hgt": V((ff, px), bf16),
        "h2": V((px, c), bf16),
        "pgr": V((s.nb, px, s.cin), bf16),
        "projt": V((2, 80, s.nb * LANES), bf16),
        "partt": V((2, 80, s.nb * LANES), bf16),
        "two": V((px, c), f32),
        "mg": V((px, c), bf16),
        "mgt": V((c, px), bf16),
        "ntg": V((px, c), f32),
        "one": V((px, c), f32),
        "br": V((px, c), bf16),
        "brt": V((c, px), bf16),
        "fg": V((s.nb * px, c), bf16),
        "con": V((6 * LANES + 48, c), f32),
        "rup": V((px, c), f32),
        "rdn": V((px, c), f32),
        "reg": V((6, 8, c), f32),
        "ng": V((px, c), f32),
        "zg": V((px, c), bf16),
        "sgx": V((160, wide), f32),
        "sgb": V((160, 4 * big + LANES), bf16),
        "sgu": V((160, 2 * big), bf16),
        "sgd": V((160, 2 * big), bf16),
        "sge": V((6, 160, LANES), bf16),
        "orow": V((s.cin, s.full_rows, big), f32),
        "st7": V((s.ne, 80, 4 * big), bf16),
        "dates": V((s.ne, 8, LANES), f32),
        "cbt": V((8, LANES), f32),
        "slat": V((4, s.nl, 2, c), f32),
        "slon": V((4, s.nz, 2, c), f32),
        "g1": V((s.rows[0], LANES), bf16),
        "g2": V((s.rows[1], LANES), bf16),
        "g3": V((s.rows[2], LANES), bf16),
        "gm": V((s.rows[3], LANES), f32),
    }
    for i in range(4):
        kinds = AllReduce.shapes(s, s.rows[i], s.colors[i], f32 if i == 3 else bf16)
        for j, kind in enumerate(kinds):
            shapes[f"ar{i}_{j}"] = kind
    shapes["wsem"] = pltpu.SemaphoreType.DMA((5,))
    shapes["osem"] = pltpu.SemaphoreType.DMA((4, 2))
    return shapes


def sem_count(s):
    per = lambda nc: 2 * (2 * (s.nl - 1) + 4 * nc + 2 * nc * (s.nz - 1))
    total = sum(per(nc) for nc in s.colors)
    total += 2 * (8 + 8 + 8 + 8) + 2 * 2 * (s.ne - 1)
    total += 4 * 2 * (s.nl - 1 + s.nz - 1)
    return total + 8


def main_kernel(s, names, *refs):
    n_in, n_out = 22, 10
    (
        state, noise, cot, date_ref, reach, enc_taps, proc_taps, dec_taps,
        ew_h, eb, gain1, shift1, pw_h, pb, gain2, shift2, uw_h, ub, dw_h, db, cw_h, cb,
    ) = refs[:n_in]
    h1o, h2o, h3o, hmo, out, sgrad, m1o, v1o, m2o, v2o = refs[n_in : n_in + n_out]
    S = dict(zip(names, refs[n_in + n_out :]))
    sems = S["sems"]
    k = Links(s, sems)
    c, ff, px, nb, cin, cj = s.c, s.ff, s.px, s.nb, s.cin, s.cj
    big = s.full_cols
    l = k.l
    row0 = l * s.hr
    edge0 = 8 * big

    loads = {}
    for n, (name, src) in enumerate(
        (("ew", ew_h), ("pw", pw_h), ("uw", uw_h), ("dw", dw_h), ("cw", cw_h))
    ):
        loads[name] = pltpu.make_async_copy(src, S[name], S["wsem"].at[n])
        loads[name].start()

    date = date_ref[0]
    live = jnp.where(date >= 0, 1.0, 0.0).astype(f32)
    xin, xj = S["xin"], S["xj"]
    picked = jnp.zeros((cin, s.full_rows, big), f32)
    for d in range(s.dates):
        picked = picked + state[d].astype(f32) * jnp.where(date == d, 1.0, 0.0).astype(f32)
    xin[0:cin] = picked
    xin[cin:cj] = noise[0].astype(f32)
    xin[80 : 80 + cin] = cot[0].astype(f32) * live
    xin[80 + cin : 160] = jnp.zeros((160 - 80 - cin, s.full_rows, big), f32)
    lane = lax.broadcasted_iota(i32, (160, LANES), 1)
    left = jnp.zeros((160, LANES), f32)
    right = jnp.zeros((160, LANES), f32)
    for q in range(4):
        row = xin[:, q, :]
        xj[:, (2 + q) * big : (3 + q) * big] = row.astype(bf16)
        rows_there = [q + 2] + ([q + 6] if q < 2 else [q - 2])
        for r in rows_there:
            moved = pltpu.roll(row[:, 0:LANES], (r * 4 + 2) % LANES, 1)
            left = jnp.where((lane >> 1) == (r * 2 + 1), moved, left)
            moved = pltpu.roll(row[:, big - LANES : big], (r * 4 + 2) % LANES, 1)
            right = jnp.where((lane >> 1) == (r * 2), moved, right)
    S["eb"][0] = left.astype(bf16)
    S["eb"][1] = right.astype(bf16)
    S["dates"][k.e] = jnp.full((8, LANES), date.astype(f32), f32)

    @pl.when(jnp.logical_not(k.has_up()))
    def _():
        xj[:, 0 : 2 * big] = jnp.zeros((160, 2 * big), bf16)
        S["hx"][0:px] = jnp.zeros((px, c), f32)
        for side in range(2):
            S["hx"][768 + side * 8 : 776 + side * 8] = jnp.zeros((8, c), f32)

    @pl.when(jnp.logical_not(k.has_down()))
    def _():
        xj[:, 6 * big : 8 * big] = jnp.zeros((160, 2 * big), bf16)
        S["hx"][2 * px : 3 * px] = jnp.zeros((px, c), f32)
        for side in range(2):
            S["hx"][768 + 32 + side * 8 : 776 + 32 + side * 8] = jnp.zeros((8, c), f32)

    offsets = {(d, 0, 0) for d in range(1, s.ne)}
    offsets |= {(0, d, 0) for d in range(1, s.nl)} | {(0, 0, d) for d in range(1, s.nz)}
    offsets |= {(0, a % s.nl, b % s.nz) for a in (1, -1) for b in (1, -1)}
    offsets = sorted(offsets)
    barrier = pltpu.get_barrier_semaphore()
    for o in offsets:
        pl.semaphore_signal(barrier, 1, device_id=k.at(*o), device_id_type=MESH)
    pl.semaphore_wait(barrier, len(offsets))

    pending = []

    def start(sends):
        for m in sends:
            m.start()
        pending.extend(sends)
        return sends

    def arrive(sends):
        for m in sends:
            m.wait_recv()

    dirs = [(dl, ds) for dl in (-1, 0, 1) for ds in (-1, 1)]

    def slot_of(dl, ds):
        return (1 - dl) * 2 + (1 - ds) // 2

    sends = [
        Send(k, xj.at[:, pl.ds(2 * big, 2 * big)], xj.at[:, pl.ds(6 * big, 2 * big)], k.at(0, -1, 0), -1),
        Send(k, xj.at[:, pl.ds(4 * big, 2 * big)], xj.at[:, pl.ds(0, 2 * big)], k.at(0, 1, 0), 1),
    ]
    for dl, ds in dirs:
        sends.append(
            Send(k, S["eb"].at[(ds + 1) // 2], S["eslot"].at[slot_of(dl, ds)], k.at(0, dl, ds), dl)
        )
    first_halo = start(sends)
    date_sends = start(
        [
            Send(k, S["dates"].at[k.e], S["dates"].at[k.e], k.at(d, 0, 0))
            for d in range(1, s.ne)
        ]
    )

    gm = S["gm"]
    gm[0:144] = jnp.zeros((144, LANES), f32)

    def band(shape, column_of):
        rows = lax.broadcasted_iota(i32, shape, 0)
        cols = lax.broadcasted_iota(i32, shape, 1)
        return column_of(rows, cols)

    def pick(d, table, like):
        value = jnp.zeros(like, f32)
        for key, scalar in table:
            value = jnp.where(d == key, scalar, value)
        return value

    def inside(grow, total):
        return jnp.logical_and(grow >= 0, grow < total)

    def edge_lane(shape):
        at = lax.broadcasted_iota(i32, shape, 1)
        r, side, m = at >> 2, (at >> 1) & 1, at & 1
        return r, jnp.where(side == 0, m - 2, big + m), at

    def build_encoder():
        em = S["em"]
        d_main = band((LANES, big), lambda j, J: J - 2 * j)
        r, J, at = edge_lane((16, LANES))
        j = lax.broadcasted_iota(i32, (16, LANES), 0)
        codes = []
        for start_row in (0, LANES - 16):
            d = J - 2 * (j + start_row)
            codes.append(jnp.where(at < 32, r * 1024 + d, -5000))
        for i in range(2):
            reached = reach[row0 + i]
            edges = [[jnp.zeros((16, LANES), f32) for _ in range(2)] for _ in range(nb)]
            for a in range(-2, 3):
                r_in = 2 * i + a + 2
                ok = inside(4 * l + r_in - 2, 2 * s.lat_total)
                masks = [d_main == b for b in range(-2, 3)]
                for kk in range(nb):
                    value = jnp.zeros((LANES, big), f32)
                    for b in range(-2, 3):
                        tap = enc_taps[kk, row0 + i, 5 * (a + 2) + b + 2]
                        tap = jnp.where(jnp.logical_and(ok, abs(b) <= reached), tap, 0.0)
                        value = jnp.where(masks[b + 2], tap, value)
                        for part in range(2):
                            edges[kk][part] = jnp.where(
                                codes[part] == r_in * 1024 + b, tap, edges[kk][part]
                            )
                    em[i, kk * LANES : (kk + 1) * LANES, (a + 2) * big : (a + 3) * big] = value.astype(bf16)
            for kk in range(nb):
                lo = kk * LANES
                em[i, lo : lo + 16, 5 * big :] = edges[kk][0].astype(bf16)
                em[i, lo + 16 : lo + LANES - 16, 5 * big :] = jnp.zeros((LANES - 32, LANES), bf16)
                em[i, lo + LANES - 16 : lo + LANES, 5 * big :] = edges[kk][1].astype(bf16)

    def build_decoder():
        dm = S["dm"]
        d_main = band((LANES, big), lambda j, J: j - (J >> 1))
        r, J, at = edge_lane((16, LANES))
        j = lax.broadcasted_iota(i32, (16, LANES), 0)
        codes = []
        for start_row in (0, LANES - 16):
            d = (j + start_row) - (J >> 1)
            codes.append(jnp.where(at < 32, r * 1024 + d, -5000))
        for i in range(2):
            edges = [[jnp.zeros((16, LANES), f32) for _ in range(2)] for _ in range(nb)]
            for n in range(6):
                r_in = 2 * i + n
                a = i + 1 - r_in // 2
                full = 4 * l + r_in - 2
                ok = inside(full, 2 * s.lat_total)
                full = jnp.clip(full, 0, 2 * s.lat_total - 1)
                reached = reach[full // 2] - 1
                masks = [d_main == b for b in range(-1, 2)]
                for kk in range(nb):
                    value = jnp.zeros((LANES, big), f32)
                    for b in range(-1, 2):
                        tap = dec_taps[kk, full, 3 * (a + 1) + b + 1]
                        tap = jnp.where(jnp.logical_and(ok, abs(b) <= reached), tap, 0.0)
                        value = jnp.where(masks[b + 1], tap, value)
                        for part in range(2):
                            edges[kk][part] = jnp.where(
                                codes[part] == r_in * 1024 + b, tap, edges[kk][part]
                            )
                    dm[i, kk * LANES : (kk + 1) * LANES, n * big : (n + 1) * big] = value.astype(bf16)
            for kk in range(nb):
                lo = kk * LANES
                dm[i, lo : lo + 16, 6 * big :] = edges[kk][0].astype(bf16)
                dm[i, lo + 16 : lo + LANES - 16, 6 * big :] = jnp.zeros((LANES - 32, LANES), bf16)
                dm[i, lo + LANES - 16 : lo + LANES, 6 * big :] = edges[kk][1].astype(bf16)

    def build_processor():
        tm = S["tm"]
        d_main = band((LANES, LANES), lambda j, J: J - j)
        at = lax.broadcasted_iota(i32, (16, 48), 1)
        slot, idx = at >> 3, at & 7
        r = 2 * (slot >> 1) + (idx >> 1)
        m = idx & 1
        J = jnp.where((slot & 1) == 0, m - 2, LANES + m)
        j = lax.broadcasted_iota(i32, (16, 48), 0)
        codes = []
        for start_row in (0, LANES - 16):
            d = J - (j + start_row)
            codes.append(jnp.where(idx < 4, r * 1024 + d, -5000))
        for i in range(2):
            reached = reach[row0 + i]
            edges = [[jnp.zeros((16, 48), f32) for _ in range(2)] for _ in range(nb)]
            for r_in in range(6):
                a = r_in - 2 - i
                if abs(a) > 2:
                    for kk in range(nb):
                        lo = kk * px + i * LANES
                        tm[lo : lo + LANES, r_in * LANES : (r_in + 1) * LANES] = jnp.zeros((LANES, LANES), bf16)
                    continue
                ok = inside(row0 + r_in - 2, s.lat_total)
                masks = [d_main == b for b in range(-2, 3)]
                for kk in range(nb):
                    value = jnp.zeros((LANES, LANES), f32)
                    for b in range(-2, 3):
                        tap = proc_taps[kk, row0 + i, 5 * (a + 2) + b + 2]
                        tap = jnp.where(jnp.logical_and(ok, abs(b) <= reached), tap, 0.0)
                        value = jnp.where(masks[b + 2], tap, value)
                        for part in range(2):
                            edges[kk][part] = jnp.where(
                                codes[part] == r_in * 1024 + b, tap, edges[kk][part]
                            )
                    lo = kk * px + i * LANES
                    tm[lo : lo + LANES, r_in * LANES : (r_in + 1) * LANES] = value.astype(bf16)
            for kk in range(nb):
                lo = kk * px + i * LANES
                tm[lo : lo + 16, 768:816] = edges[kk][0].astype(bf16)
                tm[lo + 16 : lo + LANES - 16, 768:816] = jnp.zeros((LANES - 32, 48), bf16)
                tm[lo + LANES - 16 : lo + LANES, 768:816] = edges[kk][1].astype(bf16)

    slat, slon = S["slat"], S["slon"]

    def fold(values, kind, count):
        total_a, total_b = values[0]
        for a, b in values[1:]:
            total_a = total_a + a
            total_b = total_b + b
        if kind == "moments":
            total_a = total_a * (1.0 / len(values))
            for a, b in values:
                total_b = total_b + (a - total_a) * (a - total_a) * count
        return total_a, total_b

    def stat_start(rd, a, b):
        slat[rd, k.l, 0:1, :] = a
        slat[rd, k.l, 1:2, :] = b
        return start(
            [
                Send(k, slat.at[rd, k.l], slat.at[rd, k.l], k.at(0, d, 0))
                for d in range(1, s.nl)
            ]
        )

    def stat_middle(rd, sends, kind):
        arrive(sends)
        values = [(slat[rd, n, 0:1, :], slat[rd, n, 1:2, :]) for n in range(s.nl)]
        a, b = fold(values, kind, float(px))
        slon[rd, k.z, 0:1, :] = a
        slon[rd, k.z, 1:2, :] = b
        return start(
            [
                Send(k, slon.at[rd, k.z], slon.at[rd, k.z], k.at(0, 0, d))
                for d in range(1, s.nz)
            ]
        )

    def stat_end(rd, sends, kind):
        arrive(sends)
        values = [(slon[rd, n, 0:1, :], slon[rd, n, 1:2, :]) for n in range(s.nz)]
        return fold(values, kind, float(px * s.nl))

    def moments(values):
        mean = jnp.sum(values, axis=0, keepdims=True) * (1.0 / px)
        centred = values - mean
        return mean, jnp.sum(centred * centred, axis=0, keepdims=True)

    def vec(ref):
        n = ref.shape[0]
        return ref[...].reshape(1, n)

    build_encoder()

    arrive(first_halo)
    edge = jnp.zeros((160, LANES), f32)
    for sl in (-1, 0, 1):
        for ss in (-1, 1):
            there = S["eslot"][(sl + 1) * 2 + (ss + 1) // 2].astype(f32)
            r_lo, r_hi = {-1: (0, 2), 0: (2, 6), 1: (6, 8)}[sl]
            side = (ss + 1) // 2
            lo = r_lo * 4
            if sl == -1:
                lo = jnp.where(k.has_up(), lo, 1000)
            if sl == 1:
                lo = jnp.where(k.has_down(), lo, 1000)
            good = jnp.logical_and(lane >= lo, lane < r_hi * 4)
            good = jnp.logical_and(good, ((lane >> 1) & 1) == side)
            edge = jnp.where(good, there, edge)
    xj[:, edge0:] = edge.astype(bf16)

    filte, hx = S["filte"], S["hx"]
    for i in range(2):
        em = S["em"]
        got = nt(em[i, :, 0 : 5 * big], xj[0:80, 2 * i * big : (2 * i + 5) * big])
        got = got + nt(em[i, :, 5 * big :], xj[0:80, edge0:])
        for kk in range(nb):
            filte[kk, i * LANES : (i + 1) * LANES, :] = got[kk * LANES : (kk + 1) * LANES, 0:cj].astype(bf16)
    loads["ew"].wait()
    h0 = vec(eb) + jnp.zeros((px, c), f32)
    for kk in range(nb):
        h0 = h0 + nt(filte[kk], S["ew"][kk])
    hx[px : 2 * px, :] = h0
    own = slice(px, 2 * px)
    h0 = hx[own, :]
    stat_a = stat_start(0, *moments(h0))
    pe = S["pe"]
    for side, col in ((0, 0), (1, LANES - 2)):
        for q in range(2):
            lo = px + q * LANES + col
            pe[side, 2 * q : 2 * q + 2, :] = hx[lo : lo + 2, :]
            pe[side, 4 + 2 * q : 6 + 2 * q, :] = jnp.zeros((2, c), f32)
    sends = [
        Send(k, hx.at[pl.ds(px, px)], hx.at[pl.ds(2 * px, px)], k.at(0, -1, 0), -1),
        Send(k, hx.at[pl.ds(px, px)], hx.at[pl.ds(0, px)], k.at(0, 1, 0), 1),
    ]
    for dl, ds in dirs:
        sends.append(
            Send(
                k,
                pe.at[(ds + 1) // 2],
                hx.at[pl.ds(768 + slot_of(dl, ds) * 8, 8)],
                k.at(0, dl, ds),
                dl,
            )
        )
    zero_halo = start(sends)
    build_processor()
    stat_a = stat_middle(0, stat_a, "moments")

    build_decoder()
    dm, pgr = S["dm"], S["pgr"]
    for i in range(2):
        got = nt(dm[i, :, 0 : 6 * big], xj[80 : 80 + 80, 2 * i * big : (2 * i + 6) * big])
        got = got + nt(dm[i, :, 6 * big :], xj[80 : 80 + 80, edge0:])
        for kk in range(nb):
            pgr[kk, i * LANES : (i + 1) * LANES, :] = got[kk * LANES : (kk + 1) * LANES, 0:cin].astype(bf16)
    ones = jnp.ones((16, 4 * big), bf16)
    put_misc(gm, MISC["dec_bias"], nt(ones, xj[80:160, 2 * big : 6 * big])[0:1, 0:cin])

    mean1, m2 = stat_end(0, stat_a, "moments")
    var1 = m2 * (1.0 / s.pixels)
    rstd1 = lax.rsqrt(var1 + EPS)
    m1o[...] = mean1 * live
    v1o[...] = var1 * live
    arrive(zero_halo)
    nx = S["nx"]
    scale1 = rstd1 * vec(gain1)
    bias1 = vec(shift1)

    def norm_rows(n, carry):
        here = pl.ds(pl.multiple_of(n * 48, 16), 48)
        nx[here, :] = ((hx[here, :] - mean1) * scale1 + bias1).astype(bf16)
        return carry

    lax.fori_loop(0, 17, norm_rows, 0)

    filt, tm = S["filt"], S["tm"]
    loads["pw"].wait()
    h1 = S["h1"]
    acc = hx[own, :] + vec(pb)
    for kk in range(nb):
        here = slice(kk * px, (kk + 1) * px)
        filt[here, :] = nn(tm[here, :], nx[...]).astype(bf16)
        acc = acc + nt(filt[here, :], S["pw"][kk])
    h1[...] = acc
    stat_b = stat_start(1, *moments(h1[...]))
    loads["cw"].wait()
    two, mg = S["two"], S["mg"]
    acc = nn(pgr[0], S["cw"][0])
    for kk in range(1, nb):
        acc = acc + nn(pgr[kk], S["cw"][kk])
    two[...] = acc
    mg[...] = acc.astype(bf16)
    stat_b = stat_middle(1, stat_b, "moments")
    loads["dw"].wait()
    ag, hp = S["ag"], S["hp"]
    ag[...] = nn(mg[...], S["dw"][...])
    S["mgt"][...] = mg[...].T
    put_misc(gm, MISC["down_bias"], jnp.sum(mg[...].astype(f32), axis=0, keepdims=True))
    mean2, m2 = stat_end(1, stat_b, "moments")
    var2 = m2 * (1.0 / s.pixels)
    rstd2 = lax.rsqrt(var2 + EPS)
    m2o[...] = mean2 * live
    v2o[...] = var2 * live
    scale2 = rstd2 * vec(gain2)
    bias2 = vec(shift2)
    n2 = S["n2"]

    def norm_two_rows(n, carry):
        here = pl.ds(pl.multiple_of(n * 32, 16), 32)
        n2[here, :] = ((h1[here, :] - mean2) * scale2 + bias2).astype(bf16)
        return carry

    lax.fori_loop(0, px // 32, norm_two_rows, 0)

    loads["uw"].wait()
    hp[...] = nt(n2[...], S["uw"][...])
    act, hg = S["act"], S["hg"]
    ubias = vec(ub)
    root = 0.7978845608028654

    def gelu_rows(n, carry):
        here = pl.ds(pl.multiple_of(n * 16, 16), 16)
        v = hp[here, :] + ubias
        sq = v * v
        t = jnp.tanh(root * (v + 0.044715 * (sq * v)))
        act[here, :] = (0.5 * v * (1.0 + t)).astype(bf16)
        slope = 0.5 * (1.0 + t) + (0.5 * root) * v * (1.0 - t * t) * (1.0 + (3 * 0.044715) * sq)
        hg[here, :] = (slope * ag[here, :]).astype(bf16)
        return carry

    lax.fori_loop(0, px // 16, gelu_rows, 0)
    ntg = S["ntg"]
    ntg[...] = nn(hg[...], S["uw"][...])
    grad = ntg[...]
    standard = (h1[...] - mean2) * rstd2
    sum_a = jnp.sum(grad, axis=0, keepdims=True)
    sum_b = jnp.sum(grad * standard, axis=0, keepdims=True)
    put_misc(gm, MISC["shift_two"], sum_a)
    put_misc(gm, MISC["gain_two"], sum_b)
    stat_c = stat_start(2, sum_a, sum_b)

    g1 = S["g1"]
    cols = [(lo, min(256, s.c5 * LANES - lo)) for lo in range(0, s.c5 * LANES, 256)]

    def spread(g, off, height, pitch, value, lo, width):
        for n in range(width // LANES):
            at = off + (lo // LANES + n) * pitch
            g[at : at + height, :] = value[:, n * LANES : (n + 1) * LANES].astype(bf16)

    S["hgt"][...] = hg[...].T
    for lo, width in cols:
        spread(g1, 0, ff, s.r1282, nn(S["hgt"][...], n2[:, lo : lo + width]), lo, width)
    stat_c = stat_middle(2, stat_c, "sums")
    for lo in range(0, s.f10 * LANES, 256):
        spread(g1, s.off_down, c, s.r641, nn(S["mgt"][...], act[:, lo : lo + 256]), lo, 256)
    h2 = S["h2"]
    h2[...] = (h1[...] + nt(act[...], S["dw"][...]) + vec(db)).astype(bf16)
    for kk in range(nb):
        got = tn(pgr[kk], h2[:, 0 : s.c5 * LANES])
        spread(g1, s.off_dec + kk * s.c5 * s.r80, cin, s.r80, got, 0, s.c5 * LANES)
    ar1 = AllReduce(k, g1, h1o, s.rows[0], s.colors[0], [S[f"ar0_{j}"] for j in range(4)], S["osem"].at[0])
    ar1.step()

    def weighted(ref, column):
        return jnp.sum(ref.astype(f32) * column.astype(f32), axis=0, keepdims=True)

    def put_long(name, row):
        put_misc(gm, MISC[name], row[:, 0:768])
        put_misc(gm, MISC[name] + 1, row[:, 768:])

    put_long("up_bias", jnp.sum(hg[...].astype(f32), axis=0, keepdims=True))
    put_long("up_last", weighted(hg[...], n2[:, c - 1 : c]))
    for n in range(2):
        at = s.f10 * LANES + n
        put_misc(gm, MISC["down_last"] + n, weighted(mg[...], act[:, at : at + 1]))
    for kk in range(nb):
        put_misc(gm, MISC["dec_last"] + kk, weighted(pgr[kk], h2[:, c - 1 : c]))
    ar1.step()

    sum_a, sum_b = stat_end(2, stat_c, "sums")
    g_two = vec(gain2)
    part_a = g_two * sum_a * (1.0 / s.pixels)
    part_b = g_two * sum_b * (1.0 / s.pixels)
    one, br = S["one"], S["br"]

    def one_rows(n, carry):
        here = pl.ds(pl.multiple_of(n * 32, 16), 32)
        standard = (h1[here, :] - mean2) * rstd2
        value = rstd2 * (g_two * ntg[here, :] - part_a - standard * part_b) + two[here, :]
        one[here, :] = value
        br[here, :] = value.astype(bf16)
        return carry

    lax.fori_loop(0, px // 32, one_rows, 0)
    fg = S["fg"]
    for kk in range(nb):
        fg[kk * px : (kk + 1) * px, :] = nn(br[...], S["pw"][kk]).astype(bf16)
    con = S["con"]
    con[...] = tn(tm[...], fg[...])

    def sum_rows(n, carry):
        here = pl.ds(pl.multiple_of(n * 48, 16), 48)
        value = con[here, :]
        standard = (hx[here, :] - mean1) * rstd1
        return (
            carry[0] + jnp.sum(value, axis=0, keepdims=True),
            carry[1] + jnp.sum(value * standard, axis=0, keepdims=True),
        )

    zero_row = jnp.zeros((1, c), f32)
    sum_a, sum_b = lax.fori_loop(0, 17, sum_rows, (zero_row, zero_row))
    put_misc(gm, MISC["shift_one"], sum_a)
    put_misc(gm, MISC["gain_one"], sum_b)
    stat_d = stat_start(3, sum_a, sum_b)
    sends = [
        Send(k, con.at[pl.ds(0, px)], S["rdn"], k.at(0, -1, 0), -1),
        Send(k, con.at[pl.ds(2 * px, px)], S["rup"], k.at(0, 1, 0), 1),
    ]
    for dl, ds in dirs:
        mine = (dl + 1) * 2 + (ds + 1) // 2
        sends.append(
            Send(
                k,
                con.at[pl.ds(768 + mine * 8, 8)],
                S["reg"].at[slot_of(dl, ds)],
                k.at(0, dl, ds),
                dl,
            )
        )
    back_halo = start(sends)
    g2 = S["g2"]
    S["brt"][...] = br[...].T
    for kk in range(nb):
        if kk == 1:
            stat_d = stat_middle(3, stat_d, "sums")
        for lo, width in cols:
            got = nn(S["brt"][...], filt[kk * px : (kk + 1) * px, lo : lo + width])
            spread(g2, kk * s.c5 * s.r641, c, s.r641, got, lo, width)
    ar2 = AllReduce(k, g2, h2o, s.rows[1], s.colors[1], [S[f"ar1_{j}"] for j in range(4)], S["osem"].at[1])
    ar2.step()
    put_misc(gm, MISC["proc_bias"], jnp.sum(br[...].astype(f32), axis=0, keepdims=True))
    for kk in range(nb):
        put_misc(gm, MISC["proc_last"] + kk, weighted(br[...], filt[kk * px : (kk + 1) * px, c - 1 : c]))

    arrive(back_halo)
    ng = S["ng"]
    ng[...] = con[own, :]

    @pl.when(k.has_up())
    def _():
        ng[...] = ng[...] + S["rup"][...]

    @pl.when(k.has_down())
    def _():
        ng[...] = ng[...] + S["rdn"][...]

    def add_edges(sl):
        for ss in (-1, 1):
            got = S["reg"].at[(sl + 1) * 2 + (ss + 1) // 2]
            col = 0 if ss == -1 else LANES - 2
            for q in range(2):
                lo = q * LANES + col
                ng[lo : lo + 2, :] = ng[lo : lo + 2, :] + got[2 * q : 2 * q + 2, :]

    add_edges(0)
    pl.when(k.has_up())(lambda: add_edges(-1))
    pl.when(k.has_down())(lambda: add_edges(1))
    sum_a, sum_b = stat_end(3, stat_d, "sums")
    g_one = vec(gain1)
    part_a1 = g_one * sum_a * (1.0 / s.pixels)
    part_b1 = g_one * sum_b * (1.0 / s.pixels)
    zg = S["zg"]

    def zero_rows(n, carry):
        here = pl.ds(pl.multiple_of(n * 32, 16), 32)
        there = pl.ds(pl.multiple_of(px + n * 32, 16), 32)
        standard = (hx[there, :] - mean1) * rstd1
        value = rstd1 * (g_one * ng[here, :] - part_a1 - standard * part_b1) + one[here, :]
        zg[here, :] = value.astype(bf16)
        return carry

    lax.fori_loop(0, px // 32, zero_rows, 0)

    g3 = S["g3"]
    for kk in range(nb):
        got = tn(filte[kk], zg[:, 0 : s.c5 * LANES])
        spread(g3, kk * s.c5 * s.r80, cj, s.r80, got, 0, s.c5 * LANES)
        put_misc(gm, MISC["enc_last"] + kk, weighted(filte[kk], zg[:, c - 1 : c]))
    put_misc(gm, MISC["enc_bias"], jnp.sum(zg[...].astype(f32), axis=0, keepdims=True))
    ar3 = AllReduce(k, g3, h3o, s.rows[2], s.colors[2], [S[f"ar2_{j}"] for j in range(4)], S["osem"].at[2])
    ar4 = AllReduce(k, gm, hmo, s.rows[3], s.colors[3], [S[f"ar3_{j}"] for j in range(4)], S["osem"].at[3])
    ar3.step()
    ar4.step()
    ar1.step()
    ar2.step()

    projt, partt = S["projt"], S["partt"]
    for kk in range(nb):
        here = slice(kk * LANES, (kk + 1) * LANES)
        proj = nt(h2[...], S["cw"][kk])
        part = nn(zg[...], S["ew"][kk])[:, 0:cin]
        for i in range(2):
            for ref, value in ((projt, proj), (partt, part)):
                ref[i, 0:cin, here] = value[i * LANES : (i + 1) * LANES, :].T.astype(bf16)
                ref[i, cin:80, here] = jnp.zeros((80 - cin, LANES), bf16)
    sgx = S["sgx"]
    em = S["em"]
    sgx[...] = jnp.zeros(sgx.shape, f32)
    for i in range(2):
        lo = 2 * i * big
        got = nn(projt[i], dm[i])
        sgx[0:80, lo : lo + 6 * big] = sgx[0:80, lo : lo + 6 * big] + got[:, 0 : 6 * big]
        sgx[0:80, edge0:] = sgx[0:80, edge0:] + got[:, 6 * big :]
        got = nn(partt[i], em[i])
        sgx[80:160, lo : lo + 5 * big] = sgx[80:160, lo : lo + 5 * big] + got[:, 0 : 5 * big]
        sgx[80:160, edge0:] = sgx[80:160, edge0:] + got[:, 5 * big :]
    sgb, sgu, sgd, sge = S["sgb"], S["sgu"], S["sgd"], S["sge"]
    sgb[:, 0 : 2 * big] = sgx[:, 0 : 2 * big].astype(bf16)
    sgb[:, 2 * big : 4 * big] = sgx[:, 6 * big : 8 * big].astype(bf16)
    sgb[:, 4 * big :] = sgx[:, edge0:].astype(bf16)
    sends = [
        Send(k, sgb.at[:, pl.ds(0, 2 * big)], sgd, k.at(0, -1, 0), -1),
        Send(k, sgb.at[:, pl.ds(2 * big, 2 * big)], sgu, k.at(0, 1, 0), 1),
    ]
    for dl, ds in dirs:
        sends.append(
            Send(k, sgb.at[:, pl.ds(4 * big, LANES)], sge.at[slot_of(dl, ds)], k.at(0, dl, ds), dl)
        )
    out_halo = start(sends)
    ar3.step()
    ar4.step()
    ar1.step()
    ar2.step()
    arrive(out_halo)
    up_one = jnp.where(k.has_up(), 1, 0)
    down_one = jnp.where(k.has_down(), 1, 0)
    cbt = S["cbt"]
    cbt[...] = jnp.zeros((8, LANES), f32)
    cbt[0:1, 0:cin] = vec(cb)
    bias_col = cbt[...].T[0:cin, 0:1]
    orow, st7 = S["orow"], S["st7"]

    for q in range(4):
        lo = (2 + q) * big
        value = sgx[:, lo : lo + big]
        if q < 2:
            other = sgu[:, q * big : (q + 1) * big].astype(f32)
            value = value + jnp.where(up_one == 1, other, 0.0)
        else:
            other = sgd[:, (q - 2) * big : (q - 1) * big].astype(f32)
            value = value + jnp.where(down_one == 1, other, 0.0)
        head, tail = value[:, 0:LANES], value[:, big - LANES :]
        sources = [(0, q + 2, None)]
        sources += [(-1, q + 6, up_one)] if q < 2 else [(1, q - 2, down_one)]
        for sl, r, there in sources:
            for ss in (-1, 1):
                got = sge[(sl + 1) * 2 + (ss + 1) // 2].astype(f32)
                if ss == -1:
                    moved = pltpu.roll(got, (LANES - (r * 4 + 2)) % LANES, 1)
                    bound = 2 if there is None else there * 2
                    head = head + jnp.where(lane < bound, moved, 0.0)
                else:
                    moved = pltpu.roll(got, (2 * LANES - 2 - r * 4) % LANES, 1)
                    bound = LANES - 2 if there is None else LANES - there * 2
                    tail = tail + jnp.where(lane >= bound, moved, 0.0)
        orow[:, q, 0:LANES] = (head[0:cin] + bias_col) * live
        orow[:, q, LANES:big] = (tail[0:cin] + bias_col) * live
        st7[k.e, :, q * big : q * big + LANES] = head[80:160].astype(bf16)
        st7[k.e, :, q * big + LANES : (q + 1) * big] = tail[80:160].astype(bf16)
    out[0] = orow[...].astype(bf16)
    state_sends = start(
        [Send(k, st7.at[k.e], st7.at[k.e], k.at(d, 0, 0)) for d in range(1, s.ne)]
    )
    for _ in range(2):
        ar3.step()
        ar4.step()
        ar1.step()
        ar2.step()
    arrive(date_sends)
    arrive(state_sends)
    for d in range(s.dates):
        for q in range(4):
            value = jnp.zeros((80, big), f32)
            for n in range(s.ne):
                is_d = jnp.where(S["dates"][n, 0:1, :] == float(d), 1.0, 0.0)
                is_d = jnp.concatenate([is_d] * (big // LANES), axis=1)
                value = value + is_d * st7[n, :, q * big : (q + 1) * big].astype(f32)
            orow[:, q, :] = value[0:cin]
        sgrad[d] = orow[...].astype(bf16)

    rest = [ar1, ar2, ar3, ar4]
    while any(a.stage < AllReduce.stages for a in rest):
        for a in rest:
            if a.stage < AllReduce.stages:
                a.step()
    for m in pending:
        m.wait_send()


def finish_kernel(s, names, *refs):
    h1, h2, h3, hm = refs[:4]
    (
        enc_w, enc_b, g1o, s1o, proc_w, proc_b, g2o, s2o,
        up_w, up_b, down_w, down_b, dec_w, dec_b,
    ) = refs[4:18]
    c, ff, nb, cin, cj = s.c, s.ff, s.nb, s.cin, s.cj
    turned = hm[0:144, :].T

    def tall(slot, height):
        out = []
        for t in range(-(-height // LANES)):
            n = min(LANES, height - t * LANES)
            out.append((t * LANES, n, turned[0:n, slot * 6 + t : slot * 6 + t + 1]))
        return out

    last = s.c5 * LANES
    for n in range(s.c5):
        at = n * s.r1282
        up_w[:, n * LANES : (n + 1) * LANES] = h1[at : at + ff, :].astype(f32)
    for part in range(2):
        base = part * 768
        for lo, n, col in tall(MISC["up_last"] + part, min(768, ff - base)):
            up_w[base + lo : base + lo + n, last : last + 1] = col
    for n in range(s.f10):
        at = s.off_down + n * s.r641
        down_w[:, n * LANES : (n + 1) * LANES] = h1[at : at + c, :].astype(f32)
    for part in range(2):
        at = s.f10 * LANES + part
        for lo, n, col in tall(MISC["down_last"] + part, c):
            down_w[lo : lo + n, at : at + 1] = col
    for kk in range(nb):
        for n in range(s.c5):
            at = s.off_dec + (kk * s.c5 + n) * s.r80
            dec_w[kk, :, n * LANES : (n + 1) * LANES] = h1[at : at + cin, :].astype(f32)
            at = (kk * s.c5 + n) * s.r641
            proc_w[kk, :, n * LANES : (n + 1) * LANES] = h2[at : at + c, :].astype(f32)
            at = (kk * s.c5 + n) * s.r80
            enc_w[kk, n * LANES : (n + 1) * LANES, :] = h3[at : at + cj, :].astype(f32).T
        for lo, n, col in tall(MISC["dec_last"] + kk, cin):
            dec_w[kk, lo : lo + n, last : last + 1] = col
        for lo, n, col in tall(MISC["proc_last"] + kk, c):
            proc_w[kk, lo : lo + n, last : last + 1] = col
        enc_w[kk, last : last + 1, :] = get_misc(hm, MISC["enc_last"] + kk, cj)[0]

    def flat(ref, slots):
        at = 0
        for slot, width in slots:
            for piece in get_misc(hm, slot, width):
                n = piece.shape[1]
                ref[0:1, at : at + n] = piece
                at += n

    for ref, name in (
        (enc_b, "enc_bias"), (g1o, "gain_one"), (s1o, "shift_one"), (proc_b, "proc_bias"),
        (g2o, "gain_two"), (s2o, "shift_two"), (down_b, "down_bias"),
    ):
        flat(ref, [(MISC[name], c)])
    flat(up_b, [(MISC["up_bias"], 768), (MISC["up_bias"] + 1, ff - 768)])
    flat(dec_b, [(MISC["dec_bias"], cin)])


def per_device(s, *args):
    (
        state, noise, cot, slot_date, lon_reach, enc_taps, proc_taps, dec_taps,
        enc_weight, enc_bias, gain_one, shift_one, proc_weight, proc_bias, gain_two, shift_two,
        up_weight, up_bias, down_weight, down_bias, dec_weight, dec_bias,
    ) = args
    vm = pl.BlockSpec(memory_space=pltpu.VMEM)
    sm = pl.BlockSpec(memory_space=pltpu.SMEM)
    hbm = pl.BlockSpec(memory_space=pl.ANY)
    shapes = scratch_list(s)
    shapes["sems"] = pltpu.SemaphoreType.DMA((sem_count(s),))
    names = tuple(shapes)
    in_specs = [vm] * 3 + [sm] * 5 + [
        hbm, vm, vm, vm, hbm, vm, vm, vm, hbm, vm, hbm, vm, hbm, vm,
    ]
    sd = jax.ShapeDtypeStruct
    out_shape = [
        sd((s.rows[0], LANES), bf16),
        sd((s.rows[1], LANES), bf16),
        sd((s.rows[2], LANES), bf16),
        sd((s.rows[3], LANES), f32),
        sd((1, s.cin, s.full_rows, s.full_cols), bf16),
        sd((s.dates, s.cin, s.full_rows, s.full_cols), bf16),
    ] + [sd((1, s.c), f32)] * 4
    got = pl.pallas_call(
        functools.partial(main_kernel, s, names),
        out_shape=out_shape,
        in_specs=in_specs,
        out_specs=[hbm] * 4 + [vm] * 6,
        scratch_shapes=list(shapes.values()),
        compiler_params=pltpu.CompilerParams(
            collective_id=0, has_side_effects=True, vmem_limit_bytes=60 * 2**20
        ),
        name="forecast",
    )(*args)
    h1, h2, h3, hm, output, state_grad, mean1, var1, mean2, var2 = got
    c, ff, nb = s.c, s.ff, s.nb
    outs = [
        sd((nb, c, s.cj), f32), sd((1, c), f32), sd((1, c), f32), sd((1, c), f32),
        sd((nb, c, c), f32), sd((1, c), f32), sd((1, c), f32), sd((1, c), f32),
        sd((ff, c), f32), sd((1, ff), f32), sd((c, ff), f32), sd((1, c), f32),
        sd((nb, s.cin, c), f32), sd((1, s.cin), f32),
    ]
    grads = pl.pallas_call(
        functools.partial(finish_kernel, s, names),
        out_shape=outs,
        in_specs=[vm] * 4,
        out_specs=[vm] * len(outs),
        compiler_params=pltpu.CompilerParams(vmem_limit_bytes=60 * 2**20),
        name="finish",
    )(h1, h2, h3, hm)
    grads = [g.reshape(g.shape[1]) if g.shape[0] == 1 else g for g in grads]
    return (output, state_grad, *grads, mean1, var1, mean2, var2)


def solution(mesh):
    in_specs = (
        P(None, None, "lat", "lon"),
        P("ens", None, "lat", "lon"),
        P("ens", None, "lat", "lon"),
        P("ens"),
    ) + (P(),) * 18
    out_specs = (
        (P("ens", None, "lat", "lon"), P(None, None, "lat", "lon"))
        + (P(),) * 14
        + (P("ens", None),) * 4
    )

    def run(*args):
        s = Sizes(mesh, args[0].shape, args[1].shape, args[5].shape, args[8].shape, args[16].shape)
        return jax.shard_map(
            functools.partial(per_device, s),
            mesh=mesh,
            in_specs=in_specs,
            out_specs=out_specs,
            check_vma=False,
        )(*args)

    return run
```

time: 1040 us -> 157 us (0.15)
  local copies, waits for them, and re-layouts: 455 us -> 17.3 us
  waiting for transfers between devices: 262 us -> 0 us
  blocking collectives: 131 us -> 0 us
  Pallas kernels: 0 us -> 127 us
  other arithmetic: 114 us -> 10.3 us
  matrix products: 32.2 us -> 0 us
  starting transfers between devices: 19.3 us -> 0 us
  between operations: 18.4 us -> 1.34 us
    slice x176 -> x0, local copies, waits for them, and re-layouts: 308 us -> none  [the longest x50 219 us: disco_filter(): padded[..., top:top + stride * (row_count - 1) + 1:stride, left:left + st...]
    psum x2 -> x0, waiting for transfers between devices: 241 us -> none  [the longest x1 241 us: per_device(): lax.psum((enc_weight_grad, enc_bias_grad, gain_one_grad, shift_one_grad,...]
    psum x7 -> x0, blocking collectives: 131 us -> none  [the longest x1 40.4 us: per_device(): lax.psum((enc_weight_grad, enc_bias_grad, gain_one_grad, shift_one_grad,...]
    pallas_call x0 -> x2, Pallas kernels: none -> 127 us  [the longest x1 118 us: per_device(): pl.pallas_call(functools.partial(main_kernel, s, names), out_shape=out_sh...]
    mul x94 -> x0, local copies, waits for them, and re-layouts: 101 us -> none  [the longest x50 61.7 us: disco_filter(): weighted = weights[:, None, :, position, None] * sliced[..., None, :, :, :]]
    convert_element_type x53 -> x0, other arithmetic: 50.6 us -> none  [the longest x40 23.1 us: disco_filter(): weighted = weights[:, None, :, position, None] * sliced[..., None, :, :, :]]
    reduce_sum x33 -> x0, other arithmetic: 41.4 us -> none  [the longest x3 20.6 us: proc_adjoint(): weighted = jnp.sum(taps_now[None, :, None, :, None] * block, axis=1)]
    dot_general x16 -> x0, matrix products: 32.2 us -> none  [the longest x1 3.63 us: per_device(): jnp.einsum('cf,sfhw->schw', down_weight, activated, preferred_element_typ...]
  transfers between devices with their start and end apart: 22 -> 0, of which waited for: 7 -> 0; matrix products, arithmetic and copies ran while one was open for 22% -> 0% of each run, Pallas kernels for 0% -> 0%
where the time goes in v1:
time: 157 us; the launch traced here: 156 us
  Pallas kernels  127 us (81%)
  local copies, waits for them, and re-layouts  17.3 us (11%)
  other arithmetic  10.3 us (7%)
    pallas_call x1, Pallas kernels, per_device(): pl.pallas_call(functools.partial(main_kernel, s, names), out_shape=out_sh...  118 us
    unnamed x22, local copies, waits for them, and re-layouts  17.3 us
    pallas_call x8, other arithmetic, per_device(): pl.pallas_call(functools.partial(finish_kernel, s, names), out_shape=outs...  10.3 us
    pallas_call x1, Pallas kernels, per_device(): pl.pallas_call(functools.partial(finish_kernel, s, names), out_shape=outs...  9.14 us

profile of v1, /device:TPU:0, one launch (start us, length us, event | category | flops | bytes accessed | tf_op | source)
XLA Modules:
  0.0 156.3 jit_solution(6420614630146091138)
XLA Ops:
  1.3 2.0 %copy.42.refs_8_ = bf16[3,641,80]{2,1,0:T(8,128)(2,1)} copy(bf16[3,641,80]{1,2,0:T(8,128)(2,1)} %param.30) | data formatting | bytes 615360 | tf_op args[8]
  3.3 3.7 %copy.43.refs_16_ = bf16[1282,641]{1,0:T(8,128)(2,1)} copy(bf16[1282,641]{0,1:T(8,128)(2,1)} %param.38) | data formatting | bytes 3287048 | tf_op args[16]
  7.0 118.3 %forecast.1 = (bf16[14336,128]{1,0:T(8,128)(2,1)}, bf16[10240,128]{1,0:T(8,128)(2,1)}, bf16[1536,128]{1,0:T(8,128)(2,1)}, f32[256,128]{1,0:T(8,128)}, bf16[1,72,...) custom-call(bf16[2,72,4,256]{3,2,1,0:T(4,128)(2,1)} %refs_0_.1, ...), custom_call_target="tpu_custom_call" | custom-call | tf_op jit(solution)/shard_map/forecast/pallas_call | solution.py:1172
  125.3 9.1 %finish.1 = (f32[3,641,80]{2,1,0:T(8,128)}, f32[1,641]{1,0:T(1,128)}, f32[1,641]{1,0:T(1,128)}, f32[1,641]{1,0:T(1,128)}, f32[3,641,641]{2,1,0:T(8,128)}, /*inde...) custom-call(bf16[14336,128]{1,0:T(8,128)(2,1)} %get-tuple-element.46, ...), custom_call_target="tpu_custom_call" | custom-call | tf_op jit(solution)/shard_map/finish/pallas_call | solution.py:1191
  134.4 2.4 %copy.44 = f32[3,641,80]{1,2,0:T(8,128)} copy(f32[3,641,80]{2,1,0:T(8,128)} %get-tuple-element.70) | data formatting | bytes 1230720
  136.8 1.3 reduce
  138.1 1.3 reduce.1
  139.4 1.3 reduce.2
  140.7 1.3 reduce.3
  142.0 1.3 reduce.4
  143.3 1.3 reduce.5
  144.6 1.3 reduce.7
  145.8 1.3 reduce.6
  147.1 0.0 copy-start.1
  147.2 0.0 copy-start
  147.2 0.0 copy-start.5
  147.2 0.0 copy-start.4
  147.2 0.0 copy-start.3
  147.2 0.0 copy-start.2
  147.2 5.4 %copy.45 = f32[1282,641]{0,1:T(8,128)} copy(f32[1282,641]{1,0:T(8,128)} %get-tuple-element.78) | data formatting | bytes 6574096
  152.6 0.0 copy-done.1
  152.6 0.7 copy.53
  153.3 0.0 copy-done
  153.3 0.7 copy.54
  154.0 0.0 copy-done.5
  154.0 0.6 copy.55
  154.6 0.0 copy-done.4
  154.6 0.6 copy.56
  155.2 0.0 copy-done.3
  155.2 0.6 copy.57
  155.7 0.0 copy-done.2
  155.7 0.6 copy.58
Async XLA Ops:
  147.1 5.5 %copy-start.1 = (bf16[1,72,4,256]{3,2,1,0:T(4,128)(2,1)S(1)}, bf16[1,72,4,256]{3,2,1,0:T(4,128)(2,1)}, u32[]{:S(2)}) copy-start(bf16[1,72,4,256]{3,2,1,0:T(4,128)(2,1)} %get-tuple-element.108) | copy-start | bytes 442372
  147.2 6.1 %copy-start = (bf16[2,72,4,256]{3,2,1,0:T(4,128)(2,1)S(1)}, bf16[2,72,4,256]{3,2,1,0:T(4,128)(2,1)}, u32[]{:S(2)}) copy-start(bf16[2,72,4,256]{3,2,1,0:T(4,128)(2,1)} %get-tuple-element.109) | copy-start | bytes 884740
  147.2 6.8 %copy-start.5 = (f32[1,641]{1,0:T(1,128)S(1)}, f32[1,641]{1,0:T(1,128)}, u32[]{:S(2)}) copy-start(f32[1,641]{1,0:T(1,128)} %get-tuple-element.124) | copy-start | bytes 7696
  147.2 7.4 %copy-start.4 = (f32[1,641]{1,0:T(1,128)S(1)}, f32[1,641]{1,0:T(1,128)}, u32[]{:S(2)}) copy-start(f32[1,641]{1,0:T(1,128)} %get-tuple-element.125) | copy-start | bytes 7696
  147.2 8.0 %copy-start.3 = (f32[1,641]{1,0:T(1,128)S(1)}, f32[1,641]{1,0:T(1,128)}, u32[]{:S(2)}) copy-start(f32[1,641]{1,0:T(1,128)} %get-tuple-element.126) | copy-start | bytes 7696
  147.2 8.6 %copy-start.2 = (f32[1,641]{1,0:T(1,128)S(1)}, f32[1,641]{1,0:T(1,128)}, u32[]{:S(2)}) copy-start(f32[1,641]{1,0:T(1,128)} %get-tuple-element.127) | copy-start | bytes 7696

commit v2 on v1

--- a/solution.py
+++ b/solution.py
@@ -51,9 +51,8 @@
         self.c5 = self.c // LANES
         self.f10 = self.ff // LANES
         self.r641 = up_to(self.c, 16)
-        self.r1282 = up_to(self.ff, 16)
         self.r80 = up_to(self.cj, 16)
-        self.off_down = self.c5 * self.r1282
+        self.off_down = self.f10 * self.r641
         self.off_dec = self.off_down + self.f10 * self.r641
         used1 = self.off_dec + self.nb * self.c5 * self.r80
         used2 = self.nb * self.c5 * self.r641
@@ -317,9 +316,9 @@
         "em": V((2, s.nb * LANES, 5 * big + LANES), bf16),
         "dm": V((2, s.nb * LANES, 6 * big + LANES), bf16),
         "tm": V((s.nb * px, 6 * LANES + 48), bf16),
-        "ew": V((s.nb, c, s.cj), bf16),
+        "ew": V((s.nb, s.cj, c), bf16),
         "pw": V((s.nb, c, c), bf16),
-        "uw": V((ff, c), bf16),
+        "uw": V((c, ff), bf16),
         "dw": V((c, ff), bf16),
         "cw": V((s.nb, s.cin, c), bf16),
         "filte": V((s.nb, px, s.cj), bf16),
@@ -333,7 +332,7 @@
         "ag": V((px, ff), f32),
         "act": V((px, ff), bf16),
         "hg": V((px, ff), bf16),
-        "hgt": V((ff, px), bf16),
+        "n2t": V((c, px), bf16),
         "h2": V((px, c), bf16),
         "pgr": V((s.nb, px, s.cin), bf16),
         "projt": V((2, 80, s.nb * LANES), bf16),
@@ -703,7 +702,7 @@
     loads["ew"].wait()
     h0 = vec(eb) + jnp.zeros((px, c), f32)
     for kk in range(nb):
-        h0 = h0 + nt(filte[kk], S["ew"][kk])
+        h0 = h0 + nn(filte[kk], S["ew"][kk])
     hx[px : 2 * px, :] = h0
     own = slice(px, 2 * px)
     h0 = hx[own, :]
@@ -799,7 +798,7 @@
     lax.fori_loop(0, px // 32, norm_two_rows, 0)
 
     loads["uw"].wait()
-    hp[...] = nt(n2[...], S["uw"][...])
+    hp[...] = nn(n2[...], S["uw"][...])
     act, hg = S["act"], S["hg"]
     ubias = vec(ub)
     root = 0.7978845608028654
@@ -816,7 +815,7 @@
 
     lax.fori_loop(0, px // 16, gelu_rows, 0)
     ntg = S["ntg"]
-    ntg[...] = nn(hg[...], S["uw"][...])
+    ntg[...] = nt(hg[...], S["uw"][...])
     grad = ntg[...]
     standard = (h1[...] - mean2) * rstd2
     sum_a = jnp.sum(grad, axis=0, keepdims=True)
@@ -833,9 +832,9 @@
             at = off + (lo // LANES + n) * pitch
             g[at : at + height, :] = value[:, n * LANES : (n + 1) * LANES].astype(bf16)
 
-    S["hgt"][...] = hg[...].T
-    for lo, width in cols:
-        spread(g1, 0, ff, s.r1282, nn(S["hgt"][...], n2[:, lo : lo + width]), lo, width)
+    S["n2t"][...] = n2[...].T
+    for lo in range(0, s.f10 * LANES, 256):
+        spread(g1, 0, c, s.r641, nn(S["n2t"][...], hg[:, lo : lo + 256]), lo, 256)
     stat_c = stat_middle(2, stat_c, "sums")
     for lo in range(0, s.f10 * LANES, 256):
         spread(g1, s.off_down, c, s.r641, nn(S["mgt"][...], act[:, lo : lo + 256]), lo, 256)
@@ -855,9 +854,9 @@
         put_misc(gm, MISC[name] + 1, row[:, 768:])
 
     put_long("up_bias", jnp.sum(hg[...].astype(f32), axis=0, keepdims=True))
-    put_long("up_last", weighted(hg[...], n2[:, c - 1 : c]))
     for n in range(2):
         at = s.f10 * LANES + n
+        put_misc(gm, MISC["up_last"] + n, weighted(n2[...], hg[:, at : at + 1]))
         put_misc(gm, MISC["down_last"] + n, weighted(mg[...], act[:, at : at + 1]))
     for kk in range(nb):
         put_misc(gm, MISC["dec_last"] + kk, weighted(pgr[kk], h2[:, c - 1 : c]))
@@ -984,7 +983,7 @@
     for kk in range(nb):
         here = slice(kk * LANES, (kk + 1) * LANES)
         proj = nt(h2[...], S["cw"][kk])
-        part = nn(zg[...], S["ew"][kk])[:, 0:cin]
+        part = nt(zg[...], S["ew"][kk])[:, 0:cin]
         for i in range(2):
             for ref, value in ((projt, proj), (partt, part)):
                 ref[i, 0:cin, here] = value[i * LANES : (i + 1) * LANES, :].T.astype(bf16)
@@ -1083,58 +1082,84 @@
         m.wait_send()
 
 
-def finish_kernel(s, names, *refs):
-    h1, h2, h3, hm = refs[:4]
+def finish_kernel(s, *refs):
+    h1, h2, h3, hm, output_in, state_in, m1, v1, m2, v2 = refs[:10]
     (
+        output, state_grad,
         enc_w, enc_b, g1o, s1o, proc_w, proc_b, g2o, s2o,
-        up_w, up_b, down_w, down_b, dec_w, dec_b,
-    ) = refs[4:18]
+        up_w, up_b, down_w, down_b, dec_w, dec_b, m1o, v1o, m2o, v2o,
+    ) = refs[10:30]
+    (b1, b2, b3, enc_v, proc_v, up_v, down_v, dec_v, row_v, sem_in, sem_out) = refs[30:]
     c, ff, nb, cin, cj = s.c, s.ff, s.nb, s.cin, s.cj
+    used1 = s.off_dec + nb * s.c5 * s.r80
+    third = s.c5 * s.r641
+    pieces = [(h2, b2, n * third, third) for n in range(nb)]
+    pieces += [(h1, b1, 0, s.off_down), (h1, b1, s.off_down, s.off_dec - s.off_down)]
+    pieces += [(h1, b1, s.off_dec, used1 - s.off_dec), (h3, b3, 0, nb * s.c5 * s.r80)]
+    loads = [
+        pltpu.make_async_copy(a.at[pl.ds(at, n)], b.at[pl.ds(at, n)], sem_in.at[i])
+        for i, (a, b, at, n) in enumerate(pieces)
+    ]
+    for copy in loads:
+        copy.start()
+    stores = []
+
+    def store(src, dst):
+        copy = pltpu.make_async_copy(src, dst, sem_out.at[len(stores)])
+        copy.start()
+        stores.append(copy)
+
+    store(output_in, output)
+    store(state_in, state_grad)
+    for a, b in ((m1, m1o), (v1, v1o), (m2, m2o), (v2, v2o)):
+        b[...] = a[...]
     turned = hm[0:144, :].T
 
-    def tall(slot, height):
-        out = []
+    def last_column(ref, slot, height, at):
         for t in range(-(-height // LANES)):
             n = min(LANES, height - t * LANES)
-            out.append((t * LANES, n, turned[0:n, slot * 6 + t : slot * 6 + t + 1]))
-        return out
+            ref[t * LANES : t * LANES + n, at : at + 1] = turned[0:n, slot * 6 + t : slot * 6 + t + 1]
+
+    def widen(ref, src, base, pitch, height, tiles):
+        for n in range(tiles):
+            at = base + n * pitch
+            ref[:, n * LANES : (n + 1) * LANES] = src[at : at + height, :].astype(f32)
 
     last = s.c5 * LANES
-    for n in range(s.c5):
-        at = n * s.r1282
-        up_w[:, n * LANES : (n + 1) * LANES] = h1[at : at + ff, :].astype(f32)
-    for part in range(2):
-        base = part * 768
-        for lo, n, col in tall(MISC["up_last"] + part, min(768, ff - base)):
-            up_w[base + lo : base + lo + n, last : last + 1] = col
-    for n in range(s.f10):
-        at = s.off_down + n * s.r641
-        down_w[:, n * LANES : (n + 1) * LANES] = h1[at : at + c, :].astype(f32)
-    for part in range(2):
-        at = s.f10 * LANES + part
-        for lo, n, col in tall(MISC["down_last"] + part, c):
-            down_w[lo : lo + n, at : at + 1] = col
     for kk in range(nb):
-        for n in range(s.c5):
-            at = s.off_dec + (kk * s.c5 + n) * s.r80
-            dec_w[kk, :, n * LANES : (n + 1) * LANES] = h1[at : at + cin, :].astype(f32)
-            at = (kk * s.c5 + n) * s.r641
-            proc_w[kk, :, n * LANES : (n + 1) * LANES] = h2[at : at + c, :].astype(f32)
-            at = (kk * s.c5 + n) * s.r80
-            enc_w[kk, n * LANES : (n + 1) * LANES, :] = h3[at : at + cj, :].astype(f32).T
-        for lo, n, col in tall(MISC["dec_last"] + kk, cin):
-            dec_w[kk, lo : lo + n, last : last + 1] = col
-        for lo, n, col in tall(MISC["proc_last"] + kk, c):
-            proc_w[kk, lo : lo + n, last : last + 1] = col
-        enc_w[kk, last : last + 1, :] = get_misc(hm, MISC["enc_last"] + kk, cj)[0]
+        ref = proc_v.at[kk]
+        last_column(ref, MISC["proc_last"] + kk, c, last)
+        loads[kk].wait()
+        widen(ref, b2, kk * third, s.r641, c, s.c5)
+        store(ref, proc_w.at[kk])
+    for n, (ref, name, base, to) in enumerate(
+        ((up_v, "up_last", 0, up_w), (down_v, "down_last", s.off_down, down_w))
+    ):
+        for part in range(2):
+            last_column(ref, MISC[name] + part, c, s.f10 * LANES + part)
+        loads[nb + n].wait()
+        widen(ref, b1, base, s.r641, c, s.f10)
+        store(ref, to)
+    loads[nb + 2].wait()
+    loads[nb + 3].wait()
+    for kk in range(nb):
+        ref = dec_v.at[kk]
+        last_column(ref, MISC["dec_last"] + kk, cin, last)
+        widen(ref, b1, s.off_dec + kk * s.c5 * s.r80, s.r80, cin, s.c5)
+        ref = enc_v.at[kk]
+        last_column(ref, MISC["enc_last"] + kk, cj, last)
+        widen(ref, b3, kk * s.c5 * s.r80, s.r80, cj, s.c5)
+    store(dec_v, dec_w)
+    store(enc_v, enc_w)
 
     def flat(ref, slots):
         at = 0
         for slot, width in slots:
             for piece in get_misc(hm, slot, width):
                 n = piece.shape[1]
-                ref[0:1, at : at + n] = piece
+                row_v[0:1, at : at + n] = piece
                 at += n
+        ref[...] = row_v[0:1, 0:at].reshape(at)
 
     for ref, name in (
         (enc_b, "enc_bias"), (g1o, "gain_one"), (s1o, "shift_one"), (proc_b, "proc_bias"),
@@ -1143,6 +1168,8 @@
         flat(ref, [(MISC[name], c)])
     flat(up_b, [(MISC["up_bias"], 768), (MISC["up_bias"] + 1, ff - 768)])
     flat(dec_b, [(MISC["dec_bias"], cin)])
+    for copy in stores:
+        copy.wait()
 
 
 def per_device(s, *args):
@@ -1151,6 +1178,9 @@
         enc_weight, enc_bias, gain_one, shift_one, proc_weight, proc_bias, gain_two, shift_two,
         up_weight, up_bias, down_weight, down_bias, dec_weight, dec_bias,
     ) = args
+    args = list(args)
+    args[8] = jnp.swapaxes(enc_weight, 1, 2)
+    args[16] = up_weight.T
     vm = pl.BlockSpec(memory_space=pltpu.VMEM)
     sm = pl.BlockSpec(memory_space=pltpu.SMEM)
     hbm = pl.BlockSpec(memory_space=pl.ANY)
@@ -1180,24 +1210,33 @@
         ),
         name="forecast",
     )(*args)
-    h1, h2, h3, hm, output, state_grad, mean1, var1, mean2, var2 = got
     c, ff, nb = s.c, s.ff, s.nb
-    outs = [
-        sd((nb, c, s.cj), f32), sd((1, c), f32), sd((1, c), f32), sd((1, c), f32),
-        sd((nb, c, c), f32), sd((1, c), f32), sd((1, c), f32), sd((1, c), f32),
-        sd((ff, c), f32), sd((1, ff), f32), sd((c, ff), f32), sd((1, c), f32),
-        sd((nb, s.cin, c), f32), sd((1, s.cin), f32),
-    ]
-    grads = pl.pallas_call(
-        functools.partial(finish_kernel, s, names),
+    outs = [out_shape[4], out_shape[5]] + [
+        sd((nb, s.cj, c), f32), sd((c,), f32), sd((c,), f32), sd((c,), f32),
+        sd((nb, c, c), f32), sd((c,), f32), sd((c,), f32), sd((c,), f32),
+        sd((c, ff), f32), sd((ff,), f32), sd((c, ff), f32), sd((c,), f32),
+        sd((nb, s.cin, c), f32), sd((s.cin,), f32),
+    ] + [sd((1, c), f32)] * 4
+    large = (0, 1, 2, 6, 10, 12, 14)
+    V = pltpu.VMEM
+    done = pl.pallas_call(
+        functools.partial(finish_kernel, s),
         out_shape=outs,
-        in_specs=[vm] * 4,
-        out_specs=[vm] * len(outs),
+        in_specs=[hbm] * 3 + [vm] + [hbm] * 2 + [vm] * 4,
+        out_specs=[hbm if n in large else vm for n in range(len(outs))],
+        scratch_shapes=[
+            V((s.rows[0], LANES), bf16), V((s.rows[1], LANES), bf16), V((s.rows[2], LANES), bf16),
+            V((nb, s.cj, c), f32), V((nb, c, c), f32), V((c, ff), f32), V((c, ff), f32),
+            V((nb, s.cin, c), f32), V((8, up_to(ff, LANES)), f32),
+            pltpu.SemaphoreType.DMA((8,)), pltpu.SemaphoreType.DMA((16,)),
+        ],
         compiler_params=pltpu.CompilerParams(vmem_limit_bytes=60 * 2**20),
         name="finish",
-    )(h1, h2, h3, hm)
-    grads = [g.reshape(g.shape[1]) if g.shape[0] == 1 else g for g in grads]
-    return (output, state_grad, *grads, mean1, var1, mean2, var2)
+    )(*got)
+    done = list(done)
+    done[2] = jnp.swapaxes(done[2], 1, 2)
+    done[10] = done[10].T
+    return tuple(done)
 
 
 def solution(mesh):

time: 157 us -> 137 us (0.87)
  local copies, waits for them, and re-layouts: 17.3 us -> 0 us
  other arithmetic: 10.3 us -> 0 us
  Pallas kernels: 127 us -> 135 us
    unnamed x22 -> x0, local copies, waits for them, and re-layouts: 17.3 us -> none
    pallas_call x8 -> x0, other arithmetic: 10.3 us -> none  [per_device(): pl.pallas_call(functools.partial(finish_kernel, s, names), out_shape=outs...]
    pallas_call x1, Pallas kernels: 9.14 us -> 16.3 us  [per_device(): pl.pallas_call(functools.partial(finish_kernel, s), out_shape=outs, in_sp...]
where the time goes in v2:
time: 137 us; the launch traced here: 136 us
  Pallas kernels  135 us (99%)
  between operations  1.5 us (1%)
    pallas_call x1, Pallas kernels, per_device(): pl.pallas_call(functools.partial(main_kernel, s, names), out_shape=out_sh...  118 us
    pallas_call x1, Pallas kernels, per_device(): pl.pallas_call(functools.partial(finish_kernel, s), out_shape=outs, in_sp...  16.3 us

profile of v2, /device:TPU:0, one launch (start us, length us, event | category | flops | bytes accessed | tf_op | source)
XLA Modules:
  0.0 136.1 jit_solution(9189796608134698389)
XLA Ops:
  1.3 118.3 %forecast.1 = (bf16[14336,128]{1,0:T(8,128)(2,1)}, bf16[10240,128]{1,0:T(8,128)(2,1)}, bf16[1536,128]{1,0:T(8,128)(2,1)}, f32[256,128]{1,0:T(8,128)}, bf16[1,72,...) custom-call(bf16[2,72,4,256]{3,2,1,0:T(4,128)(2,1)} %refs_0_.1, ...), custom_call_target="tpu_custom_call" | custom-call | tf_op jit(solution)/shard_map/forecast/pallas_call | solution.py:1202
  119.6 16.3 %finish.1 = (bf16[1,72,4,256]{3,2,1,0:T(4,128)(2,1)}, bf16[2,72,4,256]{3,2,1,0:T(4,128)(2,1)}, f32[3,80,641]{2,1,0:T(8,128)}, f32[641]{0:T(1024)}, f32[641]{0:T(...) custom-call(bf16[14336,128]{1,0:T(8,128)(2,1)} %get-tuple-element.50, ...), custom_call_target="tpu_custom_call" | custom-call | tf_op jit(solution)/shard_map/finish/pallas_call | solution.py:1222

commit v3 on v2

--- a/solution.py
+++ b/solution.py
@@ -14,6 +14,8 @@
 EPS = 1e-05
 LANES = 128
 AXES = ("ens", "lat", "lon")
+ROUTE_X = ("lat", "bit0", "bit1", "lon")
+ROUTE_Y = ("lat", "bit1", "bit0", "lon")
 
 
 def nn(a, b):
@@ -52,20 +54,32 @@
         self.f10 = self.ff // LANES
         self.r641 = up_to(self.c, 16)
         self.r80 = up_to(self.cj, 16)
-        self.off_down = self.f10 * self.r641
-        self.off_dec = self.off_down + self.f10 * self.r641
-        used1 = self.off_dec + self.nb * self.c5 * self.r80
-        used2 = self.nb * self.c5 * self.r641
-        used3 = self.nb * self.c5 * self.r80
-        many = 2 if self.nl == 2 else 1
+        self.off_up = self.f10 * self.r641
+        self.off_dec = self.off_up + self.f10 * self.r641
+        used = (
+            self.off_dec + self.nb * self.c5 * self.r80,
+            self.nb * self.c5 * self.r641,
+            self.nb * self.c5 * self.r80,
+        )
         unit = 16 * self.nl * self.ne * self.nz
-        self.colors = (many, many, 1, 1)
-        self.rows = (
-            up_to(used1, unit * many),
-            up_to(used2, unit * many),
-            up_to(used3, unit),
-            up_to(24 * 6, unit // 2),
-        )
+        self.rows = tuple(up_to(n, unit) for n in used) + (up_to(24 * 6, unit // 2),)
+        self.chunks = {}
+
+        def split(name, buffer, lo, hi):
+            first = lo + up_to((hi - lo) // 2, unit)
+            for n, (a, b, route) in enumerate(((lo, first, ROUTE_X), (first, hi, ROUTE_Y))):
+                if b > a:
+                    self.chunks[name + str(n)] = (buffer, a, b - a, route)
+
+        cut = self.off_up // unit * unit
+        split("A", 0, 0, cut)
+        split("B", 0, cut, self.rows[0])
+        cut = 2 * self.c5 * self.r641 // unit * unit
+        split("C", 1, 0, cut)
+        split("D", 1, cut, self.rows[1])
+        self.chunks["E0"] = (2, 0, self.rows[2], ROUTE_X)
+        self.chunks["M0"] = (3, 0, self.rows[3], ROUTE_Y)
+        self.group = self.nl * self.nz
 
 
 def add_into(dst, at, sources, count):
@@ -152,44 +166,48 @@
 
 
 class AllReduce:
-    def __init__(self, links, partial, total, rows, colors, bufs, own_sems):
-        s = links.s
-        self.k, self.g, self.h, self.nc = links, partial, total, colors
-        self.rc, self.r1, self.r2, self.rz = bufs
-        self.own_sems = own_sems
-        self.b0 = rows // s.nl
-        self.b1 = self.b0 // colors
-        self.half, self.quarter = self.b1 // 2, self.b1 // 4
-        self.zs = self.quarter // s.nz
-        self.sent = []
-        self.waiting = []
-        self.locals = []
+    def __init__(self, links, partial, total, lo, rows, route, bufs, own_sem):
+        self.k, self.g, self.h, self.route = links, partial, total, route
+        self.bufs, self.own_sem = bufs, own_sem
+        self.sent, self.waiting = [], []
         self.stage = 0
-        al = lambda v: pl.multiple_of(v, 8)
-        self.base, self.keep1, self.keep2, self.mine = [], [], [], []
-        for c in range(colors):
-            first, second = self.bits(c)
-            base = links.l * self.b0 + c * self.b1
-            keep1 = base + links.bit(first) * self.half
-            keep2 = keep1 + links.bit(second) * self.quarter
-            self.base.append(al(base))
-            self.keep1.append(al(keep1))
-            self.keep2.append(al(keep2))
-            self.mine.append(al(keep2 + links.z * self.zs))
+        self.base, self.part = [], []
+        base, size = lo, rows
+        for axis in route:
+            size = size // self.count(links.s, axis)
+            self.base.append(base)
+            self.part.append(size)
+            base = base + self.index(axis) * size
+        self.base.append(base)
+        self.last_stage = 2 * len(route)
 
     @staticmethod
-    def shapes(s, rows, colors, dtype):
-        b0 = rows // s.nl
-        b1 = b0 // colors
-        return [
-            pltpu.VMEM((s.nl - 1, b0, LANES), dtype),
-            pltpu.VMEM((colors, b1 // 2, LANES), dtype),
-            pltpu.VMEM((colors, b1 // 4, LANES), dtype),
-            pltpu.VMEM((colors, s.nz - 1, b1 // 4 // s.nz, LANES), dtype),
-        ]
-
-    def bits(self, c):
-        return (0, 1) if c == 0 else (1, 0)
+    def count(s, axis):
+        return {"lat": s.nl, "lon": s.nz}.get(axis, 2)
+
+    @staticmethod
+    def shapes(s, rows, route, dtype):
+        out = []
+        for axis in route:
+            n = AllReduce.count(s, axis)
+            rows = rows // n
+            out.append(pltpu.VMEM((n - 1, rows, LANES), dtype))
+        return out
+
+    def index(self, axis):
+        k = self.k
+        return {"lat": k.l, "lon": k.z}[axis] if axis in ("lat", "lon") else k.bit(int(axis[3:]))
+
+    def others(self, axis):
+        k, s = self.k, self.k.s
+        if axis == "lat":
+            devices = [k.at(0, d, 0) for d in range(1, s.nl)]
+            return [(dev, dev[1], n) for n, dev in enumerate(devices)]
+        if axis == "lon":
+            devices = [k.at(0, 0, d) for d in range(1, s.nz)]
+            return [(dev, dev[2], n) for n, dev in enumerate(devices)]
+        which = int(axis[3:])
+        return [(k.flip(which), 1 - k.bit(which), 0)]
 
     def send(self, src, dst, device):
         m = Send(self.k, src, dst, device)
@@ -197,68 +215,39 @@
         self.sent.append(m)
         self.waiting.append(m)
 
-    def arrive(self):
+    def step(self):
+        g, h, route = self.g, self.h, self.route
+        al = lambda v: pl.multiple_of(v, 8)
+        stage, self.stage = self.stage, self.stage + 1
         for m in self.waiting:
             m.wait_recv()
         self.waiting = []
-
-    def step(self):
-        k, s, g, h = self.k, self.k.s, self.g, self.h
-        al = lambda v: pl.multiple_of(v, 8)
-        stage, self.stage = self.stage, self.stage + 1
-        colors = range(self.nc)
-        self.arrive()
-        if stage == 0:
-            for d in range(1, s.nl):
-                to = k.at(0, d, 0)
-                self.send(g.at[pl.ds(al(to[1] * self.b0), self.b0)], self.rc.at[d - 1], to)
-        elif stage == 1:
-            add_into(g, self.base[0], [self.rc.at[d] for d in range(s.nl - 1)], self.b0)
-            for c in colors:
-                first = self.bits(c)[0]
-                away = al(self.base[c] + (1 - k.bit(first)) * self.half)
-                self.send(g.at[pl.ds(away, self.half)], self.r1.at[c], k.flip(first))
-        elif stage == 2:
-            for c in colors:
-                add_into(g, self.keep1[c], [self.r1.at[c]], self.half)
-                second = self.bits(c)[1]
-                away = al(self.keep1[c] + (1 - k.bit(second)) * self.quarter)
-                self.send(g.at[pl.ds(away, self.quarter)], self.r2.at[c], k.flip(second))
-        elif stage == 3:
-            for c in colors:
-                add_into(g, self.keep2[c], [self.r2.at[c]], self.quarter)
-                for d in range(1, s.nz):
-                    to = k.at(0, 0, d)
-                    away = al(self.keep2[c] + to[2] * self.zs)
-                    self.send(g.at[pl.ds(away, self.zs)], self.rz.at[c, d - 1], to)
-        elif stage == 4:
-            for c in colors:
-                add_into(g, self.mine[c], [self.rz.at[c, d] for d in range(s.nz - 1)], self.zs)
-                here = pl.ds(self.mine[c], self.zs)
-                for d in range(1, s.nz):
-                    self.send(g.at[here], h.at[here], k.at(0, 0, d))
-                own = pltpu.make_async_copy(g.at[here], h.at[here], self.own_sems.at[c])
-                own.start()
-                self.locals.append(own)
-        elif stage == 5:
-            for own in self.locals:
-                own.wait()
-            for c in colors:
-                here = pl.ds(self.keep2[c], self.quarter)
-                self.send(h.at[here], h.at[here], k.flip(self.bits(c)[1]))
-        elif stage == 6:
-            for c in colors:
-                here = pl.ds(self.keep1[c], self.half)
-                self.send(h.at[here], h.at[here], k.flip(self.bits(c)[0]))
-        elif stage == 7:
-            here = pl.ds(self.base[0], self.b0)
-            for d in range(1, s.nl):
-                self.send(h.at[here], h.at[here], k.at(0, d, 0))
+        depth = len(route)
+        if 0 < stage <= depth:
+            buf = self.bufs[stage - 1]
+            add_into(g, al(self.base[stage]), [buf.at[n] for n in range(buf.shape[0])], self.part[stage - 1])
+        if stage < depth:
+            size = self.part[stage]
+            for device, place, slot in self.others(route[stage]):
+                there = pl.ds(al(self.base[stage] + place * size), size)
+                self.send(g.at[there], self.bufs[stage].at[slot], device)
+        elif stage < 2 * depth:
+            level = 2 * depth - 1 - stage
+            here = pl.ds(al(self.base[level + 1]), self.part[level])
+            if stage == depth:
+                self.own = pltpu.make_async_copy(g.at[here], h.at[here], self.own_sem)
+                self.own.start()
+            if stage == depth + 1:
+                self.own.wait()
+            source = g if stage == depth else h
+            for device, _, _ in self.others(route[level]):
+                self.send(source.at[here], h.at[here], device)
         else:
             for m in self.sent:
                 m.wait_send()
 
-    stages = 9
+    def finished(self):
+        return self.stage > self.last_stage
 
 
 def misc_slots():
@@ -310,11 +299,12 @@
     V = pltpu.VMEM
     shapes = {
         "xin": V((160, s.full_rows, big), f32),
-        "xj": V((160, wide), bf16),
-        "eb": V((2, 160, LANES), bf16),
-        "eslot": V((6, 160, LANES), bf16),
-        "em": V((2, s.nb * LANES, 5 * big + LANES), bf16),
-        "dm": V((2, s.nb * LANES, 6 * big + LANES), bf16),
+        "xj": V((160, 8 * big), bf16),
+        "eb": V((2, 8, 160), f32),
+        "eslot": V((6, 8, 160), f32),
+        "xe": V((48, 160), bf16),
+        "em": V((2, s.nb * LANES, 5 * big + 48), bf16),
+        "dm": V((2, s.nb * LANES, 6 * big + 48), bf16),
         "tm": V((s.nb * px, 6 * LANES + 48), bf16),
         "ew": V((s.nb, s.cj, c), bf16),
         "pw": V((s.nb, c, c), bf16),
@@ -349,39 +339,41 @@
         "rup": V((px, c), f32),
         "rdn": V((px, c), f32),
         "reg": V((6, 8, c), f32),
-        "ng": V((px, c), f32),
         "zg": V((px, c), bf16),
         "sgx": V((160, wide), f32),
-        "sgb": V((160, 4 * big + LANES), bf16),
+        "sgb": V((160, 4 * big), bf16),
         "sgu": V((160, 2 * big), bf16),
         "sgd": V((160, 2 * big), bf16),
-        "sge": V((6, 160, LANES), bf16),
+        "sgn": V((6, 8, 160), f32),
+        "sge": V((6, 8, 160), f32),
+        "sgt": V((LANES, 160), f32),
         "orow": V((s.cin, s.full_rows, big), f32),
         "st7": V((s.ne, 80, 4 * big), bf16),
         "dates": V((s.ne, 8, LANES), f32),
         "cbt": V((8, LANES), f32),
         "slat": V((4, s.nl, 2, c), f32),
         "slon": V((4, s.nz, 2, c), f32),
+        "sall": V((4, s.group if s.group <= 16 else 1, 2, c), f32),
+        "tmt": V((6 * LANES + 48, s.nb * px), bf16),
         "g1": V((s.rows[0], LANES), bf16),
         "g2": V((s.rows[1], LANES), bf16),
         "g3": V((s.rows[2], LANES), bf16),
         "gm": V((s.rows[3], LANES), f32),
     }
-    for i in range(4):
-        kinds = AllReduce.shapes(s, s.rows[i], s.colors[i], f32 if i == 3 else bf16)
+    for name, (buffer, _, rows, route) in s.chunks.items():
+        kinds = AllReduce.shapes(s, rows, route, f32 if buffer == 3 else bf16)
         for j, kind in enumerate(kinds):
-            shapes[f"ar{i}_{j}"] = kind
+            shapes[f"ar{name}_{j}"] = kind
     shapes["wsem"] = pltpu.SemaphoreType.DMA((5,))
-    shapes["osem"] = pltpu.SemaphoreType.DMA((4, 2))
+    shapes["osem"] = pltpu.SemaphoreType.DMA((len(s.chunks),))
     return shapes
 
 
 def sem_count(s):
-    per = lambda nc: 2 * (2 * (s.nl - 1) + 4 * nc + 2 * nc * (s.nz - 1))
-    total = sum(per(nc) for nc in s.colors)
-    total += 2 * (8 + 8 + 8 + 8) + 2 * 2 * (s.ne - 1)
-    total += 4 * 2 * (s.nl - 1 + s.nz - 1)
-    return total + 8
+    total = len(s.chunks) * 2 * 2 * (s.nl - 1 + 1 + 1 + s.nz - 1)
+    total += 2 * 4 * 8 + 2 * 2 * (s.ne - 1)
+    total += 4 * 2 * (s.group - 1 if s.group <= 16 else s.nl - 1 + s.nz - 1)
+    return total
 
 
 def main_kernel(s, names, *refs):
@@ -400,6 +392,17 @@
     row0 = l * s.hr
     edge0 = 8 * big
 
+    offsets = {(d, 0, 0) for d in range(1, s.ne)}
+    if s.group <= 16:
+        offsets |= {(0, a, b) for a in range(s.nl) for b in range(s.nz)} - {(0, 0, 0)}
+    else:
+        offsets |= {(0, d, 0) for d in range(1, s.nl)} | {(0, 0, d) for d in range(1, s.nz)}
+    offsets |= {(0, a % s.nl, b % s.nz) for a in (1, -1) for b in (1, -1)}
+    offsets = sorted(offsets)
+    barrier = pltpu.get_barrier_semaphore()
+    for o in offsets:
+        pl.semaphore_signal(barrier, 1, device_id=k.at(*o), device_id_type=MESH)
+
     loads = {}
     for n, (name, src) in enumerate(
         (("ew", ew_h), ("pw", pw_h), ("uw", uw_h), ("dw", dw_h), ("cw", cw_h))
@@ -418,19 +421,17 @@
     xin[80 : 80 + cin] = cot[0].astype(f32) * live
     xin[80 + cin : 160] = jnp.zeros((160 - 80 - cin, s.full_rows, big), f32)
     lane = lax.broadcasted_iota(i32, (160, LANES), 1)
-    left = jnp.zeros((160, LANES), f32)
-    right = jnp.zeros((160, LANES), f32)
+    ends = jnp.zeros((160, LANES), f32)
     for q in range(4):
         row = xin[:, q, :]
         xj[:, (2 + q) * big : (3 + q) * big] = row.astype(bf16)
-        rows_there = [q + 2] + ([q + 6] if q < 2 else [q - 2])
-        for r in rows_there:
-            moved = pltpu.roll(row[:, 0:LANES], (r * 4 + 2) % LANES, 1)
-            left = jnp.where((lane >> 1) == (r * 2 + 1), moved, left)
-            moved = pltpu.roll(row[:, big - LANES : big], (r * 4 + 2) % LANES, 1)
-            right = jnp.where((lane >> 1) == (r * 2), moved, right)
-    S["eb"][0] = left.astype(bf16)
-    S["eb"][1] = right.astype(bf16)
+        moved = pltpu.roll(row[:, 0:LANES], q * 2, 1)
+        ends = jnp.where((lane >> 1) == q, moved, ends)
+        moved = pltpu.roll(row[:, big - LANES : big], q * 2 + 10, 1)
+        ends = jnp.where((lane >> 1) == q + 4, moved, ends)
+    turned = ends.T
+    S["eb"][0] = turned[0:8, :]
+    S["eb"][1] = turned[8:16, :]
     S["dates"][k.e] = jnp.full((8, LANES), date.astype(f32), f32)
 
     @pl.when(jnp.logical_not(k.has_up()))
@@ -447,14 +448,21 @@
         for side in range(2):
             S["hx"][768 + 32 + side * 8 : 776 + 32 + side * 8] = jnp.zeros((8, c), f32)
 
-    offsets = {(d, 0, 0) for d in range(1, s.ne)}
-    offsets |= {(0, d, 0) for d in range(1, s.nl)} | {(0, 0, d) for d in range(1, s.nz)}
-    offsets |= {(0, a % s.nl, b % s.nz) for a in (1, -1) for b in (1, -1)}
-    offsets = sorted(offsets)
-    barrier = pltpu.get_barrier_semaphore()
-    for o in offsets:
-        pl.semaphore_signal(barrier, 1, device_id=k.at(*o), device_id_type=MESH)
     pl.semaphore_wait(barrier, len(offsets))
+
+    totals = (h1o, h2o, h3o, hmo)
+    reduced = {}
+    for n, (name, (buffer, lo, rows, route)) in enumerate(s.chunks.items()):
+        bufs = [S[f"ar{name}_{j}"] for j in range(len(route))]
+        partial = S[("g1", "g2", "g3", "gm")[buffer]]
+        reduced[name] = AllReduce(k, partial, totals[buffer], lo, rows, route, bufs, S["osem"].at[n])
+
+    def ar(letters):
+        for letter in letters:
+            for n in range(2):
+                it = reduced.get(letter + str(n))
+                if it is not None and not it.finished():
+                    it.step()
 
     pending = []
 
@@ -508,21 +516,22 @@
 
     def edge_lane(shape):
         at = lax.broadcasted_iota(i32, shape, 1)
-        r, side, m = at >> 2, (at >> 1) & 1, at & 1
-        return r, jnp.where(side == 0, m - 2, big + m), at
+        slot, q, m = at >> 3, (at & 7) >> 1, at & 1
+        r = q + 2 + 4 * ((slot >> 1) - 1)
+        return r, jnp.where((slot & 1) == 0, m - 2, big + m), at
 
     def build_encoder():
         em = S["em"]
         d_main = band((LANES, big), lambda j, J: J - 2 * j)
-        r, J, at = edge_lane((16, LANES))
-        j = lax.broadcasted_iota(i32, (16, LANES), 0)
+        r, J, at = edge_lane((16, 48))
+        j = lax.broadcasted_iota(i32, (16, 48), 0)
         codes = []
         for start_row in (0, LANES - 16):
             d = J - 2 * (j + start_row)
-            codes.append(jnp.where(at < 32, r * 1024 + d, -5000))
+            codes.append(r * 1024 + d)
         for i in range(2):
             reached = reach[row0 + i]
-            edges = [[jnp.zeros((16, LANES), f32) for _ in range(2)] for _ in range(nb)]
+            edges = [[jnp.zeros((16, 48), f32) for _ in range(2)] for _ in range(nb)]
             for a in range(-2, 3):
                 r_in = 2 * i + a + 2
                 ok = inside(4 * l + r_in - 2, 2 * s.lat_total)
@@ -541,20 +550,20 @@
             for kk in range(nb):
                 lo = kk * LANES
                 em[i, lo : lo + 16, 5 * big :] = edges[kk][0].astype(bf16)
-                em[i, lo + 16 : lo + LANES - 16, 5 * big :] = jnp.zeros((LANES - 32, LANES), bf16)
+                em[i, lo + 16 : lo + LANES - 16, 5 * big :] = jnp.zeros((LANES - 32, 48), bf16)
                 em[i, lo + LANES - 16 : lo + LANES, 5 * big :] = edges[kk][1].astype(bf16)
 
     def build_decoder():
         dm = S["dm"]
         d_main = band((LANES, big), lambda j, J: j - (J >> 1))
-        r, J, at = edge_lane((16, LANES))
-        j = lax.broadcasted_iota(i32, (16, LANES), 0)
+        r, J, at = edge_lane((16, 48))
+        j = lax.broadcasted_iota(i32, (16, 48), 0)
         codes = []
         for start_row in (0, LANES - 16):
             d = (j + start_row) - (J >> 1)
-            codes.append(jnp.where(at < 32, r * 1024 + d, -5000))
+            codes.append(r * 1024 + d)
         for i in range(2):
-            edges = [[jnp.zeros((16, LANES), f32) for _ in range(2)] for _ in range(nb)]
+            edges = [[jnp.zeros((16, 48), f32) for _ in range(2)] for _ in range(nb)]
             for n in range(6):
                 r_in = 2 * i + n
                 a = i + 1 - r_in // 2
@@ -577,7 +586,7 @@
             for kk in range(nb):
                 lo = kk * LANES
                 dm[i, lo : lo + 16, 6 * big :] = edges[kk][0].astype(bf16)
-                dm[i, lo + 16 : lo + LANES - 16, 6 * big :] = jnp.zeros((LANES - 32, LANES), bf16)
+                dm[i, lo + 16 : lo + LANES - 16, 6 * big :] = jnp.zeros((LANES - 32, 48), bf16)
                 dm[i, lo + LANES - 16 : lo + LANES, 6 * big :] = edges[kk][1].astype(bf16)
 
     def build_processor():
@@ -636,7 +645,18 @@
                 total_b = total_b + (a - total_a) * (a - total_a) * count
         return total_a, total_b
 
+    single = s.group <= 16
+    sall = S["sall"]
+    place = k.l * s.nz + k.z
+
     def stat_start(rd, a, b):
+        if single:
+            sall[rd, place, 0:1, :] = a
+            sall[rd, place, 1:2, :] = b
+            others = [(0, m, n) for n in range(s.nz) for m in range(s.nl) if m or n]
+            return start(
+                [Send(k, sall.at[rd, place], sall.at[rd, place], k.at(*o)) for o in others]
+            )
         slat[rd, k.l, 0:1, :] = a
         slat[rd, k.l, 1:2, :] = b
         return start(
@@ -647,6 +667,8 @@
         )
 
     def stat_middle(rd, sends, kind):
+        if single:
+            return sends
         arrive(sends)
         values = [(slat[rd, n, 0:1, :], slat[rd, n, 1:2, :]) for n in range(s.nl)]
         a, b = fold(values, kind, float(px))
@@ -661,6 +683,9 @@
 
     def stat_end(rd, sends, kind):
         arrive(sends)
+        if single:
+            values = [(sall[rd, n, 0:1, :], sall[rd, n, 1:2, :]) for n in range(s.group)]
+            return fold(values, kind, float(px))
         values = [(slon[rd, n, 0:1, :], slon[rd, n, 1:2, :]) for n in range(s.nz)]
         return fold(values, kind, float(px * s.nl))
 
@@ -674,29 +699,28 @@
         return ref[...].reshape(1, n)
 
     build_encoder()
+    build_decoder()
+    build_processor()
 
     arrive(first_halo)
-    edge = jnp.zeros((160, LANES), f32)
-    for sl in (-1, 0, 1):
-        for ss in (-1, 1):
-            there = S["eslot"][(sl + 1) * 2 + (ss + 1) // 2].astype(f32)
-            r_lo, r_hi = {-1: (0, 2), 0: (2, 6), 1: (6, 8)}[sl]
-            side = (ss + 1) // 2
-            lo = r_lo * 4
-            if sl == -1:
-                lo = jnp.where(k.has_up(), lo, 1000)
-            if sl == 1:
-                lo = jnp.where(k.has_down(), lo, 1000)
-            good = jnp.logical_and(lane >= lo, lane < r_hi * 4)
-            good = jnp.logical_and(good, ((lane >> 1) & 1) == side)
-            edge = jnp.where(good, there, edge)
-    xj[:, edge0:] = edge.astype(bf16)
+    def absent(slot):
+        return pl.when(jnp.logical_not(k.has_up() if slot < 2 else k.has_down()))
+
+    for slot in (0, 1, 4, 5):
+        @absent(slot)
+        def _():
+            S["eslot"][slot] = jnp.zeros((8, 160), f32)
+
+    xe = S["xe"]
+    for slot in range(0, 6, 2):
+        pair = jnp.concatenate([S["eslot"][slot], S["eslot"][slot + 1]], axis=0)
+        xe[slot * 8 : slot * 8 + 16, :] = pair.astype(bf16)
 
     filte, hx = S["filte"], S["hx"]
     for i in range(2):
         em = S["em"]
         got = nt(em[i, :, 0 : 5 * big], xj[0:80, 2 * i * big : (2 * i + 5) * big])
-        got = got + nt(em[i, :, 5 * big :], xj[0:80, edge0:])
+        got = got + nn(em[i, :, 5 * big :], xe[:, 0:80])
         for kk in range(nb):
             filte[kk, i * LANES : (i + 1) * LANES, :] = got[kk * LANES : (kk + 1) * LANES, 0:cj].astype(bf16)
     loads["ew"].wait()
@@ -728,18 +752,29 @@
             )
         )
     zero_halo = start(sends)
-    build_processor()
     stat_a = stat_middle(0, stat_a, "moments")
 
-    build_decoder()
     dm, pgr = S["dm"], S["pgr"]
     for i in range(2):
         got = nt(dm[i, :, 0 : 6 * big], xj[80 : 80 + 80, 2 * i * big : (2 * i + 6) * big])
-        got = got + nt(dm[i, :, 6 * big :], xj[80 : 80 + 80, edge0:])
+        got = got + nn(dm[i, :, 6 * big :], xe[:, 80:160])
         for kk in range(nb):
             pgr[kk, i * LANES : (i + 1) * LANES, :] = got[kk * LANES : (kk + 1) * LANES, 0:cin].astype(bf16)
     ones = jnp.ones((16, 4 * big), bf16)
     put_misc(gm, MISC["dec_bias"], nt(ones, xj[80:160, 2 * big : 6 * big])[0:1, 0:cin])
+
+    loads["cw"].wait()
+    two, mg = S["two"], S["mg"]
+    acc = nn(pgr[0], S["cw"][0])
+    for kk in range(1, nb):
+        acc = acc + nn(pgr[kk], S["cw"][kk])
+    two[...] = acc
+    mg[...] = acc.astype(bf16)
+    loads["dw"].wait()
+    ag, hp = S["ag"], S["hp"]
+    ag[...] = nn(mg[...], S["dw"][...])
+    S["mgt"][...] = mg[...].T
+    put_misc(gm, MISC["down_bias"], jnp.sum(mg[...].astype(f32), axis=0, keepdims=True))
 
     mean1, m2 = stat_end(0, stat_a, "moments")
     var1 = m2 * (1.0 / s.pixels)
@@ -768,19 +803,9 @@
         acc = acc + nt(filt[here, :], S["pw"][kk])
     h1[...] = acc
     stat_b = stat_start(1, *moments(h1[...]))
-    loads["cw"].wait()
-    two, mg = S["two"], S["mg"]
-    acc = nn(pgr[0], S["cw"][0])
-    for kk in range(1, nb):
-        acc = acc + nn(pgr[kk], S["cw"][kk])
-    two[...] = acc
-    mg[...] = acc.astype(bf16)
     stat_b = stat_middle(1, stat_b, "moments")
-    loads["dw"].wait()
-    ag, hp = S["ag"], S["hp"]
-    ag[...] = nn(mg[...], S["dw"][...])
-    S["mgt"][...] = mg[...].T
-    put_misc(gm, MISC["down_bias"], jnp.sum(mg[...].astype(f32), axis=0, keepdims=True))
+    tm_t = S["tmt"]
+    tm_t[...] = tm[...].T
     mean2, m2 = stat_end(1, stat_b, "moments")
     var2 = m2 * (1.0 / s.pixels)
     rstd2 = lax.rsqrt(var2 + EPS)
@@ -832,19 +857,19 @@
             at = off + (lo // LANES + n) * pitch
             g[at : at + height, :] = value[:, n * LANES : (n + 1) * LANES].astype(bf16)
 
+    for lo in range(0, s.f10 * LANES, 256):
+        spread(g1, 0, c, s.r641, nn(S["mgt"][...], act[:, lo : lo + 256]), lo, 256)
+    ar("A")
+    stat_c = stat_middle(2, stat_c, "sums")
     S["n2t"][...] = n2[...].T
     for lo in range(0, s.f10 * LANES, 256):
-        spread(g1, 0, c, s.r641, nn(S["n2t"][...], hg[:, lo : lo + 256]), lo, 256)
-    stat_c = stat_middle(2, stat_c, "sums")
-    for lo in range(0, s.f10 * LANES, 256):
-        spread(g1, s.off_down, c, s.r641, nn(S["mgt"][...], act[:, lo : lo + 256]), lo, 256)
+        spread(g1, s.off_up, c, s.r641, nn(S["n2t"][...], hg[:, lo : lo + 256]), lo, 256)
     h2 = S["h2"]
     h2[...] = (h1[...] + nt(act[...], S["dw"][...]) + vec(db)).astype(bf16)
     for kk in range(nb):
         got = tn(pgr[kk], h2[:, 0 : s.c5 * LANES])
         spread(g1, s.off_dec + kk * s.c5 * s.r80, cin, s.r80, got, 0, s.c5 * LANES)
-    ar1 = AllReduce(k, g1, h1o, s.rows[0], s.colors[0], [S[f"ar0_{j}"] for j in range(4)], S["osem"].at[0])
-    ar1.step()
+    ar("BA")
 
     def weighted(ref, column):
         return jnp.sum(ref.astype(f32) * column.astype(f32), axis=0, keepdims=True)
@@ -853,14 +878,14 @@
         put_misc(gm, MISC[name], row[:, 0:768])
         put_misc(gm, MISC[name] + 1, row[:, 768:])
 
-    put_long("up_bias", jnp.sum(hg[...].astype(f32), axis=0, keepdims=True))
-    for n in range(2):
-        at = s.f10 * LANES + n
-        put_misc(gm, MISC["up_last"] + n, weighted(n2[...], hg[:, at : at + 1]))
-        put_misc(gm, MISC["down_last"] + n, weighted(mg[...], act[:, at : at + 1]))
-    for kk in range(nb):
-        put_misc(gm, MISC["dec_last"] + kk, weighted(pgr[kk], h2[:, c - 1 : c]))
-    ar1.step()
+    def misc_one():
+        put_long("up_bias", jnp.sum(hg[...].astype(f32), axis=0, keepdims=True))
+        for n in range(2):
+            at = s.f10 * LANES + n
+            put_misc(gm, MISC["up_last"] + n, weighted(n2[...], hg[:, at : at + 1]))
+            put_misc(gm, MISC["down_last"] + n, weighted(mg[...], act[:, at : at + 1]))
+        for kk in range(nb):
+            put_misc(gm, MISC["dec_last"] + kk, weighted(pgr[kk], h2[:, c - 1 : c]))
 
     sum_a, sum_b = stat_end(2, stat_c, "sums")
     g_two = vec(gain2)
@@ -877,11 +902,12 @@
         return carry
 
     lax.fori_loop(0, px // 32, one_rows, 0)
+    ar("B")
     fg = S["fg"]
     for kk in range(nb):
         fg[kk * px : (kk + 1) * px, :] = nn(br[...], S["pw"][kk]).astype(bf16)
     con = S["con"]
-    con[...] = tn(tm[...], fg[...])
+    con[...] = nn(S["tmt"][...], fg[...])
 
     def sum_rows(n, carry):
         here = pl.ds(pl.multiple_of(n * 48, 16), 48)
@@ -915,20 +941,20 @@
     back_halo = start(sends)
     g2 = S["g2"]
     S["brt"][...] = br[...].T
+    ar("A")
     for kk in range(nb):
         if kk == 1:
             stat_d = stat_middle(3, stat_d, "sums")
         for lo, width in cols:
             got = nn(S["brt"][...], filt[kk * px : (kk + 1) * px, lo : lo + width])
             spread(g2, kk * s.c5 * s.r641, c, s.r641, got, lo, width)
-    ar2 = AllReduce(k, g2, h2o, s.rows[1], s.colors[1], [S[f"ar1_{j}"] for j in range(4)], S["osem"].at[1])
-    ar2.step()
-    put_misc(gm, MISC["proc_bias"], jnp.sum(br[...].astype(f32), axis=0, keepdims=True))
-    for kk in range(nb):
-        put_misc(gm, MISC["proc_last"] + kk, weighted(br[...], filt[kk * px : (kk + 1) * px, c - 1 : c]))
+        if kk == 1:
+            ar("C")
+    ar("D")
+    ar("BA")
 
     arrive(back_halo)
-    ng = S["ng"]
+    ng = ntg
     ng[...] = con[own, :]
 
     @pl.when(k.has_up())
@@ -972,12 +998,12 @@
         spread(g3, kk * s.c5 * s.r80, cj, s.r80, got, 0, s.c5 * LANES)
         put_misc(gm, MISC["enc_last"] + kk, weighted(filte[kk], zg[:, c - 1 : c]))
     put_misc(gm, MISC["enc_bias"], jnp.sum(zg[...].astype(f32), axis=0, keepdims=True))
-    ar3 = AllReduce(k, g3, h3o, s.rows[2], s.colors[2], [S[f"ar2_{j}"] for j in range(4)], S["osem"].at[2])
-    ar4 = AllReduce(k, gm, hmo, s.rows[3], s.colors[3], [S[f"ar3_{j}"] for j in range(4)], S["osem"].at[3])
-    ar3.step()
-    ar4.step()
-    ar1.step()
-    ar2.step()
+    ar("E")
+    misc_one()
+    put_misc(gm, MISC["proc_bias"], jnp.sum(br[...].astype(f32), axis=0, keepdims=True))
+    for kk in range(nb):
+        put_misc(gm, MISC["proc_last"] + kk, weighted(br[...], filt[kk * px : (kk + 1) * px, c - 1 : c]))
+    ar("MCDBA")
 
     projt, partt = S["projt"], S["partt"]
     for kk in range(nb):
@@ -995,28 +1021,36 @@
         lo = 2 * i * big
         got = nn(projt[i], dm[i])
         sgx[0:80, lo : lo + 6 * big] = sgx[0:80, lo : lo + 6 * big] + got[:, 0 : 6 * big]
-        sgx[0:80, edge0:] = sgx[0:80, edge0:] + got[:, 6 * big :]
+        sgx[0:80, edge0 : edge0 + 48] = sgx[0:80, edge0 : edge0 + 48] + got[:, 6 * big :]
         got = nn(partt[i], em[i])
         sgx[80:160, lo : lo + 5 * big] = sgx[80:160, lo : lo + 5 * big] + got[:, 0 : 5 * big]
-        sgx[80:160, edge0:] = sgx[80:160, edge0:] + got[:, 5 * big :]
+        sgx[80:160, edge0 : edge0 + 48] = sgx[80:160, edge0 : edge0 + 48] + got[:, 5 * big :]
     sgb, sgu, sgd, sge = S["sgb"], S["sgu"], S["sgd"], S["sge"]
     sgb[:, 0 : 2 * big] = sgx[:, 0 : 2 * big].astype(bf16)
     sgb[:, 2 * big : 4 * big] = sgx[:, 6 * big : 8 * big].astype(bf16)
-    sgb[:, 4 * big :] = sgx[:, edge0:].astype(bf16)
+    turned = sgx[:, edge0:].T
+    for n in range(6):
+        S["sgn"][n] = turned[n * 8 : n * 8 + 8, :]
     sends = [
         Send(k, sgb.at[:, pl.ds(0, 2 * big)], sgd, k.at(0, -1, 0), -1),
         Send(k, sgb.at[:, pl.ds(2 * big, 2 * big)], sgu, k.at(0, 1, 0), 1),
     ]
     for dl, ds in dirs:
         sends.append(
-            Send(k, sgb.at[:, pl.ds(4 * big, LANES)], sge.at[slot_of(dl, ds)], k.at(0, dl, ds), dl)
+            Send(k, S["sgn"].at[(dl + 1) * 2 + (ds + 1) // 2], sge.at[slot_of(dl, ds)], k.at(0, dl, ds), dl)
         )
     out_halo = start(sends)
-    ar3.step()
-    ar4.step()
-    ar1.step()
-    ar2.step()
+    ar("CDEABM")
     arrive(out_halo)
+    sgt = S["sgt"]
+    sgt[48:LANES, :] = jnp.zeros((LANES - 48, 160), f32)
+    for slot in range(6):
+        sgt[slot * 8 : slot * 8 + 8, :] = sge[slot]
+    for slot in (0, 1, 4, 5):
+        @absent(slot)
+        def _():
+            sgt[slot * 8 : slot * 8 + 8, :] = jnp.zeros((8, 160), f32)
+    arrived = sgt[...].T
     up_one = jnp.where(k.has_up(), 1, 0)
     down_one = jnp.where(k.has_down(), 1, 0)
     cbt = S["cbt"]
@@ -1035,19 +1069,15 @@
             other = sgd[:, (q - 2) * big : (q - 1) * big].astype(f32)
             value = value + jnp.where(down_one == 1, other, 0.0)
         head, tail = value[:, 0:LANES], value[:, big - LANES :]
-        sources = [(0, q + 2, None)]
-        sources += [(-1, q + 6, up_one)] if q < 2 else [(1, q - 2, down_one)]
-        for sl, r, there in sources:
-            for ss in (-1, 1):
-                got = sge[(sl + 1) * 2 + (ss + 1) // 2].astype(f32)
-                if ss == -1:
-                    moved = pltpu.roll(got, (LANES - (r * 4 + 2)) % LANES, 1)
-                    bound = 2 if there is None else there * 2
-                    head = head + jnp.where(lane < bound, moved, 0.0)
+        for sl in (-1, 0, 1):
+            for side in range(2):
+                at = ((sl + 1) * 2 + side) * 8 + q * 2
+                if side == 0:
+                    moved = pltpu.roll(arrived, (LANES - at) % LANES, 1)
+                    head = head + jnp.where(lane < 2, moved, 0.0)
                 else:
-                    moved = pltpu.roll(got, (2 * LANES - 2 - r * 4) % LANES, 1)
-                    bound = LANES - 2 if there is None else LANES - there * 2
-                    tail = tail + jnp.where(lane >= bound, moved, 0.0)
+                    moved = pltpu.roll(arrived, LANES - 2 - at, 1)
+                    tail = tail + jnp.where(lane >= LANES - 2, moved, 0.0)
         orow[:, q, 0:LANES] = (head[0:cin] + bias_col) * live
         orow[:, q, LANES:big] = (tail[0:cin] + bias_col) * live
         st7[k.e, :, q * big : q * big + LANES] = head[80:160].astype(bf16)
@@ -1056,11 +1086,8 @@
     state_sends = start(
         [Send(k, st7.at[k.e], st7.at[k.e], k.at(d, 0, 0)) for d in range(1, s.ne)]
     )
-    for _ in range(2):
-        ar3.step()
-        ar4.step()
-        ar1.step()
-        ar2.step()
+    ar("ACBDEM")
+    ar("ABCDEM")
     arrive(date_sends)
     arrive(state_sends)
     for d in range(s.dates):
@@ -1073,11 +1100,8 @@
             orow[:, q, :] = value[0:cin]
         sgrad[d] = orow[...].astype(bf16)
 
-    rest = [ar1, ar2, ar3, ar4]
-    while any(a.stage < AllReduce.stages for a in rest):
-        for a in rest:
-            if a.stage < AllReduce.stages:
-                a.step()
+    while not all(it.finished() for it in reduced.values()):
+        ar("ABCDEM")
     for m in pending:
         m.wait_send()
 
@@ -1094,7 +1118,7 @@
     used1 = s.off_dec + nb * s.c5 * s.r80
     third = s.c5 * s.r641
     pieces = [(h2, b2, n * third, third) for n in range(nb)]
-    pieces += [(h1, b1, 0, s.off_down), (h1, b1, s.off_down, s.off_dec - s.off_down)]
+    pieces += [(h1, b1, 0, s.off_up), (h1, b1, s.off_up, s.off_dec - s.off_up)]
     pieces += [(h1, b1, s.off_dec, used1 - s.off_dec), (h3, b3, 0, nb * s.c5 * s.r80)]
     loads = [
         pltpu.make_async_copy(a.at[pl.ds(at, n)], b.at[pl.ds(at, n)], sem_in.at[i])
@@ -1109,9 +1133,7 @@
         copy.start()
         stores.append(copy)
 
-    store(output_in, output)
-    store(state_in, state_grad)
-    for a, b in ((m1, m1o), (v1, v1o), (m2, m2o), (v2, v2o)):
+    for a, b in ((output_in, output), (state_in, state_grad), (m1, m1o), (v1, v1o), (m2, m2o), (v2, v2o)):
         b[...] = a[...]
     turned = hm[0:144, :].T
 
@@ -1133,7 +1155,7 @@
         widen(ref, b2, kk * third, s.r641, c, s.c5)
         store(ref, proc_w.at[kk])
     for n, (ref, name, base, to) in enumerate(
-        ((up_v, "up_last", 0, up_w), (down_v, "down_last", s.off_down, down_w))
+        ((down_v, "down_last", 0, down_w), (up_v, "up_last", s.off_up, up_w))
     ):
         for part in range(2):
             last_column(ref, MISC[name] + part, c, s.f10 * LANES + part)
@@ -1217,12 +1239,12 @@
         sd((c, ff), f32), sd((ff,), f32), sd((c, ff), f32), sd((c,), f32),
         sd((nb, s.cin, c), f32), sd((s.cin,), f32),
     ] + [sd((1, c), f32)] * 4
-    large = (0, 1, 2, 6, 10, 12, 14)
+    large = (2, 6, 10, 12, 14)
     V = pltpu.VMEM
     done = pl.pallas_call(
         functools.partial(finish_kernel, s),
         out_shape=outs,
-        in_specs=[hbm] * 3 + [vm] + [hbm] * 2 + [vm] * 4,
+        in_specs=[hbm] * 3 + [vm] * 7,
         out_specs=[hbm if n in large else vm for n in range(len(outs))],
         scratch_shapes=[
             V((s.rows[0], LANES), bf16), V((s.rows[1], LANES), bf16), V((s.rows[2], LANES), bf16),

time: 137 us -> 119 us (0.87)
  Pallas kernels: 135 us -> 118 us
    pallas_call x1, Pallas kernels: 118 us -> 109 us  [per_device(): pl.pallas_call(functools.partial(main_kernel, s, names), out_shape=out_sh...]
    pallas_call x1, Pallas kernels: 16.3 us -> 8.83 us  [per_device(): pl.pallas_call(functools.partial(finish_kernel, s), out_shape=outs, in_sp...]
where the time goes in v3:
time: 119 us
  Pallas kernels  118 us (99%)
  between operations  1.5 us (1%)
    pallas_call x1, Pallas kernels, per_device(): pl.pallas_call(functools.partial(main_kernel, s, names), out_shape=out_sh...  109 us
    pallas_call x1, Pallas kernels, per_device(): pl.pallas_call(functools.partial(finish_kernel, s), out_shape=outs, in_sp...  8.83 us

profile of v3, /device:TPU:0, one launch (start us, length us, event | category | flops | bytes accessed | tf_op | source)
XLA Modules:
  0.0 119.2 jit_solution(9918570927828409687)
XLA Ops:
  1.3 108.9 %forecast.1 = (bf16[14336,128]{1,0:T(8,128)(2,1)}, bf16[10240,128]{1,0:T(8,128)(2,1)}, bf16[1536,128]{1,0:T(8,128)(2,1)}, f32[256,128]{1,0:T(8,128)}, bf16[1,72,...) custom-call(bf16[2,72,4,256]{3,2,1,0:T(4,128)(2,1)} %refs_0_.1, ...), custom_call_target="tpu_custom_call" | custom-call | tf_op jit(solution)/shard_map/forecast/pallas_call | solution.py:1224
  110.2 8.8 %finish.1 = (bf16[1,72,4,256]{3,2,1,0:T(4,128)(2,1)}, bf16[2,72,4,256]{3,2,1,0:T(4,128)(2,1)}, f32[3,80,641]{2,1,0:T(8,128)}, f32[641]{0:T(1024)}, f32[641]{0:T(...) custom-call(bf16[14336,128]{1,0:T(8,128)(2,1)} %get-tuple-element.50, ...), custom_call_target="tpu_custom_call" | custom-call | tf_op jit(solution)/shard_map/finish/pallas_call | solution.py:1244

commit v4 on v3

--- a/solution.py
+++ b/solution.py
@@ -1,4 +1,5 @@
 import functools
+import types
 
 import jax
 import jax.numpy as jnp
@@ -14,8 +15,16 @@
 EPS = 1e-05
 LANES = 128
 AXES = ("ens", "lat", "lon")
-ROUTE_X = ("lat", "bit0", "bit1", "lon")
-ROUTE_Y = ("lat", "bit1", "bit0", "lon")
+BIT0, BIT1, LAT, LON = range(4)
+ROUTE_X = (LAT, BIT0, BIT1, LON)
+ROUTE_Y = (LAT, BIT1, BIT0, LON)
+WSEM, OSEM, SEMS = range(3)
+ROUTE_ZX = (LAT, LON, BIT0, BIT1)
+ROUTE_ZY = (LAT, LON, BIT1, BIT0)
+PIECES = dict(
+    a=(0, 0), b=(0, 1), c=(0, 2), d=(1, 0), e=(1, 1), f=(1, 2),
+    g=(2, 0), h=(2, 1), i=(3, 0), j=(3, 1), k=(4, 0), l=(5, 0),
+)
 
 
 def nn(a, b):
@@ -65,20 +74,26 @@
         self.rows = tuple(up_to(n, unit) for n in used) + (up_to(24 * 6, unit // 2),)
         self.chunks = {}
 
-        def split(name, buffer, lo, hi):
-            first = lo + up_to((hi - lo) // 2, unit)
-            for n, (a, b, route) in enumerate(((lo, first, ROUTE_X), (first, hi, ROUTE_Y))):
-                if b > a:
-                    self.chunks[name + str(n)] = (buffer, a, b - a, route)
+        def split(piece, buffer, lo, hi, third=None):
+            units = (hi - lo) // unit
+            last = 2 if third and units >= 6 else 0
+            first = (units - last + 1) // 2
+            at = lo
+            for n, (count, route) in enumerate(
+                ((first, ROUTE_X), (units - last - first, ROUTE_Y), (last, third))
+            ):
+                if count:
+                    self.chunks[piece, n] = (buffer, at, count * unit, route)
+                at += count * unit
 
         cut = self.off_up // unit * unit
-        split("A", 0, 0, cut)
-        split("B", 0, cut, self.rows[0])
+        split(0, 0, 0, cut, ROUTE_ZX)
+        split(1, 0, cut, self.rows[0], ROUTE_ZY)
         cut = 2 * self.c5 * self.r641 // unit * unit
-        split("C", 1, 0, cut)
-        split("D", 1, cut, self.rows[1])
-        self.chunks["E0"] = (2, 0, self.rows[2], ROUTE_X)
-        self.chunks["M0"] = (3, 0, self.rows[3], ROUTE_Y)
+        split(2, 1, 0, cut)
+        split(3, 1, cut, self.rows[1])
+        self.chunks[4, 0] = (2, 0, self.rows[2], ROUTE_X)
+        self.chunks[5, 0] = (3, 0, self.rows[3], ROUTE_Y)
         self.group = self.nl * self.nz
 
 
@@ -183,7 +198,7 @@
 
     @staticmethod
     def count(s, axis):
-        return {"lat": s.nl, "lon": s.nz}.get(axis, 2)
+        return {LAT: s.nl, LON: s.nz}.get(axis, 2)
 
     @staticmethod
     def shapes(s, rows, route, dtype):
@@ -196,18 +211,17 @@
 
     def index(self, axis):
         k = self.k
-        return {"lat": k.l, "lon": k.z}[axis] if axis in ("lat", "lon") else k.bit(int(axis[3:]))
+        return {LAT: k.l, LON: k.z}[axis] if axis in (LAT, LON) else k.bit(axis)
 
     def others(self, axis):
         k, s = self.k, self.k.s
-        if axis == "lat":
+        if axis == LAT:
             devices = [k.at(0, d, 0) for d in range(1, s.nl)]
             return [(dev, dev[1], n) for n, dev in enumerate(devices)]
-        if axis == "lon":
+        if axis == LON:
             devices = [k.at(0, 0, d) for d in range(1, s.nz)]
             return [(dev, dev[2], n) for n, dev in enumerate(devices)]
-        which = int(axis[3:])
-        return [(k.flip(which), 1 - k.bit(which), 0)]
+        return [(k.flip(axis), 1 - k.bit(axis), 0)]
 
     def send(self, src, dst, device):
         m = Send(self.k, src, dst, device)
@@ -250,31 +264,9 @@
         return self.stage > self.last_stage
 
 
-def misc_slots():
-    names = [
-        ("down_bias", 1),
-        ("up_bias", 2),
-        ("gain_two", 1),
-        ("shift_two", 1),
-        ("proc_bias", 1),
-        ("gain_one", 1),
-        ("shift_one", 1),
-        ("enc_bias", 1),
-        ("up_last", 2),
-        ("down_last", 2),
-        ("proc_last", 3),
-        ("enc_last", 3),
-        ("dec_last", 3),
-        ("dec_bias", 1),
-    ]
-    table, at = {}, 0
-    for name, count in names:
-        table[name] = at
-        at += count
-    return table
-
-
-MISC = misc_slots()
+class MISC:
+    down_bias, up_bias, gain_two, shift_two, proc_bias, gain_one, shift_one, enc_bias = 0, 1, 3, 4, 5, 6, 7, 8
+    up_last, down_last, proc_last, enc_last, dec_last, dec_bias = 9, 11, 13, 16, 19, 22
 
 
 def put_misc(misc, slot, row):
@@ -297,75 +289,76 @@
     big = s.full_cols
     wide = 8 * big + LANES
     V = pltpu.VMEM
-    shapes = {
-        "xin": V((160, s.full_rows, big), f32),
-        "xj": V((160, 8 * big), bf16),
-        "eb": V((2, 8, 160), f32),
-        "eslot": V((6, 8, 160), f32),
-        "xe": V((48, 160), bf16),
-        "em": V((2, s.nb * LANES, 5 * big + 48), bf16),
-        "dm": V((2, s.nb * LANES, 6 * big + 48), bf16),
-        "tm": V((s.nb * px, 6 * LANES + 48), bf16),
-        "ew": V((s.nb, s.cj, c), bf16),
-        "pw": V((s.nb, c, c), bf16),
-        "uw": V((c, ff), bf16),
-        "dw": V((c, ff), bf16),
-        "cw": V((s.nb, s.cin, c), bf16),
-        "filte": V((s.nb, px, s.cj), bf16),
-        "hx": V((6 * LANES + 48, c), f32),
-        "nx": V((6 * LANES + 48, c), bf16),
-        "pe": V((2, 8, c), f32),
-        "filt": V((s.nb * px, c), bf16),
-        "h1": V((px, c), f32),
-        "n2": V((px, c), bf16),
-        "hp": V((px, ff), f32),
-        "ag": V((px, ff), f32),
-        "act": V((px, ff), bf16),
-        "hg": V((px, ff), bf16),
-        "n2t": V((c, px), bf16),
-        "h2": V((px, c), bf16),
-        "pgr": V((s.nb, px, s.cin), bf16),
-        "projt": V((2, 80, s.nb * LANES), bf16),
-        "partt": V((2, 80, s.nb * LANES), bf16),
-        "two": V((px, c), f32),
-        "mg": V((px, c), bf16),
-        "mgt": V((c, px), bf16),
-        "ntg": V((px, c), f32),
-        "one": V((px, c), f32),
-        "br": V((px, c), bf16),
-        "brt": V((c, px), bf16),
-        "fg": V((s.nb * px, c), bf16),
-        "con": V((6 * LANES + 48, c), f32),
-        "rup": V((px, c), f32),
-        "rdn": V((px, c), f32),
-        "reg": V((6, 8, c), f32),
-        "zg": V((px, c), bf16),
-        "sgx": V((160, wide), f32),
-        "sgb": V((160, 4 * big), bf16),
-        "sgu": V((160, 2 * big), bf16),
-        "sgd": V((160, 2 * big), bf16),
-        "sgn": V((6, 8, 160), f32),
-        "sge": V((6, 8, 160), f32),
-        "sgt": V((LANES, 160), f32),
-        "orow": V((s.cin, s.full_rows, big), f32),
-        "st7": V((s.ne, 80, 4 * big), bf16),
-        "dates": V((s.ne, 8, LANES), f32),
-        "cbt": V((8, LANES), f32),
-        "slat": V((4, s.nl, 2, c), f32),
-        "slon": V((4, s.nz, 2, c), f32),
-        "sall": V((4, s.group if s.group <= 16 else 1, 2, c), f32),
-        "tmt": V((6 * LANES + 48, s.nb * px), bf16),
-        "g1": V((s.rows[0], LANES), bf16),
-        "g2": V((s.rows[1], LANES), bf16),
-        "g3": V((s.rows[2], LANES), bf16),
-        "gm": V((s.rows[3], LANES), f32),
-    }
+    shapes = dict(
+        xin=V((160, s.full_rows, big), f32),
+        xj=V((160, 8 * big), bf16),
+        eb=V((2, 8, 160), f32),
+        eslot=V((6, 8, 160), f32),
+        xe=V((48, 160), bf16),
+        em=V((2, s.nb * LANES, 5 * big + 48), bf16),
+        dm=V((2, s.nb * LANES, 6 * big + 48), bf16),
+        tm=V((s.nb * px, 6 * LANES + 48), bf16),
+        ew=V((s.nb, s.cj, c), bf16),
+        pw=V((s.nb, c, c), bf16),
+        uw=V((c, ff), bf16),
+        dw=V((c, ff), bf16),
+        cw=V((s.nb, s.cin, c), bf16),
+        filte=V((s.nb, px, s.cj), bf16),
+        hx=V((6 * LANES + 48, c), f32),
+        nx=V((6 * LANES + 48, c), bf16),
+        pe=V((2, 8, c), f32),
+        filt=V((s.nb * px, c), bf16),
+        h1=V((px, c), f32),
+        n2=V((px, c), bf16),
+        hp=V((px, ff), f32),
+        ag=V((px, ff), f32),
+        act=V((px, ff), bf16),
+        hg=V((px, ff), bf16),
+        n2t=V((c, px), bf16),
+        h2=V((px, c), bf16),
+        pgr=V((s.nb, px, s.cin), bf16),
+        projt=V((2, 80, s.nb * LANES), bf16),
+        partt=V((2, 80, s.nb * LANES), bf16),
+        two=V((px, c), f32),
+        mg=V((px, c), bf16),
+        mgt=V((c, px), bf16),
+        ntg=V((px, c), f32),
+        one=V((px, c), f32),
+        br=V((px, c), bf16),
+        brt=V((c, px), bf16),
+        fg=V((s.nb * px, c), bf16),
+        con=V((6 * LANES + 48, c), f32),
+        rup=V((px, c), f32),
+        rdn=V((px, c), f32),
+        reg=V((6, 8, c), f32),
+        zg=V((px, c), bf16),
+        sgx=V((160, wide), f32),
+        sgb=V((160, 4 * big), bf16),
+        sgu=V((160, 2 * big), bf16),
+        sgd=V((160, 2 * big), bf16),
+        sgn=V((6, 8, 160), f32),
+        sge=V((6, 8, 160), f32),
+        sgt=V((LANES, 160), f32),
+        orow=V((s.cin, s.full_rows, big), f32),
+        st7=V((s.ne, 80, 4 * big), bf16),
+        dates=V((s.ne, 8, LANES), f32),
+        cbt=V((8, LANES), f32),
+        slat=V((4, s.nl, 2, c), f32),
+        slon=V((4, s.nz, 2, c), f32),
+        sall=V((4, s.group if s.group <= 16 else 1, 2, c), f32),
+        tmt=V((6 * LANES + 48, s.nb * px), bf16),
+        g1=V((s.rows[0], LANES), bf16),
+        g2=V((s.rows[1], LANES), bf16),
+        g3=V((s.rows[2], LANES), bf16),
+        gm=V((s.rows[3], LANES), f32),
+    )
     for name, (buffer, _, rows, route) in s.chunks.items():
         kinds = AllReduce.shapes(s, rows, route, f32 if buffer == 3 else bf16)
         for j, kind in enumerate(kinds):
-            shapes[f"ar{name}_{j}"] = kind
-    shapes["wsem"] = pltpu.SemaphoreType.DMA((5,))
-    shapes["osem"] = pltpu.SemaphoreType.DMA((len(s.chunks),))
+            shapes[name, j] = kind
+    shapes[WSEM] = pltpu.SemaphoreType.DMA((5,))
+    shapes[OSEM] = pltpu.SemaphoreType.DMA((len(s.chunks),))
+    shapes[SEMS] = pltpu.SemaphoreType.DMA((sem_count(s),))
     return shapes
 
 
@@ -383,8 +376,9 @@
         ew_h, eb, gain1, shift1, pw_h, pb, gain2, shift2, uw_h, ub, dw_h, db, cw_h, cb,
     ) = refs[:n_in]
     h1o, h2o, h3o, hmo, out, sgrad, m1o, v1o, m2o, v2o = refs[n_in : n_in + n_out]
-    S = dict(zip(names, refs[n_in + n_out :]))
-    sems = S["sems"]
+    table = dict(zip(names, refs[n_in + n_out :]))
+    S = types.SimpleNamespace(**{n: r for n, r in table.items() if isinstance(n, str)})
+    sems = table[SEMS]
     k = Links(s, sems)
     c, ff, px, nb, cin, cj = s.c, s.ff, s.px, s.nb, s.cin, s.cj
     big = s.full_cols
@@ -403,16 +397,18 @@
     for o in offsets:
         pl.semaphore_signal(barrier, 1, device_id=k.at(*o), device_id_type=MESH)
 
-    loads = {}
-    for n, (name, src) in enumerate(
-        (("ew", ew_h), ("pw", pw_h), ("uw", uw_h), ("dw", dw_h), ("cw", cw_h))
+    loads, weights = types.SimpleNamespace(), []
+    for n, (src, to) in enumerate(
+        ((ew_h, S.ew), (pw_h, S.pw), (uw_h, S.uw), (dw_h, S.dw), (cw_h, S.cw))
     ):
-        loads[name] = pltpu.make_async_copy(src, S[name], S["wsem"].at[n])
-        loads[name].start()
+        copy = pltpu.make_async_copy(src, to, table[WSEM].at[n])
+        copy.start()
+        weights.append(copy)
+    loads.ew, loads.pw, loads.uw, loads.dw, loads.cw = weights
 
     date = date_ref[0]
     live = jnp.where(date >= 0, 1.0, 0.0).astype(f32)
-    xin, xj = S["xin"], S["xj"]
+    xin, xj = S.xin, S.xj
     picked = jnp.zeros((cin, s.full_rows, big), f32)
     for d in range(s.dates):
         picked = picked + state[d].astype(f32) * jnp.where(date == d, 1.0, 0.0).astype(f32)
@@ -430,39 +426,38 @@
         moved = pltpu.roll(row[:, big - LANES : big], q * 2 + 10, 1)
         ends = jnp.where((lane >> 1) == q + 4, moved, ends)
     turned = ends.T
-    S["eb"][0] = turned[0:8, :]
-    S["eb"][1] = turned[8:16, :]
-    S["dates"][k.e] = jnp.full((8, LANES), date.astype(f32), f32)
+    S.eb[0] = turned[0:8, :]
+    S.eb[1] = turned[8:16, :]
+    S.dates[k.e] = jnp.full((8, LANES), date.astype(f32), f32)
 
     @pl.when(jnp.logical_not(k.has_up()))
     def _():
         xj[:, 0 : 2 * big] = jnp.zeros((160, 2 * big), bf16)
-        S["hx"][0:px] = jnp.zeros((px, c), f32)
+        S.hx[0:px] = jnp.zeros((px, c), f32)
         for side in range(2):
-            S["hx"][768 + side * 8 : 776 + side * 8] = jnp.zeros((8, c), f32)
+            S.hx[768 + side * 8 : 776 + side * 8] = jnp.zeros((8, c), f32)
 
     @pl.when(jnp.logical_not(k.has_down()))
     def _():
         xj[:, 6 * big : 8 * big] = jnp.zeros((160, 2 * big), bf16)
-        S["hx"][2 * px : 3 * px] = jnp.zeros((px, c), f32)
+        S.hx[2 * px : 3 * px] = jnp.zeros((px, c), f32)
         for side in range(2):
-            S["hx"][768 + 32 + side * 8 : 776 + 32 + side * 8] = jnp.zeros((8, c), f32)
+            S.hx[768 + 32 + side * 8 : 776 + 32 + side * 8] = jnp.zeros((8, c), f32)
 
     pl.semaphore_wait(barrier, len(offsets))
 
     totals = (h1o, h2o, h3o, hmo)
     reduced = {}
     for n, (name, (buffer, lo, rows, route)) in enumerate(s.chunks.items()):
-        bufs = [S[f"ar{name}_{j}"] for j in range(len(route))]
-        partial = S[("g1", "g2", "g3", "gm")[buffer]]
-        reduced[name] = AllReduce(k, partial, totals[buffer], lo, rows, route, bufs, S["osem"].at[n])
+        bufs = [table[name, j] for j in range(len(route))]
+        partial = (S.g1, S.g2, S.g3, S.gm)[buffer]
+        reduced[name] = AllReduce(k, partial, totals[buffer], lo, rows, route, bufs, table[OSEM].at[n])
 
     def ar(letters):
         for letter in letters:
-            for n in range(2):
-                it = reduced.get(letter + str(n))
-                if it is not None and not it.finished():
-                    it.step()
+            it = reduced.get(PIECES[letter])
+            if it is not None and not it.finished():
+                it.step()
 
     pending = []
 
@@ -487,17 +482,17 @@
     ]
     for dl, ds in dirs:
         sends.append(
-            Send(k, S["eb"].at[(ds + 1) // 2], S["eslot"].at[slot_of(dl, ds)], k.at(0, dl, ds), dl)
+            Send(k, S.eb.at[(ds + 1) // 2], S.eslot.at[slot_of(dl, ds)], k.at(0, dl, ds), dl)
         )
     first_halo = start(sends)
     date_sends = start(
         [
-            Send(k, S["dates"].at[k.e], S["dates"].at[k.e], k.at(d, 0, 0))
+            Send(k, S.dates.at[k.e], S.dates.at[k.e], k.at(d, 0, 0))
             for d in range(1, s.ne)
         ]
     )
 
-    gm = S["gm"]
+    gm = S.gm
     gm[0:144] = jnp.zeros((144, LANES), f32)
 
     def band(shape, column_of):
@@ -521,7 +516,7 @@
         return r, jnp.where((slot & 1) == 0, m - 2, big + m), at
 
     def build_encoder():
-        em = S["em"]
+        em = S.em
         d_main = band((LANES, big), lambda j, J: J - 2 * j)
         r, J, at = edge_lane((16, 48))
         j = lax.broadcasted_iota(i32, (16, 48), 0)
@@ -554,7 +549,7 @@
                 em[i, lo + LANES - 16 : lo + LANES, 5 * big :] = edges[kk][1].astype(bf16)
 
     def build_decoder():
-        dm = S["dm"]
+        dm = S.dm
         d_main = band((LANES, big), lambda j, J: j - (J >> 1))
         r, J, at = edge_lane((16, 48))
         j = lax.broadcasted_iota(i32, (16, 48), 0)
@@ -590,7 +585,7 @@
                 dm[i, lo + LANES - 16 : lo + LANES, 6 * big :] = edges[kk][1].astype(bf16)
 
     def build_processor():
-        tm = S["tm"]
+        tm = S.tm
         d_main = band((LANES, LANES), lambda j, J: J - j)
         at = lax.broadcasted_iota(i32, (16, 48), 1)
         slot, idx = at >> 3, at & 7
@@ -632,21 +627,21 @@
                 tm[lo + 16 : lo + LANES - 16, 768:816] = jnp.zeros((LANES - 32, 48), bf16)
                 tm[lo + LANES - 16 : lo + LANES, 768:816] = edges[kk][1].astype(bf16)
 
-    slat, slon = S["slat"], S["slon"]
+    slat, slon = S.slat, S.slon
 
     def fold(values, kind, count):
         total_a, total_b = values[0]
         for a, b in values[1:]:
             total_a = total_a + a
             total_b = total_b + b
-        if kind == "moments":
+        if kind:
             total_a = total_a * (1.0 / len(values))
             for a, b in values:
                 total_b = total_b + (a - total_a) * (a - total_a) * count
         return total_a, total_b
 
     single = s.group <= 16
-    sall = S["sall"]
+    sall = S.sall
     place = k.l * s.nz + k.z
 
     def stat_start(rd, a, b):
@@ -709,29 +704,29 @@
     for slot in (0, 1, 4, 5):
         @absent(slot)
         def _():
-            S["eslot"][slot] = jnp.zeros((8, 160), f32)
-
-    xe = S["xe"]
+            S.eslot[slot] = jnp.zeros((8, 160), f32)
+
+    xe = S.xe
     for slot in range(0, 6, 2):
-        pair = jnp.concatenate([S["eslot"][slot], S["eslot"][slot + 1]], axis=0)
+        pair = jnp.concatenate([S.eslot[slot], S.eslot[slot + 1]], axis=0)
         xe[slot * 8 : slot * 8 + 16, :] = pair.astype(bf16)
 
-    filte, hx = S["filte"], S["hx"]
+    filte, hx = S.filte, S.hx
     for i in range(2):
-        em = S["em"]
+        em = S.em
         got = nt(em[i, :, 0 : 5 * big], xj[0:80, 2 * i * big : (2 * i + 5) * big])
         got = got + nn(em[i, :, 5 * big :], xe[:, 0:80])
         for kk in range(nb):
             filte[kk, i * LANES : (i + 1) * LANES, :] = got[kk * LANES : (kk + 1) * LANES, 0:cj].astype(bf16)
-    loads["ew"].wait()
+    loads.ew.wait()
     h0 = vec(eb) + jnp.zeros((px, c), f32)
     for kk in range(nb):
-        h0 = h0 + nn(filte[kk], S["ew"][kk])
+        h0 = h0 + nn(filte[kk], S.ew[kk])
     hx[px : 2 * px, :] = h0
     own = slice(px, 2 * px)
     h0 = hx[own, :]
     stat_a = stat_start(0, *moments(h0))
-    pe = S["pe"]
+    pe = S.pe
     for side, col in ((0, 0), (1, LANES - 2)):
         for q in range(2):
             lo = px + q * LANES + col
@@ -752,37 +747,37 @@
             )
         )
     zero_halo = start(sends)
-    stat_a = stat_middle(0, stat_a, "moments")
-
-    dm, pgr = S["dm"], S["pgr"]
+    stat_a = stat_middle(0, stat_a, True)
+
+    dm, pgr = S.dm, S.pgr
     for i in range(2):
         got = nt(dm[i, :, 0 : 6 * big], xj[80 : 80 + 80, 2 * i * big : (2 * i + 6) * big])
         got = got + nn(dm[i, :, 6 * big :], xe[:, 80:160])
         for kk in range(nb):
             pgr[kk, i * LANES : (i + 1) * LANES, :] = got[kk * LANES : (kk + 1) * LANES, 0:cin].astype(bf16)
     ones = jnp.ones((16, 4 * big), bf16)
-    put_misc(gm, MISC["dec_bias"], nt(ones, xj[80:160, 2 * big : 6 * big])[0:1, 0:cin])
-
-    loads["cw"].wait()
-    two, mg = S["two"], S["mg"]
-    acc = nn(pgr[0], S["cw"][0])
+    put_misc(gm, MISC.dec_bias, nt(ones, xj[80:160, 2 * big : 6 * big])[0:1, 0:cin])
+
+    loads.cw.wait()
+    two, mg = S.two, S.mg
+    acc = nn(pgr[0], S.cw[0])
     for kk in range(1, nb):
-        acc = acc + nn(pgr[kk], S["cw"][kk])
+        acc = acc + nn(pgr[kk], S.cw[kk])
     two[...] = acc
     mg[...] = acc.astype(bf16)
-    loads["dw"].wait()
-    ag, hp = S["ag"], S["hp"]
-    ag[...] = nn(mg[...], S["dw"][...])
-    S["mgt"][...] = mg[...].T
-    put_misc(gm, MISC["down_bias"], jnp.sum(mg[...].astype(f32), axis=0, keepdims=True))
-
-    mean1, m2 = stat_end(0, stat_a, "moments")
+    loads.dw.wait()
+    ag, hp = S.ag, S.hp
+    ag[...] = nn(mg[...], S.dw[...])
+    S.mgt[...] = mg[...].T
+    put_misc(gm, MISC.down_bias, jnp.sum(mg[...].astype(f32), axis=0, keepdims=True))
+
+    mean1, m2 = stat_end(0, stat_a, True)
     var1 = m2 * (1.0 / s.pixels)
     rstd1 = lax.rsqrt(var1 + EPS)
     m1o[...] = mean1 * live
     v1o[...] = var1 * live
     arrive(zero_halo)
-    nx = S["nx"]
+    nx = S.nx
     scale1 = rstd1 * vec(gain1)
     bias1 = vec(shift1)
 
@@ -793,27 +788,27 @@
 
     lax.fori_loop(0, 17, norm_rows, 0)
 
-    filt, tm = S["filt"], S["tm"]
-    loads["pw"].wait()
-    h1 = S["h1"]
+    filt, tm = S.filt, S.tm
+    loads.pw.wait()
+    h1 = S.h1
     acc = hx[own, :] + vec(pb)
     for kk in range(nb):
         here = slice(kk * px, (kk + 1) * px)
         filt[here, :] = nn(tm[here, :], nx[...]).astype(bf16)
-        acc = acc + nt(filt[here, :], S["pw"][kk])
+        acc = acc + nt(filt[here, :], S.pw[kk])
     h1[...] = acc
     stat_b = stat_start(1, *moments(h1[...]))
-    stat_b = stat_middle(1, stat_b, "moments")
-    tm_t = S["tmt"]
+    stat_b = stat_middle(1, stat_b, True)
+    tm_t = S.tmt
     tm_t[...] = tm[...].T
-    mean2, m2 = stat_end(1, stat_b, "moments")
+    mean2, m2 = stat_end(1, stat_b, True)
     var2 = m2 * (1.0 / s.pixels)
     rstd2 = lax.rsqrt(var2 + EPS)
     m2o[...] = mean2 * live
     v2o[...] = var2 * live
     scale2 = rstd2 * vec(gain2)
     bias2 = vec(shift2)
-    n2 = S["n2"]
+    n2 = S.n2
 
     def norm_two_rows(n, carry):
         here = pl.ds(pl.multiple_of(n * 32, 16), 32)
@@ -822,9 +817,9 @@
 
     lax.fori_loop(0, px // 32, norm_two_rows, 0)
 
-    loads["uw"].wait()
-    hp[...] = nn(n2[...], S["uw"][...])
-    act, hg = S["act"], S["hg"]
+    loads.uw.wait()
+    hp[...] = nn(n2[...], S.uw[...])
+    act, hg = S.act, S.hg
     ubias = vec(ub)
     root = 0.7978845608028654
 
@@ -839,59 +834,60 @@
         return carry
 
     lax.fori_loop(0, px // 16, gelu_rows, 0)
-    ntg = S["ntg"]
-    ntg[...] = nt(hg[...], S["uw"][...])
+    g1 = S.g1
+    cols = [(lo, min(256, s.c5 * LANES - lo)) for lo in range(0, s.c5 * LANES, 256)]
+
+    def spread(g, off, height, pitch, value, lo, width):
+        for n in range(width // LANES):
+            at = off + (lo // LANES + n) * pitch
+            g[at : at + height, :] = value[:, n * LANES : (n + 1) * LANES].astype(bf16)
+
+    for lo in range(0, s.f10 * LANES, 256):
+        spread(g1, 0, c, s.r641, nn(S.mgt[...], act[:, lo : lo + 256]), lo, 256)
+    ar("a")
+    S.n2t[...] = n2[...].T
+    for lo in range(0, s.f10 * LANES, 256):
+        spread(g1, s.off_up, c, s.r641, nn(S.n2t[...], hg[:, lo : lo + 256]), lo, 256)
+    h2 = S.h2
+    h2[...] = (h1[...] + nt(act[...], S.dw[...]) + vec(db)).astype(bf16)
+    for kk in range(nb):
+        got = tn(pgr[kk], h2[:, 0 : s.c5 * LANES])
+        spread(g1, s.off_dec + kk * s.c5 * s.r80, cin, s.r80, got, 0, s.c5 * LANES)
+    ar("bea")
+    ntg = S.ntg
+    ntg[...] = nt(hg[...], S.uw[...])
     grad = ntg[...]
     standard = (h1[...] - mean2) * rstd2
     sum_a = jnp.sum(grad, axis=0, keepdims=True)
     sum_b = jnp.sum(grad * standard, axis=0, keepdims=True)
-    put_misc(gm, MISC["shift_two"], sum_a)
-    put_misc(gm, MISC["gain_two"], sum_b)
+    put_misc(gm, MISC.shift_two, sum_a)
+    put_misc(gm, MISC.gain_two, sum_b)
     stat_c = stat_start(2, sum_a, sum_b)
 
-    g1 = S["g1"]
-    cols = [(lo, min(256, s.c5 * LANES - lo)) for lo in range(0, s.c5 * LANES, 256)]
-
-    def spread(g, off, height, pitch, value, lo, width):
-        for n in range(width // LANES):
-            at = off + (lo // LANES + n) * pitch
-            g[at : at + height, :] = value[:, n * LANES : (n + 1) * LANES].astype(bf16)
-
-    for lo in range(0, s.f10 * LANES, 256):
-        spread(g1, 0, c, s.r641, nn(S["mgt"][...], act[:, lo : lo + 256]), lo, 256)
-    ar("A")
-    stat_c = stat_middle(2, stat_c, "sums")
-    S["n2t"][...] = n2[...].T
-    for lo in range(0, s.f10 * LANES, 256):
-        spread(g1, s.off_up, c, s.r641, nn(S["n2t"][...], hg[:, lo : lo + 256]), lo, 256)
-    h2 = S["h2"]
-    h2[...] = (h1[...] + nt(act[...], S["dw"][...]) + vec(db)).astype(bf16)
-    for kk in range(nb):
-        got = tn(pgr[kk], h2[:, 0 : s.c5 * LANES])
-        spread(g1, s.off_dec + kk * s.c5 * s.r80, cin, s.r80, got, 0, s.c5 * LANES)
-    ar("BA")
+    ar("dbecdfc")
+    stat_c = stat_middle(2, stat_c, False)
 
     def weighted(ref, column):
         return jnp.sum(ref.astype(f32) * column.astype(f32), axis=0, keepdims=True)
 
-    def put_long(name, row):
-        put_misc(gm, MISC[name], row[:, 0:768])
-        put_misc(gm, MISC[name] + 1, row[:, 768:])
+    def put_long(slot, row):
+        put_misc(gm, slot, row[:, 0:768])
+        put_misc(gm, slot + 1, row[:, 768:])
 
     def misc_one():
-        put_long("up_bias", jnp.sum(hg[...].astype(f32), axis=0, keepdims=True))
+        put_long(MISC.up_bias, jnp.sum(hg[...].astype(f32), axis=0, keepdims=True))
         for n in range(2):
             at = s.f10 * LANES + n
-            put_misc(gm, MISC["up_last"] + n, weighted(n2[...], hg[:, at : at + 1]))
-            put_misc(gm, MISC["down_last"] + n, weighted(mg[...], act[:, at : at + 1]))
+            put_misc(gm, MISC.up_last + n, weighted(n2[...], hg[:, at : at + 1]))
+            put_misc(gm, MISC.down_last + n, weighted(mg[...], act[:, at : at + 1]))
         for kk in range(nb):
-            put_misc(gm, MISC["dec_last"] + kk, weighted(pgr[kk], h2[:, c - 1 : c]))
-
-    sum_a, sum_b = stat_end(2, stat_c, "sums")
+            put_misc(gm, MISC.dec_last + kk, weighted(pgr[kk], h2[:, c - 1 : c]))
+
+    sum_a, sum_b = stat_end(2, stat_c, False)
     g_two = vec(gain2)
     part_a = g_two * sum_a * (1.0 / s.pixels)
     part_b = g_two * sum_b * (1.0 / s.pixels)
-    one, br = S["one"], S["br"]
+    one, br = S.one, S.br
 
     def one_rows(n, carry):
         here = pl.ds(pl.multiple_of(n * 32, 16), 32)
@@ -902,12 +898,12 @@
         return carry
 
     lax.fori_loop(0, px // 32, one_rows, 0)
-    ar("B")
-    fg = S["fg"]
+    ar("af")
+    fg = S.fg
     for kk in range(nb):
-        fg[kk * px : (kk + 1) * px, :] = nn(br[...], S["pw"][kk]).astype(bf16)
-    con = S["con"]
-    con[...] = nn(S["tmt"][...], fg[...])
+        fg[kk * px : (kk + 1) * px, :] = nn(br[...], S.pw[kk]).astype(bf16)
+    con = S.con
+    con[...] = nn(S.tmt[...], fg[...])
 
     def sum_rows(n, carry):
         here = pl.ds(pl.multiple_of(n * 48, 16), 48)
@@ -920,12 +916,12 @@
 
     zero_row = jnp.zeros((1, c), f32)
     sum_a, sum_b = lax.fori_loop(0, 17, sum_rows, (zero_row, zero_row))
-    put_misc(gm, MISC["shift_one"], sum_a)
-    put_misc(gm, MISC["gain_one"], sum_b)
+    put_misc(gm, MISC.shift_one, sum_a)
+    put_misc(gm, MISC.gain_one, sum_b)
     stat_d = stat_start(3, sum_a, sum_b)
     sends = [
-        Send(k, con.at[pl.ds(0, px)], S["rdn"], k.at(0, -1, 0), -1),
-        Send(k, con.at[pl.ds(2 * px, px)], S["rup"], k.at(0, 1, 0), 1),
+        Send(k, con.at[pl.ds(0, px)], S.rdn, k.at(0, -1, 0), -1),
+        Send(k, con.at[pl.ds(2 * px, px)], S.rup, k.at(0, 1, 0), 1),
     ]
     for dl, ds in dirs:
         mine = (dl + 1) * 2 + (ds + 1) // 2
@@ -933,41 +929,41 @@
             Send(
                 k,
                 con.at[pl.ds(768 + mine * 8, 8)],
-                S["reg"].at[slot_of(dl, ds)],
+                S.reg.at[slot_of(dl, ds)],
                 k.at(0, dl, ds),
                 dl,
             )
         )
     back_halo = start(sends)
-    g2 = S["g2"]
-    S["brt"][...] = br[...].T
-    ar("A")
+    g2 = S.g2
+    S.brt[...] = br[...].T
+    ar("b")
     for kk in range(nb):
         if kk == 1:
-            stat_d = stat_middle(3, stat_d, "sums")
+            stat_d = stat_middle(3, stat_d, False)
         for lo, width in cols:
-            got = nn(S["brt"][...], filt[kk * px : (kk + 1) * px, lo : lo + width])
+            got = nn(S.brt[...], filt[kk * px : (kk + 1) * px, lo : lo + width])
             spread(g2, kk * s.c5 * s.r641, c, s.r641, got, lo, width)
         if kk == 1:
-            ar("C")
-    ar("D")
-    ar("BA")
+            ar("gdceb")
+    ar("ijh")
 
     arrive(back_halo)
+    ar("afgjdhb")
     ng = ntg
     ng[...] = con[own, :]
 
     @pl.when(k.has_up())
     def _():
-        ng[...] = ng[...] + S["rup"][...]
+        ng[...] = ng[...] + S.rup[...]
 
     @pl.when(k.has_down())
     def _():
-        ng[...] = ng[...] + S["rdn"][...]
+        ng[...] = ng[...] + S.rdn[...]
 
     def add_edges(sl):
         for ss in (-1, 1):
-            got = S["reg"].at[(sl + 1) * 2 + (ss + 1) // 2]
+            got = S.reg.at[(sl + 1) * 2 + (ss + 1) // 2]
             col = 0 if ss == -1 else LANES - 2
             for q in range(2):
                 lo = q * LANES + col
@@ -976,11 +972,11 @@
     add_edges(0)
     pl.when(k.has_up())(lambda: add_edges(-1))
     pl.when(k.has_down())(lambda: add_edges(1))
-    sum_a, sum_b = stat_end(3, stat_d, "sums")
+    sum_a, sum_b = stat_end(3, stat_d, False)
     g_one = vec(gain1)
     part_a1 = g_one * sum_a * (1.0 / s.pixels)
     part_b1 = g_one * sum_b * (1.0 / s.pixels)
-    zg = S["zg"]
+    zg = S.zg
 
     def zero_rows(n, carry):
         here = pl.ds(pl.multiple_of(n * 32, 16), 32)
@@ -992,30 +988,30 @@
 
     lax.fori_loop(0, px // 32, zero_rows, 0)
 
-    g3 = S["g3"]
+    g3 = S.g3
     for kk in range(nb):
         got = tn(filte[kk], zg[:, 0 : s.c5 * LANES])
         spread(g3, kk * s.c5 * s.r80, cj, s.r80, got, 0, s.c5 * LANES)
-        put_misc(gm, MISC["enc_last"] + kk, weighted(filte[kk], zg[:, c - 1 : c]))
-    put_misc(gm, MISC["enc_bias"], jnp.sum(zg[...].astype(f32), axis=0, keepdims=True))
-    ar("E")
+        put_misc(gm, MISC.enc_last + kk, weighted(filte[kk], zg[:, c - 1 : c]))
+    put_misc(gm, MISC.enc_bias, jnp.sum(zg[...].astype(f32), axis=0, keepdims=True))
+    ar("k")
     misc_one()
-    put_misc(gm, MISC["proc_bias"], jnp.sum(br[...].astype(f32), axis=0, keepdims=True))
+    put_misc(gm, MISC.proc_bias, jnp.sum(br[...].astype(f32), axis=0, keepdims=True))
     for kk in range(nb):
-        put_misc(gm, MISC["proc_last"] + kk, weighted(br[...], filt[kk * px : (kk + 1) * px, c - 1 : c]))
-    ar("MCDBA")
-
-    projt, partt = S["projt"], S["partt"]
+        put_misc(gm, MISC.proc_last + kk, weighted(br[...], filt[kk * px : (kk + 1) * px, c - 1 : c]))
+    ar("ajekgfid")
+
+    projt, partt = S.projt, S.partt
     for kk in range(nb):
         here = slice(kk * LANES, (kk + 1) * LANES)
-        proj = nt(h2[...], S["cw"][kk])
-        part = nt(zg[...], S["ew"][kk])[:, 0:cin]
+        proj = nt(h2[...], S.cw[kk])
+        part = nt(zg[...], S.ew[kk])[:, 0:cin]
         for i in range(2):
             for ref, value in ((projt, proj), (partt, part)):
                 ref[i, 0:cin, here] = value[i * LANES : (i + 1) * LANES, :].T.astype(bf16)
                 ref[i, cin:80, here] = jnp.zeros((80 - cin, LANES), bf16)
-    sgx = S["sgx"]
-    em = S["em"]
+    sgx = S.sgx
+    em = S.em
     sgx[...] = jnp.zeros(sgx.shape, f32)
     for i in range(2):
         lo = 2 * i * big
@@ -1025,24 +1021,25 @@
         got = nn(partt[i], em[i])
         sgx[80:160, lo : lo + 5 * big] = sgx[80:160, lo : lo + 5 * big] + got[:, 0 : 5 * big]
         sgx[80:160, edge0 : edge0 + 48] = sgx[80:160, edge0 : edge0 + 48] + got[:, 5 * big :]
-    sgb, sgu, sgd, sge = S["sgb"], S["sgu"], S["sgd"], S["sge"]
+    sgb, sgu, sgd, sge = S.sgb, S.sgu, S.sgd, S.sge
     sgb[:, 0 : 2 * big] = sgx[:, 0 : 2 * big].astype(bf16)
     sgb[:, 2 * big : 4 * big] = sgx[:, 6 * big : 8 * big].astype(bf16)
     turned = sgx[:, edge0:].T
     for n in range(6):
-        S["sgn"][n] = turned[n * 8 : n * 8 + 8, :]
+        S.sgn[n] = turned[n * 8 : n * 8 + 8, :]
     sends = [
         Send(k, sgb.at[:, pl.ds(0, 2 * big)], sgd, k.at(0, -1, 0), -1),
         Send(k, sgb.at[:, pl.ds(2 * big, 2 * big)], sgu, k.at(0, 1, 0), 1),
     ]
     for dl, ds in dirs:
         sends.append(
-            Send(k, S["sgn"].at[(dl + 1) * 2 + (ds + 1) // 2], sge.at[slot_of(dl, ds)], k.at(0, dl, ds), dl)
+            Send(k, S.sgn.at[(dl + 1) * 2 + (ds + 1) // 2], sge.at[slot_of(dl, ds)], k.at(0, dl, ds), dl)
         )
     out_halo = start(sends)
-    ar("CDEABM")
+    ar("hagbkfelcl")
     arrive(out_halo)
-    sgt = S["sgt"]
+    ar("iahldcgiebdhlkjafgiehklcbjgi")
+    sgt = S.sgt
     sgt[48:LANES, :] = jnp.zeros((LANES - 48, 160), f32)
     for slot in range(6):
         sgt[slot * 8 : slot * 8 + 8, :] = sge[slot]
@@ -1053,11 +1050,11 @@
     arrived = sgt[...].T
     up_one = jnp.where(k.has_up(), 1, 0)
     down_one = jnp.where(k.has_down(), 1, 0)
-    cbt = S["cbt"]
+    cbt = S.cbt
     cbt[...] = jnp.zeros((8, LANES), f32)
     cbt[0:1, 0:cin] = vec(cb)
     bias_col = cbt[...].T[0:cin, 0:1]
-    orow, st7 = S["orow"], S["st7"]
+    orow, st7 = S.orow, S.st7
 
     for q in range(4):
         lo = (2 + q) * big
@@ -1086,22 +1083,23 @@
     state_sends = start(
         [Send(k, st7.at[k.e], st7.at[k.e], k.at(d, 0, 0)) for d in range(1, s.ne)]
     )
-    ar("ACBDEM")
-    ar("ABCDEM")
+    ar("ckhfdljkiglgcjble")
     arrive(date_sends)
     arrive(state_sends)
+    ar("dahfk")
     for d in range(s.dates):
         for q in range(4):
             value = jnp.zeros((80, big), f32)
             for n in range(s.ne):
-                is_d = jnp.where(S["dates"][n, 0:1, :] == float(d), 1.0, 0.0)
+                is_d = jnp.where(S.dates[n, 0:1, :] == float(d), 1.0, 0.0)
                 is_d = jnp.concatenate([is_d] * (big // LANES), axis=1)
                 value = value + is_d * st7[n, :, q * big : (q + 1) * big].astype(f32)
             orow[:, q, :] = value[0:cin]
         sgrad[d] = orow[...].astype(bf16)
 
+    ar("elijkfhcij")
     while not all(it.finished() for it in reduced.values()):
-        ar("ABCDEM")
+        ar("abcdefghijkl")
     for m in pending:
         m.wait_send()
 
@@ -1150,15 +1148,15 @@
     last = s.c5 * LANES
     for kk in range(nb):
         ref = proc_v.at[kk]
-        last_column(ref, MISC["proc_last"] + kk, c, last)
+        last_column(ref, MISC.proc_last + kk, c, last)
         loads[kk].wait()
         widen(ref, b2, kk * third, s.r641, c, s.c5)
         store(ref, proc_w.at[kk])
-    for n, (ref, name, base, to) in enumerate(
-        ((down_v, "down_last", 0, down_w), (up_v, "up_last", s.off_up, up_w))
+    for n, (ref, slot, base, to) in enumerate(
+        ((down_v, MISC.down_last, 0, down_w), (up_v, MISC.up_last, s.off_up, up_w))
     ):
         for part in range(2):
-            last_column(ref, MISC[name] + part, c, s.f10 * LANES + part)
+            last_column(ref, slot + part, c, s.f10 * LANES + part)
         loads[nb + n].wait()
         widen(ref, b1, base, s.r641, c, s.f10)
         store(ref, to)
@@ -1166,10 +1164,10 @@
     loads[nb + 3].wait()
     for kk in range(nb):
         ref = dec_v.at[kk]
-        last_column(ref, MISC["dec_last"] + kk, cin, last)
+        last_column(ref, MISC.dec_last + kk, cin, last)
         widen(ref, b1, s.off_dec + kk * s.c5 * s.r80, s.r80, cin, s.c5)
         ref = enc_v.at[kk]
-        last_column(ref, MISC["enc_last"] + kk, cj, last)
+        last_column(ref, MISC.enc_last + kk, cj, last)
         widen(ref, b3, kk * s.c5 * s.r80, s.r80, cj, s.c5)
     store(dec_v, dec_w)
     store(enc_v, enc_w)
@@ -1183,13 +1181,13 @@
                 at += n
         ref[...] = row_v[0:1, 0:at].reshape(at)
 
-    for ref, name in (
-        (enc_b, "enc_bias"), (g1o, "gain_one"), (s1o, "shift_one"), (proc_b, "proc_bias"),
-        (g2o, "gain_two"), (s2o, "shift_two"), (down_b, "down_bias"),
+    for ref, slot in (
+        (enc_b, MISC.enc_bias), (g1o, MISC.gain_one), (s1o, MISC.shift_one), (proc_b, MISC.proc_bias),
+        (g2o, MISC.gain_two), (s2o, MISC.shift_two), (down_b, MISC.down_bias),
     ):
-        flat(ref, [(MISC[name], c)])
-    flat(up_b, [(MISC["up_bias"], 768), (MISC["up_bias"] + 1, ff - 768)])
-    flat(dec_b, [(MISC["dec_bias"], cin)])
+        flat(ref, [(slot, c)])
+    flat(up_b, [(MISC.up_bias, 768), (MISC.up_bias + 1, ff - 768)])
+    flat(dec_b, [(MISC.dec_bias, cin)])
     for copy in stores:
         copy.wait()
 
@@ -1207,7 +1205,6 @@
     sm = pl.BlockSpec(memory_space=pltpu.SMEM)
     hbm = pl.BlockSpec(memory_space=pl.ANY)
     shapes = scratch_list(s)
-    shapes["sems"] = pltpu.SemaphoreType.DMA((sem_count(s),))
     names = tuple(shapes)
     in_specs = [vm] * 3 + [sm] * 5 + [
         hbm, vm, vm, vm, hbm, vm, vm, vm, hbm, vm, hbm, vm, hbm, vm,

time: 119 us -> 113 us (0.950)
  Pallas kernels: 118 us -> 111 us
    pallas_call x1, Pallas kernels: 109 us -> 102 us  [per_device(): pl.pallas_call(functools.partial(main_kernel, s, names), out_shape=out_sh...]
where the time goes in v4:
time: 113 us; the launch traced here: 112 us
  Pallas kernels  111 us (98%)
  between operations  1.5 us (1%)
    pallas_call x1, Pallas kernels, per_device(): pl.pallas_call(functools.partial(main_kernel, s, names), out_shape=out_sh...  102 us
    pallas_call x1, Pallas kernels, per_device(): pl.pallas_call(functools.partial(finish_kernel, s), out_shape=outs, in_sp...  8.83 us

profile of v4, /device:TPU:0, one launch (start us, length us, event | category | flops | bytes accessed | tf_op | source)
XLA Modules:
  0.0 112.3 jit_solution(14683217734237331777)
XLA Ops:
  1.3 102.0 %forecast.1 = (bf16[14336,128]{1,0:T(8,128)(2,1)}, bf16[10240,128]{1,0:T(8,128)(2,1)}, bf16[1536,128]{1,0:T(8,128)(2,1)}, f32[256,128]{1,0:T(8,128)}, bf16[1,72,...) custom-call(bf16[2,72,4,256]{3,2,1,0:T(4,128)(2,1)} %refs_0_.1, ...), custom_call_target="tpu_custom_call" | custom-call | tf_op jit(solution)/shard_map/forecast/pallas_call | solution.py:1221
  103.3 8.8 %finish.1 = (bf16[1,72,4,256]{3,2,1,0:T(4,128)(2,1)}, bf16[2,72,4,256]{3,2,1,0:T(4,128)(2,1)}, f32[3,80,641]{2,1,0:T(8,128)}, f32[641]{0:T(1024)}, f32[641]{0:T(...) custom-call(bf16[14336,128]{1,0:T(8,128)(2,1)} %get-tuple-element.50, ...), custom_call_target="tpu_custom_call" | custom-call | tf_op jit(solution)/shard_map/finish/pallas_call | solution.py:1241

commit v5 on v4

--- a/solution.py
+++ b/solution.py
@@ -23,7 +23,7 @@
 ROUTE_ZY = (LAT, LON, BIT1, BIT0)
 PIECES = dict(
     a=(0, 0), b=(0, 1), c=(0, 2), d=(1, 0), e=(1, 1), f=(1, 2),
-    g=(2, 0), h=(2, 1), i=(3, 0), j=(3, 1), k=(4, 0), l=(5, 0),
+    g=(2, 0), h=(2, 1), i=(3, 0), j=(3, 1), k=(4, 0), l=(5, 0), m=(2, 2), n=(3, 2),
 )
 
 
@@ -74,9 +74,9 @@
         self.rows = tuple(up_to(n, unit) for n in used) + (up_to(24 * 6, unit // 2),)
         self.chunks = {}
 
-        def split(piece, buffer, lo, hi, third=None):
+        def split(piece, buffer, lo, hi, third, last):
             units = (hi - lo) // unit
-            last = 2 if third and units >= 6 else 0
+            last = last if units >= 3 * last else 0
             first = (units - last + 1) // 2
             at = lo
             for n, (count, route) in enumerate(
@@ -87,11 +87,11 @@
                 at += count * unit
 
         cut = self.off_up // unit * unit
-        split(0, 0, 0, cut, ROUTE_ZX)
-        split(1, 0, cut, self.rows[0], ROUTE_ZY)
+        split(0, 0, 0, cut, ROUTE_ZX, 2)
+        split(1, 0, cut, self.rows[0], ROUTE_ZY, 2)
         cut = 2 * self.c5 * self.r641 // unit * unit
-        split(2, 1, 0, cut)
-        split(3, 1, cut, self.rows[1])
+        split(2, 1, 0, cut, ROUTE_ZX, 0)
+        split(3, 1, cut, self.rows[1], ROUTE_ZY, 0)
         self.chunks[4, 0] = (2, 0, self.rows[2], ROUTE_X)
         self.chunks[5, 0] = (3, 0, self.rows[3], ROUTE_Y)
         self.group = self.nl * self.nz
@@ -290,6 +290,14 @@
     wide = 8 * big + LANES
     V = pltpu.VMEM
     shapes = dict(
+        state=V((s.dates, s.cin, s.full_rows, big), bf16),
+        noise=V((1, s.noise, s.full_rows, big), bf16),
+        cot=V((1, s.cin, s.full_rows, big), bf16),
+        eb_v=V((c,), f32), gain1=V((c,), f32), shift1=V((c,), f32), pb=V((c,), f32), gain2=V((c,), f32),
+        shift2=V((c,), f32), ub=V((ff,), f32), db=V((c,), f32), cb=V((s.cin,), f32),
+        out=V((1, s.cin, s.full_rows, big), bf16),
+        sgrad=V((s.dates, s.cin, s.full_rows, big), bf16),
+        means=V((4, 1, c), f32),
         xin=V((160, s.full_rows, big), f32),
         xj=V((160, 8 * big), bf16),
         eb=V((2, 8, 160), f32),
@@ -356,7 +364,7 @@
         kinds = AllReduce.shapes(s, rows, route, f32 if buffer == 3 else bf16)
         for j, kind in enumerate(kinds):
             shapes[name, j] = kind
-    shapes[WSEM] = pltpu.SemaphoreType.DMA((5,))
+    shapes[WSEM] = pltpu.SemaphoreType.DMA((23,))
     shapes[OSEM] = pltpu.SemaphoreType.DMA((len(s.chunks),))
     shapes[SEMS] = pltpu.SemaphoreType.DMA((sem_count(s),))
     return shapes
@@ -364,7 +372,7 @@
 
 def sem_count(s):
     total = len(s.chunks) * 2 * 2 * (s.nl - 1 + 1 + 1 + s.nz - 1)
-    total += 2 * 4 * 8 + 2 * 2 * (s.ne - 1)
+    total += 2 * 4 * 8 + 2 * (s.ne - 1) + 2 * 6
     total += 4 * 2 * (s.group - 1 if s.group <= 16 else s.nl - 1 + s.nz - 1)
     return total
 
@@ -372,10 +380,10 @@
 def main_kernel(s, names, *refs):
     n_in, n_out = 22, 10
     (
-        state, noise, cot, date_ref, reach, enc_taps, proc_taps, dec_taps,
-        ew_h, eb, gain1, shift1, pw_h, pb, gain2, shift2, uw_h, ub, dw_h, db, cw_h, cb,
+        state_h, noise_h, cot_h, date_ref, reach, enc_taps, proc_taps, dec_taps,
+        ew_h, eb_h, gain1_h, shift1_h, pw_h, pb_h, gain2_h, shift2_h, uw_h, ub_h, dw_h, db_h, cw_h, cb_h,
     ) = refs[:n_in]
-    h1o, h2o, h3o, hmo, out, sgrad, m1o, v1o, m2o, v2o = refs[n_in : n_in + n_out]
+    h1o, h2o, h3o, hmo, out_h, sgrad_h, m1_h, v1_h, m2_h, v2_h = refs[n_in : n_in + n_out]
     table = dict(zip(names, refs[n_in + n_out :]))
     S = types.SimpleNamespace(**{n: r for n, r in table.items() if isinstance(n, str)})
     sems = table[SEMS]
@@ -397,14 +405,40 @@
     for o in offsets:
         pl.semaphore_signal(barrier, 1, device_id=k.at(*o), device_id_type=MESH)
 
-    loads, weights = types.SimpleNamespace(), []
-    for n, (src, to) in enumerate(
-        ((ew_h, S.ew), (pw_h, S.pw), (uw_h, S.uw), (dw_h, S.dw), (cw_h, S.cw))
-    ):
+    def fetch(n, src, to):
         copy = pltpu.make_async_copy(src, to, table[WSEM].at[n])
         copy.start()
-        weights.append(copy)
-    loads.ew, loads.pw, loads.uw, loads.dw, loads.cw = weights
+        return copy
+
+    state, noise, cot = S.state, S.noise, S.cot
+    fields = [fetch(n, *pair) for n, pair in enumerate(((state_h, state), (noise_h, noise), (cot_h, cot)))]
+    eb, gain1, shift1, pb, gain2, shift2 = S.eb_v, S.gain1, S.shift1, S.pb, S.gain2, S.shift2
+    ub, db, cb = S.ub, S.db, S.cb
+    vectors = [
+        fetch(3 + n, *pair)
+        for n, pair in enumerate(
+            (
+                (eb_h, eb), (gain1_h, gain1), (shift1_h, shift1), (pb_h, pb), (gain2_h, gain2),
+                (shift2_h, shift2), (ub_h, ub), (db_h, db), (cb_h, cb),
+            )
+        )
+    ]
+    loads = types.SimpleNamespace()
+    loads.ew, loads.pw, loads.cw, loads.dw, loads.uw = [
+        fetch(12 + n, *pair)
+        for n, pair in enumerate(
+            ((ew_h, S.ew), (pw_h, S.pw), (cw_h, S.cw), (dw_h, S.dw), (uw_h, S.uw))
+        )
+    ]
+    finals = []
+
+    def keep(src, to):
+        copy = pltpu.make_async_copy(src, to, table[WSEM].at[17 + len(finals)])
+        copy.start()
+        finals.append(copy)
+
+    for copy in fields:
+        copy.wait()
 
     date = date_ref[0]
     live = jnp.where(date >= 0, 1.0, 0.0).astype(f32)
@@ -718,6 +752,8 @@
         got = got + nn(em[i, :, 5 * big :], xe[:, 0:80])
         for kk in range(nb):
             filte[kk, i * LANES : (i + 1) * LANES, :] = got[kk * LANES : (kk + 1) * LANES, 0:cj].astype(bf16)
+    for copy in vectors:
+        copy.wait()
     loads.ew.wait()
     h0 = vec(eb) + jnp.zeros((px, c), f32)
     for kk in range(nb):
@@ -765,17 +801,14 @@
         acc = acc + nn(pgr[kk], S.cw[kk])
     two[...] = acc
     mg[...] = acc.astype(bf16)
-    loads.dw.wait()
-    ag, hp = S.ag, S.hp
-    ag[...] = nn(mg[...], S.dw[...])
-    S.mgt[...] = mg[...].T
-    put_misc(gm, MISC.down_bias, jnp.sum(mg[...].astype(f32), axis=0, keepdims=True))
 
     mean1, m2 = stat_end(0, stat_a, True)
     var1 = m2 * (1.0 / s.pixels)
     rstd1 = lax.rsqrt(var1 + EPS)
-    m1o[...] = mean1 * live
-    v1o[...] = var1 * live
+    S.means[0] = mean1 * live
+    S.means[1] = var1 * live
+    keep(S.means.at[0], m1_h)
+    keep(S.means.at[1], v1_h)
     arrive(zero_halo)
     nx = S.nx
     scale1 = rstd1 * vec(gain1)
@@ -799,13 +832,20 @@
     h1[...] = acc
     stat_b = stat_start(1, *moments(h1[...]))
     stat_b = stat_middle(1, stat_b, True)
+    loads.dw.wait()
+    ag, hp = S.ag, S.hp
+    ag[...] = nn(mg[...], S.dw[...])
+    S.mgt[...] = mg[...].T
+    put_misc(gm, MISC.down_bias, jnp.sum(mg[...].astype(f32), axis=0, keepdims=True))
     tm_t = S.tmt
     tm_t[...] = tm[...].T
     mean2, m2 = stat_end(1, stat_b, True)
     var2 = m2 * (1.0 / s.pixels)
     rstd2 = lax.rsqrt(var2 + EPS)
-    m2o[...] = mean2 * live
-    v2o[...] = var2 * live
+    S.means[2] = mean2 * live
+    S.means[3] = var2 * live
+    keep(S.means.at[2], m2_h)
+    keep(S.means.at[3], v2_h)
     scale2 = rstd2 * vec(gain2)
     bias2 = vec(shift2)
     n2 = S.n2
@@ -844,7 +884,7 @@
 
     for lo in range(0, s.f10 * LANES, 256):
         spread(g1, 0, c, s.r641, nn(S.mgt[...], act[:, lo : lo + 256]), lo, 256)
-    ar("a")
+    ar("ba")
     S.n2t[...] = n2[...].T
     for lo in range(0, s.f10 * LANES, 256):
         spread(g1, s.off_up, c, s.r641, nn(S.n2t[...], hg[:, lo : lo + 256]), lo, 256)
@@ -853,7 +893,7 @@
     for kk in range(nb):
         got = tn(pgr[kk], h2[:, 0 : s.c5 * LANES])
         spread(g1, s.off_dec + kk * s.c5 * s.r80, cin, s.r80, got, 0, s.c5 * LANES)
-    ar("bea")
+    ar("bace")
     ntg = S.ntg
     ntg[...] = nt(hg[...], S.uw[...])
     grad = ntg[...]
@@ -864,7 +904,7 @@
     put_misc(gm, MISC.gain_two, sum_b)
     stat_c = stat_start(2, sum_a, sum_b)
 
-    ar("dbecdfc")
+    ar("cdfed")
     stat_c = stat_middle(2, stat_c, False)
 
     def weighted(ref, column):
@@ -884,6 +924,7 @@
             put_misc(gm, MISC.dec_last + kk, weighted(pgr[kk], h2[:, c - 1 : c]))
 
     sum_a, sum_b = stat_end(2, stat_c, False)
+    ar("fb")
     g_two = vec(gain2)
     part_a = g_two * sum_a * (1.0 / s.pixels)
     part_b = g_two * sum_b * (1.0 / s.pixels)
@@ -898,7 +939,7 @@
         return carry
 
     lax.fori_loop(0, px // 32, one_rows, 0)
-    ar("af")
+    ar("a")
     fg = S.fg
     for kk in range(nb):
         fg[kk * px : (kk + 1) * px, :] = nn(br[...], S.pw[kk]).astype(bf16)
@@ -937,7 +978,6 @@
     back_halo = start(sends)
     g2 = S.g2
     S.brt[...] = br[...].T
-    ar("b")
     for kk in range(nb):
         if kk == 1:
             stat_d = stat_middle(3, stat_d, False)
@@ -945,11 +985,11 @@
             got = nn(S.brt[...], filt[kk * px : (kk + 1) * px, lo : lo + width])
             spread(g2, kk * s.c5 * s.r641, c, s.r641, got, lo, width)
         if kk == 1:
-            ar("gdceb")
-    ar("ijh")
+            ar("edgha")
+    ar("ijbchg")
 
     arrive(back_halo)
-    ar("afgjdhb")
+    ar("ei")
     ng = ntg
     ng[...] = con[own, :]
 
@@ -987,6 +1027,7 @@
         return carry
 
     lax.fori_loop(0, px // 32, zero_rows, 0)
+    ar("c")
 
     g3 = S.g3
     for kk in range(nb):
@@ -994,12 +1035,12 @@
         spread(g3, kk * s.c5 * s.r80, cj, s.r80, got, 0, s.c5 * LANES)
         put_misc(gm, MISC.enc_last + kk, weighted(filte[kk], zg[:, c - 1 : c]))
     put_misc(gm, MISC.enc_bias, jnp.sum(zg[...].astype(f32), axis=0, keepdims=True))
-    ar("k")
+    ar("adj")
     misc_one()
     put_misc(gm, MISC.proc_bias, jnp.sum(br[...].astype(f32), axis=0, keepdims=True))
     for kk in range(nb):
         put_misc(gm, MISC.proc_last + kk, weighted(br[...], filt[kk * px : (kk + 1) * px, c - 1 : c]))
-    ar("ajekgfid")
+    ar("k")
 
     projt, partt = S.projt, S.partt
     for kk in range(nb):
@@ -1036,9 +1077,9 @@
             Send(k, S.sgn.at[(dl + 1) * 2 + (ds + 1) // 2], sge.at[slot_of(dl, ds)], k.at(0, dl, ds), dl)
         )
     out_halo = start(sends)
-    ar("hagbkfelcl")
+    ar("fkcbgjaiheldf")
     arrive(out_halo)
-    ar("iahldcgiebdhlkjafgiehklcbjgi")
+    ar("l")
     sgt = S.sgt
     sgt[48:LANES, :] = jnp.zeros((LANES - 48, 160), f32)
     for slot in range(6):
@@ -1079,14 +1120,30 @@
         orow[:, q, LANES:big] = (tail[0:cin] + bias_col) * live
         st7[k.e, :, q * big : q * big + LANES] = head[80:160].astype(bf16)
         st7[k.e, :, q * big + LANES : (q + 1) * big] = tail[80:160].astype(bf16)
-    out[0] = orow[...].astype(bf16)
+    S.out[0] = orow[...].astype(bf16)
+    keep(S.out, out_h)
+    def state_piece(slot, half):
+        return st7.at[slot, :, pl.ds(half * 2 * big, 2 * big)]
+
+    e_x, e_y = k.flip(0)[0], k.flip(1)[0]
     state_sends = start(
-        [Send(k, st7.at[k.e], st7.at[k.e], k.at(d, 0, 0)) for d in range(1, s.ne)]
+        [
+            Send(k, state_piece(k.e, half), state_piece(k.e, half), k.flip(half))
+            for half in range(2)
+        ]
     )
-    ar("ckhfdljkiglgcjble")
+    ar("ckfgbahefidbgl")
+    arrive(state_sends)
+    state_sends = start(
+        [
+            Send(k, state_piece(slot, half), state_piece(slot, half), k.flip(1 - half))
+            for half, slots in ((0, (k.e, e_x)), (1, (k.e, e_y)))
+            for slot in slots
+        ]
+    )
+    ar("kdhbjgieklhjgckihdjlekdafljiagklhcke")
     arrive(date_sends)
     arrive(state_sends)
-    ar("dahfk")
     for d in range(s.dates):
         for q in range(4):
             value = jnp.zeros((80, big), f32)
@@ -1095,23 +1152,29 @@
                 is_d = jnp.concatenate([is_d] * (big // LANES), axis=1)
                 value = value + is_d * st7[n, :, q * big : (q + 1) * big].astype(f32)
             orow[:, q, :] = value[0:cin]
-        sgrad[d] = orow[...].astype(bf16)
-
-    ar("elijkfhcij")
+        S.sgrad[d] = orow[...].astype(bf16)
+    keep(S.sgrad, sgrad_h)
+
+    ar("bfhjiclfgjil")
     while not all(it.finished() for it in reduced.values()):
-        ar("abcdefghijkl")
+        ar("abcdefghijklmn")
     for m in pending:
         m.wait_send()
+    for copy in finals:
+        copy.wait()
 
 
 def finish_kernel(s, *refs):
-    h1, h2, h3, hm, output_in, state_in, m1, v1, m2, v2 = refs[:10]
+    h1, h2, h3, hm_h, output_in, state_in, m1, v1, m2, v2 = refs[:10]
     (
         output, state_grad,
         enc_w, enc_b, g1o, s1o, proc_w, proc_b, g2o, s2o,
         up_w, up_b, down_w, down_b, dec_w, dec_b, m1o, v1o, m2o, v2o,
     ) = refs[10:30]
-    (b1, b2, b3, enc_v, proc_v, up_v, down_v, dec_v, row_v, sem_in, sem_out) = refs[30:]
+    (
+        b1, b2, b3, enc_v, proc_v, up_v, down_v, dec_v, row_v, hm, out_v, state_v, means_v,
+        *vectors, sem_in, sem_out,
+    ) = refs[30:]
     c, ff, nb, cin, cj = s.c, s.ff, s.nb, s.cin, s.cj
     used1 = s.off_dec + nb * s.c5 * s.r80
     third = s.c5 * s.r641
@@ -1122,7 +1185,18 @@
         pltpu.make_async_copy(a.at[pl.ds(at, n)], b.at[pl.ds(at, n)], sem_in.at[i])
         for i, (a, b, at, n) in enumerate(pieces)
     ]
+    passed = [(output_in, out_v, output), (state_in, state_v, state_grad)]
+    passed += [
+        (a, means_v.at[n], b) for n, (a, b) in enumerate(((m1, m1o), (v1, v1o), (m2, m2o), (v2, v2o)))
+    ]
+    small = pltpu.make_async_copy(hm_h, hm, sem_in.at[len(pieces)])
+    small.start()
     for copy in loads:
+        copy.start()
+    early = [
+        pltpu.make_async_copy(a, b, sem_in.at[len(pieces) + 1 + n]) for n, (a, b, _) in enumerate(passed)
+    ]
+    for copy in early:
         copy.start()
     stores = []
 
@@ -1131,8 +1205,7 @@
         copy.start()
         stores.append(copy)
 
-    for a, b in ((output_in, output), (state_in, state_grad), (m1, m1o), (v1, v1o), (m2, m2o), (v2, v2o)):
-        b[...] = a[...]
+    small.wait()
     turned = hm[0:144, :].T
 
     def last_column(ref, slot, height, at):
@@ -1140,35 +1213,42 @@
             n = min(LANES, height - t * LANES)
             ref[t * LANES : t * LANES + n, at : at + 1] = turned[0:n, slot * 6 + t : slot * 6 + t + 1]
 
-    def widen(ref, src, base, pitch, height, tiles):
+    def widen(ref, src, base, pitch, tiles, lo, hi):
         for n in range(tiles):
             at = base + n * pitch
-            ref[:, n * LANES : (n + 1) * LANES] = src[at : at + height, :].astype(f32)
+            ref[lo:hi, n * LANES : (n + 1) * LANES] = src[at + lo : at + hi, :].astype(f32)
 
     last = s.c5 * LANES
+    half = up_to(c // 2, 16)
+    cuts = (0, half, c)
     for kk in range(nb):
         ref = proc_v.at[kk]
         last_column(ref, MISC.proc_last + kk, c, last)
         loads[kk].wait()
-        widen(ref, b2, kk * third, s.r641, c, s.c5)
-        store(ref, proc_w.at[kk])
+        for lo, hi in zip(cuts, cuts[1:]):
+            widen(ref, b2, kk * third, s.r641, s.c5, lo, hi)
+            store(ref.at[pl.ds(lo, hi - lo)], proc_w.at[kk, pl.ds(lo, hi - lo)])
     for n, (ref, slot, base, to) in enumerate(
         ((down_v, MISC.down_last, 0, down_w), (up_v, MISC.up_last, s.off_up, up_w))
     ):
         for part in range(2):
             last_column(ref, slot + part, c, s.f10 * LANES + part)
         loads[nb + n].wait()
-        widen(ref, b1, base, s.r641, c, s.f10)
-        store(ref, to)
+        for lo, hi in zip(cuts, cuts[1:]):
+            widen(ref, b1, base, s.r641, s.f10, lo, hi)
+            store(ref.at[pl.ds(lo, hi - lo)], to.at[pl.ds(lo, hi - lo)])
     loads[nb + 2].wait()
     loads[nb + 3].wait()
     for kk in range(nb):
         ref = dec_v.at[kk]
         last_column(ref, MISC.dec_last + kk, cin, last)
-        widen(ref, b1, s.off_dec + kk * s.c5 * s.r80, s.r80, cin, s.c5)
+        widen(ref, b1, s.off_dec + kk * s.c5 * s.r80, s.r80, s.c5, 0, cin)
         ref = enc_v.at[kk]
         last_column(ref, MISC.enc_last + kk, cj, last)
-        widen(ref, b3, kk * s.c5 * s.r80, s.r80, cj, s.c5)
+        widen(ref, b3, kk * s.c5 * s.r80, s.r80, s.c5, 0, cj)
+    for copy, (_, there, to) in zip(early, passed):
+        copy.wait()
+        store(there, to)
     store(dec_v, dec_w)
     store(enc_v, enc_w)
 
@@ -1179,7 +1259,9 @@
                 n = piece.shape[1]
                 row_v[0:1, at : at + n] = piece
                 at += n
-        ref[...] = row_v[0:1, 0:at].reshape(at)
+        there = vectors.pop()
+        there[...] = row_v[0:1, 0:at].reshape(at)
+        store(there, ref)
 
     for ref, slot in (
         (enc_b, MISC.enc_bias), (g1o, MISC.gain_one), (s1o, MISC.shift_one), (proc_b, MISC.proc_bias),
@@ -1206,9 +1288,7 @@
     hbm = pl.BlockSpec(memory_space=pl.ANY)
     shapes = scratch_list(s)
     names = tuple(shapes)
-    in_specs = [vm] * 3 + [sm] * 5 + [
-        hbm, vm, vm, vm, hbm, vm, vm, vm, hbm, vm, hbm, vm, hbm, vm,
-    ]
+    in_specs = [hbm] * 3 + [sm] * 5 + [hbm] * 14
     sd = jax.ShapeDtypeStruct
     out_shape = [
         sd((s.rows[0], LANES), bf16),
@@ -1222,7 +1302,7 @@
         functools.partial(main_kernel, s, names),
         out_shape=out_shape,
         in_specs=in_specs,
-        out_specs=[hbm] * 4 + [vm] * 6,
+        out_specs=[hbm] * 10,
         scratch_shapes=list(shapes.values()),
         compiler_params=pltpu.CompilerParams(
             collective_id=0, has_side_effects=True, vmem_limit_bytes=60 * 2**20
@@ -1236,18 +1316,19 @@
         sd((c, ff), f32), sd((ff,), f32), sd((c, ff), f32), sd((c,), f32),
         sd((nb, s.cin, c), f32), sd((s.cin,), f32),
     ] + [sd((1, c), f32)] * 4
-    large = (2, 6, 10, 12, 14)
     V = pltpu.VMEM
     done = pl.pallas_call(
         functools.partial(finish_kernel, s),
         out_shape=outs,
-        in_specs=[hbm] * 3 + [vm] * 7,
-        out_specs=[hbm if n in large else vm for n in range(len(outs))],
+        in_specs=[hbm] * 10,
+        out_specs=[hbm] * len(outs),
         scratch_shapes=[
             V((s.rows[0], LANES), bf16), V((s.rows[1], LANES), bf16), V((s.rows[2], LANES), bf16),
             V((nb, s.cj, c), f32), V((nb, c, c), f32), V((c, ff), f32), V((c, ff), f32),
-            V((nb, s.cin, c), f32), V((8, up_to(ff, LANES)), f32),
-            pltpu.SemaphoreType.DMA((8,)), pltpu.SemaphoreType.DMA((16,)),
+            V((nb, s.cin, c), f32), V((8, up_to(ff, LANES)), f32), V((s.rows[3], LANES), f32),
+            V(out_shape[4].shape, bf16), V(out_shape[5].shape, bf16), V((4, 1, c), f32),
+            V((s.cin,), f32), V((ff,), f32), *[V((c,), f32)] * 7,
+            pltpu.SemaphoreType.DMA((16,)), pltpu.SemaphoreType.DMA((32,)),
         ],
         compiler_params=pltpu.CompilerParams(vmem_limit_bytes=60 * 2**20),
         name="finish",

time: 113 us -> 106 us (0.938)
  Pallas kernels: 111 us -> 104 us
    pallas_call x1, Pallas kernels: 102 us -> 96.9 us  [per_device(): pl.pallas_call(functools.partial(main_kernel, s, names), out_shape=out_sh...]
    pallas_call x1, Pallas kernels: 8.83 us -> 7.48 us  [per_device(): pl.pallas_call(functools.partial(finish_kernel, s), out_shape=outs, in_sp...]
where the time goes in v5:
time: 106 us
  Pallas kernels  104 us (98%)
  between operations  1.5 us (1%)
    pallas_call x1, Pallas kernels, per_device(): pl.pallas_call(functools.partial(main_kernel, s, names), out_shape=out_sh...  96.9 us
    pallas_call x1, Pallas kernels, per_device(): pl.pallas_call(functools.partial(finish_kernel, s), out_shape=outs, in_sp...  7.48 us

profile of v5, /device:TPU:0, one launch (start us, length us, event | category | flops | bytes accessed | tf_op | source)
XLA Modules:
  0.0 105.9 jit_solution(16803782658399686779)
XLA Ops:
  1.3 96.9 %forecast.1 = (bf16[14336,128]{1,0:T(8,128)(2,1)}, bf16[10240,128]{1,0:T(8,128)(2,1)}, bf16[1536,128]{1,0:T(8,128)(2,1)}, f32[256,128]{1,0:T(8,128)}, bf16[1,72,...) custom-call(bf16[2,72,4,256]{3,2,1,0:T(4,128)(2,1)} %refs_0_.1, ...), custom_call_target="tpu_custom_call" | custom-call | tf_op jit(solution)/shard_map/forecast/pallas_call | solution.py:1301
  98.3 7.5 %finish.1 = (bf16[1,72,4,256]{3,2,1,0:T(4,128)(2,1)}, bf16[2,72,4,256]{3,2,1,0:T(4,128)(2,1)}, f32[3,80,641]{2,1,0:T(8,128)}, f32[641]{0:T(1024)}, f32[641]{0:T(...) custom-call(bf16[14336,128]{1,0:T(8,128)(2,1)} %get-tuple-element.50, ...), custom_call_target="tpu_custom_call" | custom-call | tf_op jit(solution)/shard_map/finish/pallas_call | solution.py:1320

commit v6 on v5

--- a/solution.py
+++ b/solution.py
@@ -298,6 +298,9 @@
         out=V((1, s.cin, s.full_rows, big), bf16),
         sgrad=V((s.dates, s.cin, s.full_rows, big), bf16),
         means=V((4, 1, c), f32),
+        date=pltpu.SMEM((1,), i32), reach=pltpu.SMEM((s.lat_total,), i32),
+        enc_taps=pltpu.SMEM((s.nb, s.lat_total, 25), f32), proc_taps=pltpu.SMEM((s.nb, s.lat_total, 25), f32),
+        dec_taps=pltpu.SMEM((s.nb, 2 * s.lat_total, 9), f32),
         xin=V((160, s.full_rows, big), f32),
         xj=V((160, 8 * big), bf16),
         eb=V((2, 8, 160), f32),
@@ -314,7 +317,9 @@
         filte=V((s.nb, px, s.cj), bf16),
         hx=V((6 * LANES + 48, c), f32),
         nx=V((6 * LANES + 48, c), bf16),
-        pe=V((2, 8, c), f32),
+        pe=V((2, 4, c), f32),
+        he=V((6, 4, c), f32),
+        ce=V((6, 4, c), f32),
         filt=V((s.nb * px, c), bf16),
         h1=V((px, c), f32),
         n2=V((px, c), bf16),
@@ -338,7 +343,7 @@
         con=V((6 * LANES + 48, c), f32),
         rup=V((px, c), f32),
         rdn=V((px, c), f32),
-        reg=V((6, 8, c), f32),
+        reg=V((6, 4, c), f32),
         zg=V((px, c), bf16),
         sgx=V((160, wide), f32),
         sgb=V((160, 4 * big), bf16),
@@ -364,7 +369,7 @@
         kinds = AllReduce.shapes(s, rows, route, f32 if buffer == 3 else bf16)
         for j, kind in enumerate(kinds):
             shapes[name, j] = kind
-    shapes[WSEM] = pltpu.SemaphoreType.DMA((23,))
+    shapes[WSEM] = pltpu.SemaphoreType.DMA((28,))
     shapes[OSEM] = pltpu.SemaphoreType.DMA((len(s.chunks),))
     shapes[SEMS] = pltpu.SemaphoreType.DMA((sem_count(s),))
     return shapes
@@ -380,7 +385,7 @@
 def main_kernel(s, names, *refs):
     n_in, n_out = 22, 10
     (
-        state_h, noise_h, cot_h, date_ref, reach, enc_taps, proc_taps, dec_taps,
+        state_h, noise_h, cot_h, date_h, reach_h, enc_taps_h, proc_taps_h, dec_taps_h,
         ew_h, eb_h, gain1_h, shift1_h, pw_h, pb_h, gain2_h, shift2_h, uw_h, ub_h, dw_h, db_h, cw_h, cb_h,
     ) = refs[:n_in]
     h1o, h2o, h3o, hmo, out_h, sgrad_h, m1_h, v1_h, m2_h, v2_h = refs[n_in : n_in + n_out]
@@ -410,6 +415,17 @@
         copy.start()
         return copy
 
+    date_ref, reach = S.date, S.reach
+    enc_taps, proc_taps, dec_taps = S.enc_taps, S.proc_taps, S.dec_taps
+    scalars = [
+        fetch(23 + n, *pair)
+        for n, pair in enumerate(
+            (
+                (date_h, date_ref), (reach_h, reach), (enc_taps_h, enc_taps),
+                (proc_taps_h, proc_taps), (dec_taps_h, dec_taps),
+            )
+        )
+    ]
     state, noise, cot = S.state, S.noise, S.cot
     fields = [fetch(n, *pair) for n, pair in enumerate(((state_h, state), (noise_h, noise), (cot_h, cot)))]
     eb, gain1, shift1, pb, gain2, shift2 = S.eb_v, S.gain1, S.shift1, S.pb, S.gain2, S.shift2
@@ -437,7 +453,7 @@
         copy.start()
         finals.append(copy)
 
-    for copy in fields:
+    for copy in fields + scalars:
         copy.wait()
 
     date = date_ref[0]
@@ -469,14 +485,14 @@
         xj[:, 0 : 2 * big] = jnp.zeros((160, 2 * big), bf16)
         S.hx[0:px] = jnp.zeros((px, c), f32)
         for side in range(2):
-            S.hx[768 + side * 8 : 776 + side * 8] = jnp.zeros((8, c), f32)
+            S.he[side] = jnp.zeros((4, c), f32)
 
     @pl.when(jnp.logical_not(k.has_down()))
     def _():
         xj[:, 6 * big : 8 * big] = jnp.zeros((160, 2 * big), bf16)
         S.hx[2 * px : 3 * px] = jnp.zeros((px, c), f32)
         for side in range(2):
-            S.hx[768 + 32 + side * 8 : 776 + 32 + side * 8] = jnp.zeros((8, c), f32)
+            S.he[4 + side] = jnp.zeros((4, c), f32)
 
     pl.semaphore_wait(barrier, len(offsets))
 
@@ -767,7 +783,6 @@
         for q in range(2):
             lo = px + q * LANES + col
             pe[side, 2 * q : 2 * q + 2, :] = hx[lo : lo + 2, :]
-            pe[side, 4 + 2 * q : 6 + 2 * q, :] = jnp.zeros((2, c), f32)
     sends = [
         Send(k, hx.at[pl.ds(px, px)], hx.at[pl.ds(2 * px, px)], k.at(0, -1, 0), -1),
         Send(k, hx.at[pl.ds(px, px)], hx.at[pl.ds(0, px)], k.at(0, 1, 0), 1),
@@ -777,7 +792,7 @@
             Send(
                 k,
                 pe.at[(ds + 1) // 2],
-                hx.at[pl.ds(768 + slot_of(dl, ds) * 8, 8)],
+                S.he.at[slot_of(dl, ds)],
                 k.at(0, dl, ds),
                 dl,
             )
@@ -810,6 +825,9 @@
     keep(S.means.at[0], m1_h)
     keep(S.means.at[1], v1_h)
     arrive(zero_halo)
+    for slot in range(6):
+        lo = 768 + slot * 8
+        hx[lo : lo + 8, :] = jnp.concatenate([S.he[slot], jnp.zeros((4, c), f32)], axis=0)
     nx = S.nx
     scale1 = rstd1 * vec(gain1)
     bias1 = vec(shift1)
@@ -960,6 +978,8 @@
     put_misc(gm, MISC.shift_one, sum_a)
     put_misc(gm, MISC.gain_one, sum_b)
     stat_d = stat_start(3, sum_a, sum_b)
+    for slot in range(6):
+        S.ce[slot] = con[768 + slot * 8 : 772 + slot * 8, :]
     sends = [
         Send(k, con.at[pl.ds(0, px)], S.rdn, k.at(0, -1, 0), -1),
         Send(k, con.at[pl.ds(2 * px, px)], S.rup, k.at(0, 1, 0), 1),
@@ -969,7 +989,7 @@
         sends.append(
             Send(
                 k,
-                con.at[pl.ds(768 + mine * 8, 8)],
+                S.ce.at[mine],
                 S.reg.at[slot_of(dl, ds)],
                 k.at(0, dl, ds),
                 dl,
@@ -1288,7 +1308,7 @@
     hbm = pl.BlockSpec(memory_space=pl.ANY)
     shapes = scratch_list(s)
     names = tuple(shapes)
-    in_specs = [hbm] * 3 + [sm] * 5 + [hbm] * 14
+    in_specs = [hbm] * 22
     sd = jax.ShapeDtypeStruct
     out_shape = [
         sd((s.rows[0], LANES), bf16),

time: 106 us -> 103 us (0.972)
  Pallas kernels: 104 us -> 102 us
    pallas_call x1, Pallas kernels: 96.9 us -> 94.3 us  [per_device(): pl.pallas_call(functools.partial(main_kernel, s, names), out_shape=out_sh...]
where the time goes in v6:
time: 103 us
  Pallas kernels  102 us (99%)
  between operations  1.5 us (1%)
    pallas_call x1, Pallas kernels, per_device(): pl.pallas_call(functools.partial(main_kernel, s, names), out_shape=out_sh...  94.3 us
    pallas_call x1, Pallas kernels, per_device(): pl.pallas_call(functools.partial(finish_kernel, s), out_shape=outs, in_sp...  7.48 us

profile of v6, /device:TPU:0, one launch (start us, length us, event | category | flops | bytes accessed | tf_op | source)
XLA Modules:
  0.0 103.3 jit_solution(11201399915941464287)
XLA Ops:
  1.3 94.3 %forecast.1 = (bf16[14336,128]{1,0:T(8,128)(2,1)}, bf16[10240,128]{1,0:T(8,128)(2,1)}, bf16[1536,128]{1,0:T(8,128)(2,1)}, f32[256,128]{1,0:T(8,128)}, bf16[1,72,...) custom-call(bf16[2,72,4,256]{3,2,1,0:T(4,128)(2,1)} %refs_0_.1, ...), custom_call_target="tpu_custom_call" | custom-call | tf_op jit(solution)/shard_map/forecast/pallas_call | solution.py:1321
  95.6 7.5 %finish.1 = (bf16[1,72,4,256]{3,2,1,0:T(4,128)(2,1)}, bf16[2,72,4,256]{3,2,1,0:T(4,128)(2,1)}, f32[3,80,641]{2,1,0:T(8,128)}, f32[641]{0:T(1024)}, f32[641]{0:T(...) custom-call(bf16[14336,128]{1,0:T(8,128)(2,1)} %get-tuple-element.50, ...), custom_call_target="tpu_custom_call" | custom-call | tf_op jit(solution)/shard_map/finish/pallas_call | solution.py:1340

commit v7 on v6

--- a/solution.py
+++ b/solution.py
@@ -885,9 +885,11 @@
         here = pl.ds(pl.multiple_of(n * 16, 16), 16)
         v = hp[here, :] + ubias
         sq = v * v
-        t = jnp.tanh(root * (v + 0.044715 * (sq * v)))
-        act[here, :] = (0.5 * v * (1.0 + t)).astype(bf16)
-        slope = 0.5 * (1.0 + t) + (0.5 * root) * v * (1.0 - t * t) * (1.0 + (3 * 0.044715) * sq)
+        t = jnp.tanh(v * (root + (0.044715 * root) * sq))
+        part = 0.5 * t + 0.5
+        active = v * part
+        act[here, :] = active.astype(bf16)
+        slope = part + active * (1.0 - part) * (2.0 * root + (6.0 * 0.044715 * root) * sq)
         hg[here, :] = (slope * ag[here, :]).astype(bf16)
         return carry
 
@@ -911,7 +913,7 @@
     for kk in range(nb):
         got = tn(pgr[kk], h2[:, 0 : s.c5 * LANES])
         spread(g1, s.off_dec + kk * s.c5 * s.r80, cin, s.r80, got, 0, s.c5 * LANES)
-    ar("bace")
+    ar("bceafd")
     ntg = S.ntg
     ntg[...] = nt(hg[...], S.uw[...])
     grad = ntg[...]
@@ -922,7 +924,7 @@
     put_misc(gm, MISC.gain_two, sum_b)
     stat_c = stat_start(2, sum_a, sum_b)
 
-    ar("cdfed")
+    ar("ecdfb")
     stat_c = stat_middle(2, stat_c, False)
 
     def weighted(ref, column):
@@ -942,7 +944,6 @@
             put_misc(gm, MISC.dec_last + kk, weighted(pgr[kk], h2[:, c - 1 : c]))
 
     sum_a, sum_b = stat_end(2, stat_c, False)
-    ar("fb")
     g_two = vec(gain2)
     part_a = g_two * sum_a * (1.0 / s.pixels)
     part_b = g_two * sum_b * (1.0 / s.pixels)
@@ -998,6 +999,7 @@
     back_halo = start(sends)
     g2 = S.g2
     S.brt[...] = br[...].T
+    ar("e")
     for kk in range(nb):
         if kk == 1:
             stat_d = stat_middle(3, stat_d, False)
@@ -1005,11 +1007,11 @@
             got = nn(S.brt[...], filt[kk * px : (kk + 1) * px, lo : lo + width])
             spread(g2, kk * s.c5 * s.r641, c, s.r641, got, lo, width)
         if kk == 1:
-            ar("edgha")
-    ar("ijbchg")
+            ar("agdhb")
+    ar("igh")
 
     arrive(back_halo)
-    ar("ei")
+    ar("e")
     ng = ntg
     ng[...] = con[own, :]
 
@@ -1047,7 +1049,7 @@
         return carry
 
     lax.fori_loop(0, px // 32, zero_rows, 0)
-    ar("c")
+    ar("f")
 
     g3 = S.g3
     for kk in range(nb):
@@ -1055,12 +1057,12 @@
         spread(g3, kk * s.c5 * s.r80, cj, s.r80, got, 0, s.c5 * LANES)
         put_misc(gm, MISC.enc_last + kk, weighted(filte[kk], zg[:, c - 1 : c]))
     put_misc(gm, MISC.enc_bias, jnp.sum(zg[...].astype(f32), axis=0, keepdims=True))
-    ar("adj")
+    ar("ia")
     misc_one()
     put_misc(gm, MISC.proc_bias, jnp.sum(br[...].astype(f32), axis=0, keepdims=True))
     for kk in range(nb):
         put_misc(gm, MISC.proc_last + kk, weighted(br[...], filt[kk * px : (kk + 1) * px, c - 1 : c]))
-    ar("k")
+    ar("b")
 
     projt, partt = S.projt, S.partt
     for kk in range(nb):
@@ -1097,9 +1099,9 @@
             Send(k, S.sgn.at[(dl + 1) * 2 + (ds + 1) // 2], sge.at[slot_of(dl, ds)], k.at(0, dl, ds), dl)
         )
     out_halo = start(sends)
-    ar("fkcbgjaiheldf")
+    ar("gdfhkcjlaekljbg")
     arrive(out_halo)
-    ar("l")
+    ar("f")
     sgt = S.sgt
     sgt[48:LANES, :] = jnp.zeros((LANES - 48, 160), f32)
     for slot in range(6):
@@ -1152,7 +1154,7 @@
             for half in range(2)
         ]
     )
-    ar("ckfgbahefidbgl")
+    ar("icadfhkl")
     arrive(state_sends)
     state_sends = start(
         [
@@ -1161,9 +1163,10 @@
             for slot in slots
         ]
     )
-    ar("kdhbjgieklhjgckihdjlekdafljiagklhcke")
+    ar("cgiadkjehlbcjdgkeabihgljckilfdh")
     arrive(date_sends)
     arrive(state_sends)
+    ar("jdilkjegc")
     for d in range(s.dates):
         for q in range(4):
             value = jnp.zeros((80, big), f32)
@@ -1175,7 +1178,7 @@
         S.sgrad[d] = orow[...].astype(bf16)
     keep(S.sgrad, sgrad_h)
 
-    ar("bfhjiclfgjil")
+    ar("fblcihekjiflhkgj")
     while not all(it.finished() for it in reduced.values()):
         ar("abcdefghijklmn")
     for m in pending:

time: 103 us -> 103 us (level)
  no operation moved by 1% of the time
where the time goes in v7:
time: 103 us
  Pallas kernels  101 us (98%)
  between operations  1.5 us (1%)
    pallas_call x1, Pallas kernels, per_device(): pl.pallas_call(functools.partial(main_kernel, s, names), out_shape=out_sh...  93.9 us
    pallas_call x1, Pallas kernels, per_device(): pl.pallas_call(functools.partial(finish_kernel, s), out_shape=outs, in_sp...  7.48 us

profile of v7, /device:TPU:0, one launch (start us, length us, event | category | flops | bytes accessed | tf_op | source)
XLA Modules:
  0.0 102.9 jit_solution(18365668866914217388)
XLA Ops:
  1.3 93.9 %forecast.1 = (bf16[14336,128]{1,0:T(8,128)(2,1)}, bf16[10240,128]{1,0:T(8,128)(2,1)}, bf16[1536,128]{1,0:T(8,128)(2,1)}, f32[256,128]{1,0:T(8,128)}, bf16[1,72,...) custom-call(bf16[2,72,4,256]{3,2,1,0:T(4,128)(2,1)} %refs_0_.1, ...), custom_call_target="tpu_custom_call" | custom-call | tf_op jit(solution)/shard_map/forecast/pallas_call | solution.py:1324
  95.2 7.5 %finish.1 = (bf16[1,72,4,256]{3,2,1,0:T(4,128)(2,1)}, bf16[2,72,4,256]{3,2,1,0:T(4,128)(2,1)}, f32[3,80,641]{2,1,0:T(8,128)}, f32[641]{0:T(1024)}, f32[641]{0:T(...) custom-call(bf16[14336,128]{1,0:T(8,128)(2,1)} %get-tuple-element.50, ...), custom_call_target="tpu_custom_call" | custom-call | tf_op jit(solution)/shard_map/finish/pallas_call | solution.py:1343

commit v8 on v7

--- a/solution.py
+++ b/solution.py
@@ -746,6 +746,7 @@
     build_encoder()
     build_decoder()
     build_processor()
+    S.tmt[...] = S.tm[...].T
 
     arrive(first_halo)
     def absent(slot):
@@ -855,8 +856,6 @@
     ag[...] = nn(mg[...], S.dw[...])
     S.mgt[...] = mg[...].T
     put_misc(gm, MISC.down_bias, jnp.sum(mg[...].astype(f32), axis=0, keepdims=True))
-    tm_t = S.tmt
-    tm_t[...] = tm[...].T
     mean2, m2 = stat_end(1, stat_b, True)
     var2 = m2 * (1.0 / s.pixels)
     rstd2 = lax.rsqrt(var2 + EPS)

time: 103 us -> 103 us (level)
  no operation moved by 1% of the time
where the time goes in v8:
time: 103 us
  Pallas kernels  101 us (98%)
  between operations  1.5 us (1%)
    pallas_call x1, Pallas kernels, per_device(): pl.pallas_call(functools.partial(main_kernel, s, names), out_shape=out_sh...  93.8 us
    pallas_call x1, Pallas kernels, per_device(): pl.pallas_call(functools.partial(finish_kernel, s), out_shape=outs, in_sp...  7.48 us

profile of v8, /device:TPU:0, one launch (start us, length us, event | category | flops | bytes accessed | tf_op | source)
XLA Modules:
  0.0 102.8 jit_solution(7805020350321775304)
XLA Ops:
  1.3 93.8 %forecast.1 = (bf16[14336,128]{1,0:T(8,128)(2,1)}, bf16[10240,128]{1,0:T(8,128)(2,1)}, bf16[1536,128]{1,0:T(8,128)(2,1)}, f32[256,128]{1,0:T(8,128)}, bf16[1,72,...) custom-call(bf16[2,72,4,256]{3,2,1,0:T(4,128)(2,1)} %refs_0_.1, ...), custom_call_target="tpu_custom_call" | custom-call | tf_op jit(solution)/shard_map/forecast/pallas_call | solution.py:1323
  95.2 7.5 %finish.1 = (bf16[1,72,4,256]{3,2,1,0:T(4,128)(2,1)}, bf16[2,72,4,256]{3,2,1,0:T(4,128)(2,1)}, f32[3,80,641]{2,1,0:T(8,128)}, f32[641]{0:T(1024)}, f32[641]{0:T(...) custom-call(bf16[14336,128]{1,0:T(8,128)(2,1)} %get-tuple-element.50, ...), custom_call_target="tpu_custom_call" | custom-call | tf_op jit(solution)/shard_map/finish/pallas_call | solution.py:1342
